TPU v7x, 256 devices: a whole 4x4x8 slice. The times are simulated.
256 devices in a mesh: dp: 64 (over y, z, core), mp: 4 (over x).
Axes of the slice: x: 4, y: 4, z: 8, core: 2. Of those that a mesh axis runs over, the one named last changes fastest.
Arguments:
- cand_item: int32 [512, 128], P(('dp', 'mp')), may hold values from 0 to 131071, as said below
- list_place: int32 [512], replicated, may hold values from 0 to 511, as said below
- item_table: bfloat16 [131072, 768], P('dp', 'mp'), may hold values from -6 to 6
- query_vec: bfloat16 [512, 768], P(('dp', 'mp')), may hold values from -1.796875 to 1.796875
- labels: int32 [512, 128], P(('dp', 'mp')), may hold values from 0 to 4
- query_weight: bfloat16 [768, 768], replicated, may hold values from -0.75 to 0.75
- key_weight: bfloat16 [768, 768], replicated, may hold values from -0.75 to 0.75
- value_weight: bfloat16 [768, 768], replicated, may hold values from -0.21875 to 0.21875
- output_weight: bfloat16 [768, 768], replicated, may hold values from -0.21875 to 0.21875
- gain_attn: float32 [768], replicated, may hold values from 0.1 to 1.9
- gain_score: float32 [768], replicated, may hold values from 0.1 to 1.9
- w_score: float32 [768], replicated, may hold values from -0.6 to 0.6
Outputs:
- losses: float32 [512], P(('dp', 'mp'))
- table_grad: float32 [131072, 768], P('dp', 'mp')
- query_grad: float32 [512, 768], P(('dp', 'mp'))
- query_weight_gradient: float32 [768, 768], P('dp')
- key_weight_gradient: float32 [768, 768], P('dp')
- value_weight_gradient: float32 [768, 768], P('dp')
- output_weight_gradient: float32 [768, 768], P('dp')
- grad_gain_attn: float32 [768], replicated
- grad_gain_score: float32 [768], replicated
- grad_w_score: float32 [768], replicated
Inputs may be any that keep to these rules, and one draw needn't show every extreme that they name: `cand_item`: item i lies in list i // 256 at place i % 256. Of the 1024 candidates of the queries of one index of dp (aligned blocks of rows), at most 32 lie in lists stored on one index of dp; one index of dp, the same for every block, holds exactly 32 of the candidates of every block. A permutation: list l is stored as rows list_place[l] * 256 to list_place[l] * 256 + 255 of item_table.
All inputs are finite; a program needn't handle non-finite values.
Results may differ from a plain program's by a relative error of at most 0.025.
Values may be sent and summed in bfloat16 or wider, within the bound.
No kernel may reach another device: no remote copies, remote signals or barrier semaphores. Data moves between devices by JAX's collectives and lax.ppermute only.
A program may use at most 128 MiB of HBM per device.

v0:
```python
import jax
import jax.numpy as jnp
from jax import lax
from jax.experimental import pallas as pl
from jax.experimental.pallas import tpu as pltpu
from jax.sharding import Mesh
from jax.sharding import PartitionSpec as P

HEADS = 12
LIST_LEN = 256
EPSILON = 1e-06
SCORE_CAP = 20.0
RANK_CAP = 30.0

ROWS = ("y", "z", "c")
CAP = 32
SLAB = 192
BF = jnp.bfloat16
F32 = jnp.float32
MIB = 1024 * 1024


def dot(a, b, ca=1, cb=0):
    return lax.dot_general(a, b, (((ca,), (cb,)), ((), ())), preferred_element_type=F32)


def iota(shape, dim):
    return lax.broadcasted_iota(jnp.int32, shape, dim)


def whole(n):
    return [pl.BlockSpec(memory_space=pltpu.VMEM)] * n


def inside(x):
    return pltpu.with_memory_space_constraint(x, pltpu.VMEM)


def stays(x):
    return pltpu.with_memory_space_constraint(x, pltpu.HBM)


def call(kernel, out_shape, args, mib, flops, size, scratch=(), scalars=0, left=(), awaited=()):
    many = isinstance(out_shape, (list, tuple))
    outs = out_shape if many else [out_shape]
    specs = [
        pl.BlockSpec(memory_space=pltpu.HBM if getattr(o, "memory_space", None) == pltpu.HBM else pltpu.VMEM)
        for o in outs
    ]
    in_specs = [pl.BlockSpec(memory_space=pltpu.SMEM)] * scalars + whole(len(args) - scalars)
    args = list(args)
    for i in left:
        in_specs[i] = pl.BlockSpec(memory_space=pltpu.HBM)
        args[i] = stays(args[i])
    in_specs += [pl.BlockSpec(memory_space=pl.ANY)] * len(awaited)

    def run(*refs):
        kernel(*refs[: len(args)], *refs[len(args) + len(awaited) :])

    return pl.pallas_call(
        run,
        out_shape=out_shape,
        in_specs=in_specs,
        out_specs=specs if many else specs[0],
        scratch_shapes=list(scratch),
        compiler_params=pltpu.CompilerParams(vmem_limit_bytes=mib * MIB),
        cost_estimate=pl.CostEstimate(flops=flops, bytes_accessed=size, transcendentals=0),
    )(*args, *awaited)


def shift(x, axis, by):
    return lax.ppermute(x, axis, [(i, (i + by) % 4) for i in range(4)])


def exchange(blocks, axis):
    far = shift(blocks[2], axis, 2)
    return [blocks[0], shift(blocks[1], axis, 1), far, shift(blocks[3], axis, 3)]


def collect(me, refs, held):
    for k, ref in enumerate(refs):
        held[(me - k) & 3] = ref[...]


def low_half(shape):
    return iota(shape, len(shape) - 1) < 64


def swap_halves(t):
    return jnp.concatenate([t[..., 64:], t[..., :64]], axis=-1)


def spread_tail(t):
    t = t.astype(F32)
    other = swap_halves(t)
    low = low_half(t.shape)
    return jnp.concatenate([jnp.where(low, t, other), jnp.where(low, other, t)], axis=1)


def unpack(block):
    b, rows, _ = block.shape
    n = rows // 3
    main = block[:, : 2 * n, :].reshape(b * 2 * n, 128)
    tail = spread_tail(block[:, 2 * n :, :]).astype(BF).reshape(b * 2 * n, 128)
    return jnp.concatenate([main, tail], axis=1)


def pack(full, n):
    tail = full[:, 128:]
    tail = jnp.where(low_half((n, 128)), tail[:n], tail[n:])
    return jnp.concatenate([full[:, :128], tail], axis=0).astype(BF)


def as_column(row):
    return jnp.transpose(jnp.broadcast_to(row, (128, 128)))


def routing_kernel(me_ref, a_ref, b_ref, c_ref, d_ref, place_hbm, request_ref, slot_ref, held, place_ref, sem):
    me = me_ref[0]
    copies = [
        pltpu.make_async_copy(place_hbm, place_ref, sem.at[0]),
        pltpu.make_async_copy(a_ref, held.at[me], sem.at[1]),
    ]
    for c in copies:
        c.start()
    for k, ref in ((1, b_ref), (2, c_ref), (3, d_ref)):
        held[(me - k) & 3] = ref[...]
    for c in copies:
        c.wait()
    place = place_ref[...]
    lists = place.shape[1]
    lane = iota((128, 128), 1)
    owner_of_list = jnp.broadcast_to(place >> 3, (128, lists))
    row = iota((128, lists), 0)
    lookup = jnp.where(owner_of_list == row, 1.0, 0.0)
    lookup = jnp.where(row == 64, jnp.broadcast_to(place & 7, (128, lists)).astype(F32), lookup)
    lookup = lookup.astype(BF)
    before = (iota((128, 128), 1) < iota((128, 128), 0)).astype(F32).astype(BF)
    carry = jnp.zeros((1, 128), F32)
    request = jnp.zeros((128, 128), F32)
    for q in range(slot_ref.shape[0]):
        ids = as_column(held[q // 2, q % 2 : q % 2 + 1, :])
        list_id = ids >> 8
        chosen = jnp.concatenate(
            [(list_id == lane + 128 * t).astype(F32).astype(BF) for t in range(lists // 128)], axis=1
        )
        found = dot(chosen, lookup, 1, 1)
        sub = jnp.sum(jnp.where(lane == 64, found, 0.0), 1, keepdims=True)
        onehot = jnp.where(lane < 64, found, 0.0)
        onehot_low = onehot.astype(BF)
        ahead = dot(before, onehot_low) + carry
        carry = carry + jnp.sum(onehot, 0, keepdims=True)
        rank = jnp.sum(onehot * ahead, 1, keepdims=True)
        owner = jnp.sum(onehot * lane.astype(F32), 1, keepdims=True)
        slot = jnp.broadcast_to(owner * CAP + rank, (128, 128))
        slot_ref[q : q + 1, :] = jnp.transpose(slot)[0:1, :].astype(jnp.int32)
        rank = rank.astype(jnp.int32)
        place_in = (ids & 255).astype(F32)
        entry = jnp.where(rank == lane, sub + 1.0, jnp.where(rank == lane - CAP, place_in, 0.0))
        request = request + dot(onehot_low, entry.astype(BF), 0, 0)
    high = request[:64, :CAP]
    low = request[:64, CAP : 2 * CAP]
    asked = (high - 1.0) * LIST_LEN + low
    request_ref[...] = jnp.where(high > 0.5, asked, -1.0).astype(jnp.int32)


def four_groups(asked):
    part = asked.shape[0] // 4
    return jnp.concatenate([asked[part * k : part * (k + 1)] for k in range(4)], axis=1)


def load_kernel(table_hbm, table_ref, sem):
    copies = [
        pltpu.make_async_copy(table_hbm, table_ref.at[pl.ds(0, SLAB)], sem.at[0]),
        pltpu.make_async_copy(table_hbm.at[pl.ds(128, 64)], table_ref.at[pl.ds(SLAB, 64)], sem.at[1]),
    ]
    for c in copies:
        c.start()
    for c in copies:
        c.wait()


def owner_kernel(asked_ref, table_ref, out_ref):
    asked = four_groups(asked_ref[...])
    part = asked.shape[0]
    stored = table_ref.shape[1]
    step = 4
    for r in range(0, part, step):
        column = jnp.concatenate([as_column(asked[r + i : r + i + 1]) for i in range(step)], axis=0)
        lane = iota((128 * step, 128), 1)
        chosen = jnp.concatenate(
            [(column == lane + 128 * t).astype(F32).astype(BF) for t in range(stored // 128)], axis=1
        )
        rows = dot(chosen, table_ref[...], 1, 1)
        for i in range(step):
            for k in range(4):
                at = 128 * i + CAP * k
                out_ref[part * k + r + i] = pack(rows[at : at + CAP], CAP // 2)


def pieces_kernel(me_ref, slot_ref, fetched_ref, own_hbm, *refs):
    out_refs, own_ref, sem = refs[:3], refs[3], refs[4]
    fetched = unpack(fetched_ref[...])
    slots = fetched.shape[0]
    copy = pltpu.make_async_copy(own_ref, own_hbm, sem.at[0])
    for k, out_ref in enumerate((own_ref, *out_refs)):
        m = (me_ref[0] + k) & 3
        column = jnp.concatenate([as_column(slot_ref[pl.ds(2 * m + i, 1), :]) for i in (0, 1)], axis=0)
        lane = iota((256, 128), 1)
        chosen = jnp.concatenate(
            [(column == lane + 128 * t).astype(F32).astype(BF) for t in range(slots // 128)], axis=1
        )
        out_ref[...] = pack(dot(chosen, fetched), 128)
        if k == 0:
            copy.start()
    copy.wait()


def slots_kernel(me_ref, slot_ref, a_ref, b_ref, c_ref, d_ref, out_ref, held):
    collect(me_ref[0], (a_ref, b_ref, c_ref, d_ref), held)
    grads = unpack(held[...])
    groups = out_ref.shape[0]
    step = 16 * CAP
    for r in range(0, groups * CAP, step):
        row = iota((step, 128), 0) + r
        chosen = jnp.concatenate(
            [
                (jnp.broadcast_to(slot_ref[q : q + 1, :], (step, 128)) == row).astype(F32).astype(BF)
                for q in range(slot_ref.shape[0])
            ],
            axis=1,
        )
        rows = dot(chosen, grads)
        for i in range(16):
            out_ref[r // CAP + i] = pack(rows[CAP * i : CAP * (i + 1)], CAP // 2)


def landing_kernel(asked_ref, arrived_ref, out_ref):
    arrived = unpack(arrived_ref[...])
    stored = out_ref.shape[1]
    slots = arrived.shape[0]
    asked = four_groups(asked_ref[...])
    part = asked.shape[0]
    columns = [as_column(asked[r : r + 1]) for r in range(part)]
    column = jnp.concatenate(
        [columns[g % part][CAP * (g // part) : CAP * (g // part + 1)] for g in range(4 * part)], axis=0
    )
    step = 512
    lane = iota((slots, 128), 1)
    for r in range(0, stored, step):
        chosen = jnp.concatenate(
            [(column == lane + (r + 128 * t)).astype(F32).astype(BF) for t in range(step // 128)], axis=1
        )
        out_ref[:, r : r + step] = dot(arrived, chosen, 0, 0)[:SLAB]


def lane_mean(x):
    return jnp.sum(x, 1, keepdims=True) * (1.0 / x.shape[1])


def step_kernel(
    me_ref,
    core_ref,
    a_hbm,
    b_ref,
    c_ref,
    d_ref,
    query_ref,
    labels_ref,
    wq_hbm,
    wk_hbm,
    wv_hbm,
    wo_hbm,
    gain_attn_ref,
    gain_score_ref,
    w_score_ref,
    losses_ref,
    query_grad_ref,
    base_0_ref,
    base_1_ref,
    base_2_ref,
    base_3_ref,
    keep_hbm,
    send_hbm,
    vectors_ref,
    held,
    scores_t,
    attend_t,
    wq_ref,
    wk_ref,
    wv_ref,
    wo_ref,
    keep_ref,
    send_ref,
    sem,
):
    me = me_ref[0]
    own = pltpu.make_async_copy(a_hbm, held.at[me], sem.at[4])
    own.start()
    sources = (wq_hbm, wk_hbm, wv_hbm, wo_hbm)
    weights = (wq_ref, wk_ref, wv_ref, wo_ref)
    copies = [pltpu.make_async_copy(a, b, sem.at[i]) for i, (a, b) in enumerate(zip(sources, weights))]
    for c in copies:
        c.start()
    for k, ref in ((1, b_ref), (2, c_ref), (3, d_ref)):
        held[(me - k) & 3] = ref[...]
    own.wait()
    queries, width = query_ref.shape
    size = 128
    head = width // HEADS
    pairs = HEADS // 2
    shrink = head ** (-0.5)
    low = low_half((size, 128))

    parts = []
    for m in range(4):
        main = held[m, :256, :].astype(F32)
        tail = held[m, 256:, :].astype(F32)
        parts += [main, jnp.concatenate([tail[:, :64], tail[:, 64:]], axis=0)]
    rows_in = jnp.concatenate(parts, axis=1)
    vecs = query_ref[...].astype(F32)
    vecs = jnp.concatenate([jnp.broadcast_to(vecs[q : q + 1], (size, width)) for q in range(queries)], axis=0)
    base = rows_in + vecs
    inv_one = 1.0 / jnp.sqrt(lane_mean(base * base) + EPSILON)
    normed_one = base * inv_one
    gain_attn = gain_attn_ref[...]
    first_input = (normed_one * gain_attn).astype(BF)
    copies[0].wait()
    q_all = dot(first_input, wq_ref[...]).astype(BF)
    copies[1].wait()
    k_all = dot(first_input, wk_ref[...]).astype(BF)
    copies[2].wait()
    v_all = dot(first_input, wv_ref[...]).astype(BF)

    def cut(x, q, p):
        return x[size * q : size * (q + 1), 128 * p : 128 * (p + 1)]

    zero = jnp.zeros((size, 128), BF)

    def heads_apart(x):
        return jnp.concatenate([jnp.where(low, x, zero), jnp.where(low, zero, x)], axis=0)

    def heads_joined(x):
        return jnp.where(low, x[:size], x[size:])

    context = []
    for q in range(queries):
        line = []
        for p in range(pairs):
            logits = dot(cut(k_all, q, p), heads_apart(cut(q_all, q, p)), 1, 1)
            th = jnp.tanh(logits * (shrink / SCORE_CAP))
            raised = jnp.exp(SCORE_CAP * th)
            attend = raised * (1.0 / jnp.sum(raised, 0, keepdims=True))
            scores_t[q * pairs + p] = th
            attend_t[q * pairs + p] = attend
            line.append(heads_joined(dot(attend.astype(BF), cut(v_all, q, p), 0, 0)))
        context.append(jnp.concatenate(line, axis=1))
    context = jnp.concatenate(context, axis=0).astype(BF)

    copies[3].wait()
    mixed = base + dot(context, wo_ref[...])
    inv_two = 1.0 / jnp.sqrt(lane_mean(mixed * mixed) + EPSILON)
    normed_two = mixed * inv_two
    gain_score = gain_score_ref[...]
    w_score = w_score_ref[...]
    scaled_two = normed_two * gain_score
    capped_scores = jnp.tanh(jnp.sum(scaled_two * w_score, 1, keepdims=True) * (1.0 / RANK_CAP))
    scores = RANK_CAP * capped_scores
    raised = jnp.exp(scores)
    relevance = jnp.exp(labels_ref[...].astype(F32))
    target = relevance / jnp.sum(relevance, 1, keepdims=True)
    diffs = []
    for q in range(queries):
        at = slice(size * q, size * (q + 1))
        total = jnp.sum(raised[at], 0, keepdims=True)
        wanted = as_column(target[q : q + 1])[:, 0:1]
        loss = jnp.log(total) - jnp.sum(wanted * scores[at], 0, keepdims=True)
        losses_ref[q : q + 1, :] = jnp.broadcast_to(loss, (1, 128))
        diffs.append(raised[at] / total - wanted)
    diff_raw = jnp.concatenate(diffs, axis=0) * (1.0 - capped_scores * capped_scores)
    grad_w_score = jnp.sum(scaled_two * diff_raw, 0, keepdims=True)
    diff_scaled = diff_raw * w_score
    grad_gain_score = jnp.sum(normed_two * diff_scaled, 0, keepdims=True)
    diff_normed = diff_scaled * gain_score
    diff_mixed = (diff_normed - normed_two * lane_mean(diff_normed * normed_two)) * inv_two
    diff_low = diff_mixed.astype(BF)
    diff_context = dot(diff_low, wo_ref[...], 1, 1).astype(BF)

    diff_q, diff_k, diff_v = [], [], []
    for q in range(queries):
        line_q, line_k, line_v = [], [], []
        for p in range(pairs):
            th = scores_t[q * pairs + p]
            attend = attend_t[q * pairs + p]
            split = heads_apart(cut(diff_context, q, p))
            diff_attend = dot(cut(v_all, q, p), split, 1, 1)
            line_v.append(dot(attend.astype(BF), split))
            inner = diff_attend - jnp.sum(attend * diff_attend, 0, keepdims=True)
            diff_logits = (attend * inner * (1.0 - th * th) * shrink).astype(BF)
            line_q.append(heads_joined(dot(diff_logits, cut(k_all, q, p), 0, 0)))
            line_k.append(dot(diff_logits, heads_apart(cut(q_all, q, p))))
        diff_q.append(jnp.concatenate(line_q, axis=1))
        diff_k.append(jnp.concatenate(line_k, axis=1))
        diff_v.append(jnp.concatenate(line_v, axis=1))
    diff_q = jnp.concatenate(diff_q, axis=0).astype(BF)
    diff_k = jnp.concatenate(diff_k, axis=0).astype(BF)
    diff_v = jnp.concatenate(diff_v, axis=0).astype(BF)

    first_core = core_ref[0] == 0
    first_pair = (first_input, first_input, diff_q, diff_k)
    second_pair = (first_input, context, diff_v, diff_low)
    for i in range(4):
        keep_ref[i] = jnp.where(first_core, first_pair[i], second_pair[i])
        send_ref[i] = jnp.where(first_core, second_pair[i], first_pair[i])
    sent = [
        pltpu.make_async_copy(send_ref, send_hbm, sem.at[5]),
        pltpu.make_async_copy(keep_ref, keep_hbm, sem.at[6]),
    ]
    for c in sent:
        c.start()

    diff_input = dot(diff_q, wq_ref[...], 1, 1) + dot(diff_k, wk_ref[...], 1, 1) + dot(diff_v, wv_ref[...], 1, 1)
    grad_gain_attn = jnp.sum(normed_one * diff_input, 0, keepdims=True)
    diff_first = diff_input * gain_attn
    diff_base = diff_mixed + (diff_first - normed_one * lane_mean(diff_first * normed_one)) * inv_one
    for q in range(queries):
        query_grad_ref[q : q + 1, :] = jnp.sum(diff_base[size * q : size * (q + 1)], 0, keepdims=True)
    for m in range(4):
        slab = diff_base[:, SLAB * m : SLAB * (m + 1)]
        held[m, :256, :] = slab[:, :128].astype(BF)
        held[m, 256:, :] = jnp.concatenate([slab[:128, 128:], slab[128:, 128:]], axis=1).astype(BF)
    for k, ref in enumerate((base_0_ref, base_1_ref, base_2_ref, base_3_ref)):
        ref[...] = held[(me + k) & 3]
    vectors = [
        v[:, 128 * t : 128 * (t + 1)]
        for v in (grad_gain_attn, grad_gain_score, grad_w_score)
        for t in range(width // 128)
    ]
    vectors_ref[...] = jnp.concatenate(vectors + [jnp.zeros((32 - len(vectors), 128), F32)], axis=0)
    for c in sent:
        c.wait()


def gradients_kernel(me_ref, keep_hbm, other_ref, vectors_ref, *refs):
    out_refs, (grads, held, keep_ref, sem) = refs[:4], refs[4:]
    copy = pltpu.make_async_copy(keep_hbm, keep_ref, sem.at[0])
    copy.start()
    for j in (0, 1):
        grads[j] = dot(other_ref[j], other_ref[2 + j], 0, 0)
    copy.wait()
    for j in (0, 1):
        grads[j] = grads[j] + dot(keep_ref[j], keep_ref[2 + j], 0, 0)

    def assemble(at, carry):
        rows48 = jnp.concatenate([grads[j, pl.ds(pl.multiple_of(24 * at, 8), 24), :] for j in (0, 1)], axis=0)
        for m in range(4):
            tiles = []
            for h in range(9 * m, 9 * m + 9):
                rb, t = h // 6, h % 6
                tiles.append(rows48[8 * rb : 8 * rb + 8, 128 * t : 128 * (t + 1)])
            tiles.append(vectors_ref[8 * m : 8 * m + 8, :])
            held[m, at] = jnp.concatenate(tiles, axis=0).astype(BF)
        return carry

    lax.fori_loop(0, held.shape[1], assemble, 0)
    for k, ref in enumerate(out_refs):
        ref[...] = held[(me_ref[0] + k) & 3]


def plus(*refs):
    total = refs[0].astype(F32)
    for r in refs[1:]:
        total = total + r.astype(F32)
    return total.astype(BF)


def sum_kernel(*refs):
    refs[-1][...] = plus(*[r[...] for r in refs[:-1]])


def last_kernel(parts_ref, out_ref):
    total = plus(*[parts_ref[i] for i in range(parts_ref.shape[0])])
    for i in range(out_ref.shape[0]):
        out_ref[i] = total


def finish_kernel(core_ref, blocks_ref, q_ref, k_ref, v_ref, o_ref, *vec_refs):
    blocks = blocks_ref[...].astype(F32)
    first_core = core_ref[0] == 0
    rows48, vectors = [], []
    for at in (0, 4):
        tiles = [blocks[at + m, 8 * i : 8 * i + 8] for m in range(4) for i in range(9)]
        rows48.append(
            jnp.concatenate([jnp.concatenate(tiles[6 * rb : 6 * rb + 6], axis=1) for rb in range(6)], axis=0)
        )
        vectors.append(jnp.concatenate([blocks[at + m, 72:] for m in range(4)], axis=0))
    for pair, refs in ((rows48[0], (q_ref, k_ref)), (rows48[1], (v_ref, o_ref))):
        for i, ref in enumerate(refs):
            ref[...] = jnp.where(first_core, pair[24 * i : 24 * i + 12], pair[24 * i + 12 : 24 * i + 24])
    vectors = vectors[0] + vectors[1]
    for i, ref in enumerate(vec_refs):
        for t in range(6):
            ref[pl.ds(128 * t, 128)] = vectors[6 * i + t]


def shape(dims, kind=BF):
    return jax.ShapeDtypeStruct(dims, kind)


def swap(x, axes):
    return lax.all_to_all(x, axes, split_axis=0, concat_axis=0, tiled=True)


def body(
    cand_item,
    list_place,
    item_table,
    query_vec,
    labels,
    query_weight,
    key_weight,
    value_weight,
    output_weight,
    gain_attn,
    gain_score,
    w_score,
):
    queries, size = cand_item.shape
    stored, slab = item_table.shape
    width = query_vec.shape[1]
    n_dp = lax.axis_size(ROWS)
    n_mp = lax.axis_size("x")
    n_yz = lax.axis_size(("y", "z"))
    slots = n_dp * CAP

    along_x = lax.axis_index("x").astype(jnp.int32).reshape(1)
    core = lax.axis_index("c").astype(jnp.int32).reshape(1)

    ids = exchange([cand_item] * 4, "x")
    request, slot = call(
        routing_kernel,
        [shape((n_dp, CAP), jnp.int32), shape((n_mp * queries, size), jnp.int32)],
        (along_x, *ids, list_place.reshape(1, -1)),
        8, 3 * 10**8, 10**6,
        [
            pltpu.VMEM((n_mp, queries, size), jnp.int32),
            pltpu.VMEM((1, list_place.shape[0]), jnp.int32),
            pltpu.SemaphoreType.DMA((2,)),
        ],
        1, (1, 5),
    )
    asked = swap(request, ROWS)
    table = call(
        load_kernel, pltpu.VMEM((256, stored), BF), (item_table.T,), 4, 10**6, 2 * 10**6,
        [pltpu.SemaphoreType.DMA((2,))], 0, (0,), (request,),
    )
    found = call(
        owner_kernel, shape((n_dp, 48, 128)), (asked, inside(table)), 16, 2 * 10**9, 2 * 10**6
    )
    fetched = swap(found, ROWS)
    pieces = call(
        pieces_kernel, [pltpu.HBM((384, 128), BF)] + [shape((384, 128))] * 3, (along_x, slot, fetched),
        16, 10**9, 2 * 10**6, [pltpu.VMEM((384, 128), BF), pltpu.SemaphoreType.DMA((1,))], 1,
    )
    rows_in = exchange(pieces, "x")
    acts = pltpu.HBM((4, queries * size, width), BF)
    outs = call(
        step_kernel,
        [shape((queries, 128), F32), shape((queries, width), F32)]
        + [shape((384, 128))] * n_mp
        + [acts] * 2
        + [shape((32, 128), F32)],
        (
            along_x, core, *rows_in, query_vec, labels,
            query_weight, key_weight, value_weight, output_weight,
            gain_attn.reshape(1, -1), gain_score.reshape(1, -1), w_score.reshape(1, -1),
        ),
        32, 4 * 10**9, 10**7,
        [
            pltpu.VMEM((n_mp, 384, 128), BF),
            pltpu.VMEM((HEADS * queries // 2, 128, 256), F32),
            pltpu.VMEM((HEADS * queries // 2, 128, 256), F32),
        ]
        + [pltpu.VMEM((width, width), BF)] * 4
        + [pltpu.VMEM((4, queries * size, width), BF)] * 2
        + [pltpu.SemaphoreType.DMA((7,))],
        2, (2, 8, 9, 10, 11),
    )
    losses, query_grad, diff_base = outs[0], outs[1], outs[2:6]
    keep, send, vectors = outs[6:]

    column_grads = exchange(diff_base, "x")

    other = lax.ppermute(send, "c", [(0, 1), (1, 0)])
    block = shape((n_yz, 80, 128))
    blocks = call(
        gradients_kernel, [block] * n_mp, (along_x, keep, other, vectors), 32, 2 * 10**9, 10**7,
        [
            pltpu.VMEM((2, width, width), F32),
            pltpu.VMEM((n_mp, n_yz, 80, 128), BF),
            pltpu.VMEM((4, queries * size, width), BF),
            pltpu.SemaphoreType.DMA((1,)),
        ],
        1, (1,), column_grads[1:],
    )
    blocks = exchange(blocks, "x")

    outgoing = call(
        slots_kernel, shape((n_dp, 48, 128)), (along_x, slot, *column_grads), 16, 10**9, 2 * 10**6,
        [pltpu.VMEM((n_mp, 384, 128), BF)], 1, awaited=(blocks[0],),
    )
    arrived = swap(outgoing, ROWS)
    table_grad = call(
        landing_kernel,
        shape((slab, stored), F32),
        (asked, arrived),
        20, 2 * 10**9, 4 * 10**6,
    ).T

    over_x = call(sum_kernel, block, tuple(blocks), 8, 10**6, 10**7, awaited=(arrived,))
    copies = call(last_kernel, shape((2 * n_mp, 80, 128)), (swap(over_x, ("y", "z")),), 4, 10**6, 10**6)
    blocks = swap(copies, ("c", "x"))
    rows = width // n_dp
    finished = call(
        finish_kernel,
        [shape((rows, width), F32)] * 4 + [shape((width,), F32)] * 3,
        (core, blocks), 4, 10**6, 10**6, (), 1,
    )
    return (
        losses[:, 0],
        table_grad,
        query_grad,
        *finished,
    )


def solution(mesh):
    grid = Mesh(mesh.devices.reshape(4, 8, 2, 4), ("y", "z", "c", "x"))
    each = P(("y", "z", "c", "x"), None)
    placed = (each, P(), P(ROWS, "x"), each, each, P(), P(), P(), P(), P(), P(), P())
    return jax.shard_map(
        body,
        mesh=grid,
        in_specs=placed,
        out_specs=(
            P(("y", "z", "c", "x")),
            P(ROWS, "x"),
            each,
            P(ROWS, None),
            P(ROWS, None),
            P(ROWS, None),
            P(ROWS, None),
            P(),
            P(),
            P(),
        ),
        check_vma=False,
    )
```

profile of v0, /device:TPU:1, one launch (start us, length us, event | category | flops | bytes accessed | tf_op | source)
XLA Modules:
  0.0 187.0 jit_solution(8112199771030968460)
XLA Ops:
  0.6 3.7 %collective-permute-start.1 = (s32[2,128]{1,0:T(2,128)}, s32[2,128]{1,0:T(2,128)S(1)}, u32[]{:S(2)}, u32[]{:S(2)}) collective-permute-start(s32[2,128]{1,0:T(2,128)} %refs_1_.1), channel_id=1, source_target_pairs={{0,2},{1,3},{2,0},{3,1},{4,6},{5,7},{6,4},{7,5},{8,10},{9,11},{10,... | collective-permute-start | bytes 3080 | tf_op jit(solution)/shard_map/ppermute | solution.py:72
  4.3 0.3 collective-permute-start
  4.6 2.4 %collective-permute-start.2 = (s32[2,128]{1,0:T(2,128)}, s32[2,128]{1,0:T(2,128)S(1)}, u32[]{:S(2)}, u32[]{:S(2)}) collective-permute-start(s32[2,128]{1,0:T(2,128)} %refs_1_.1), channel_id=1, source_target_pairs={{0,3},{1,0},{2,1},{3,2},{4,7},{5,4},{6,5},{7,6},{8,11},{9,8},{10,9... | collective-permute-start | bytes 3080 | tf_op jit(solution)/shard_map/ppermute | solution.py:72
  7.0 0.0 collective-permute-done.1.refs_3_
  7.0 1.5 collective-permute-done.refs_2_
  8.4 0.0 collective-permute-done.2.refs_4_
  8.4 4.1 %shard_map.195 = (s32[64,32]{1,0:T(8,128)}, s32[8,128]{1,0:T(8,128)S(1)}) custom-call(s32[1]{0:T(128)} %bitcast.refs_0_, s32[2,128]{1,0:T(2,128)} %refs_1_.1, s32[2,128]{1,0:T(2,128)S(1)} %collective-permute-done.refs_2_, s32[2,128]{1,0:T(2,128)S(1)} %collective-permute-done.1.refs_3_, s32[2,128]{1,0:T(2,128)S(1)} %collective-permute-done.2.refs_4_, ...), custom_call_target="tpu_custom_call" | custom-call | flops 300000000 | bytes 1000000 | tf_op jit(solution)/shard_map/pallas_call | solution.py:60
  12.6 13.5 %all-to-all-start = ((s32[64,1,32]{2,1,0:T(1,128)}), s32[64,1,32]{2,1,0:T(1,128)S(1)}, u32[]{:S(2)}, u32[]{:S(2)}) async-start(s32[64,1,32]{2,1,0:T(1,128)} %bitcast.4), calls=%async_computation | async-start | bytes 65536 | tf_op jit(solution)/shard_map/all_to_all | solution.py:511
  26.1 1.2 shard_map.196.refs_1_
  27.3 8.0 %all-to-all-done = s32[64,1,32]{2,1,0:T(1,128)S(1)} async-done(((s32[64,1,32]{2,1,0:T(1,128)}), s32[64,1,32]{2,1,0:T(1,128)S(1)}, u32[]{:S(2)}, u32[]{:S(2)}) %all-to-all-start) | async-done | bytes 8224 | tf_op jit(solution)/shard_map/all_to_all | solution.py:511
  35.3 2.4 %shard_map.197 = bf16[64,48,128]{2,1,0:T(8,128)(2,1)S(1)} custom-call(s32[64,32]{1,0:T(8,128)S(1)} %bitcast.9, bf16[256,2048]{1,0:T(8,128)(2,1)S(1)} %shard_map.196.refs_1_), custom_call_target="tpu_custom_call" | custom-call | flops 2000000000 | bytes 2000000 | tf_op jit(solution)/shard_map/pallas_call | solution.py:60
  37.7 27.0 %all_to_all.31.refs_2_ = bf16[64,48,128]{2,1,0:T(8,128)(2,1)S(1)} all-to-all(bf16[64,48,128]{2,1,0:T(8,128)(2,1)S(1)} %shard_map.197), channel_id=1, replica_groups=mesh['y'=4,'z'=8,'c'=2,'x'=4] {'y','z','c'}, dimensions={0} | all-to-all | bytes 1572864 | tf_op jit(solution)/shard_map/all_to_all | solution.py:511
  64.7 0.0 copy-start.3
  64.7 0.0 copy-start.4
  64.7 0.0 copy-start.5
  64.7 0.0 copy-start.1
  64.7 0.0 copy-start.2
  64.8 1.8 shard_map.198
  66.6 0.1 collective-permute-start.3
  66.7 4.1 %collective-permute-start.4 = (bf16[384,128]{1,0:T(8,128)(2,1)S(1)}, bf16[384,128]{1,0:T(8,128)(2,1)S(1)}, u32[]{:S(2)}, u32[]{:S(2)}) collective-permute-start(bf16[384,128]{1,0:T(8,128)(2,1)S(1)} %get-tuple-element.40), channel_id=1, source_target_pairs={{0,2},{1,3},{2,0},{3,1},{4,6},{5,7},{6,4},{7,5},{8,10},{9,11},{10,... | collective-permute-start | bytes 294920 | tf_op jit(solution)/shard_map/ppermute | solution.py:72
  70.8 0.0 collective-permute-start.5
  70.8 0.0 copy-done.3
  70.8 0.0 copy-done.4
  70.8 0.0 copy-done.5
  70.9 1.6 collective-permute-done.3.refs_3_
  72.4 3.0 %collective-permute-done.4.refs_4_ = bf16[384,128]{1,0:T(8,128)(2,1)S(1)} collective-permute-done((bf16[384,128]{1,0:T(8,128)(2,1)S(1)}, bf16[384,128]{1,0:T(8,128)(2,1)S(1)}, u32[]{:S(2)}, u32[]{:S(2)}) %collective-permute-start.4) | collective-permute-done | bytes 98336 | tf_op jit(solution)/shard_map/ppermute | solution.py:72
  75.4 0.0 collective-permute-done.5.refs_5_
  75.4 0.0 copy-done.1
  75.4 0.0 copy-done.2
  75.4 12.7 %shard_map.199 = (f32[2,128]{1,0:T(2,128)S(1)}, f32[2,768]{1,0:T(2,128)}, bf16[384,128]{1,0:T(8,128)(2,1)S(1)}, bf16[384,128]{1,0:T(8,128)(2,1)S(1)}, bf16[384,1...) custom-call(s32[1]{0:T(128)} %bitcast.refs_0_, ...), custom_call_target="tpu_custom_call" | custom-call | flops 4000000000 | bytes 10000000 | tf_op jit(solution)/shard_map/pallas_call | solution.py:60
  88.2 1.3 collective-permute-start.9
  89.5 0.0 collective-permute-start.6
  89.5 3.1 %collective-permute-start.7 = (bf16[384,128]{1,0:T(8,128)(2,1)S(1)}, bf16[384,128]{1,0:T(8,128)(2,1)S(1)}, u32[]{:S(2)}, u32[]{:S(2)}) collective-permute-start(bf16[384,128]{1,0:T(8,128)(2,1)S(1)} %get-tuple-element.45), channel_id=1, source_target_pairs={{0,2},{1,3},{2,0},{3,1},{4,6},{5,7},{6,4},{7,5},{8,10},{9,11},{10,... | collective-permute-start | bytes 294920 | tf_op jit(solution)/shard_map/ppermute | solution.py:72
  92.6 0.0 collective-permute-start.8
  92.6 2.5 %collective-permute-done.6.refs_4_.refs_3_ = bf16[384,128]{1,0:T(8,128)(2,1)S(1)} collective-permute-done((bf16[384,128]{1,0:T(8,128)(2,1)S(1)}, bf16[384,128]{1,0:T(8,128)(2,1)S(1)}, u32[]{:S(2)}, u32[]{:S(2)}) %collective-permute-start.6) | collective-permute-done | bytes 98336 | tf_op jit(solution)/shard_map/ppermute | solution.py:72
  95.1 2.5 %collective-permute-done.7.refs_5_.refs_4_ = bf16[384,128]{1,0:T(8,128)(2,1)S(1)} collective-permute-done((bf16[384,128]{1,0:T(8,128)(2,1)S(1)}, bf16[384,128]{1,0:T(8,128)(2,1)S(1)}, u32[]{:S(2)}, u32[]{:S(2)}) %collective-permute-start.7) | collective-permute-done | bytes 98336 | tf_op jit(solution)/shard_map/ppermute | solution.py:72
  97.6 0.0 collective-permute-done.8.refs_6_.refs_5_
  97.6 0.0 collective-permute-done.9.refs_2_
  97.6 4.3 %shard_map.200 = (bf16[32,80,128]{2,1,0:T(8,128)(2,1)S(1)}, bf16[32,80,128]{2,1,0:T(8,128)(2,1)}, bf16[32,80,128]{2,1,0:T(8,128)(2,1)}, bf16[32,80,128]{2,1,0:T(8,128)(2,1)S(1)}) custom-call(s32[1]{0:T(128)} %bitcast.refs_0_, bf16[4,256,768]{2,1,0:T(8,128)(2,1)} %get-tuple-element.47.refs_1_, bf16[4,256,768]{2,1,0:T(8,128)(2,1)S(1)} %collective-permute-done.9.refs_2_, ...), custom_call_target="tpu_custom_call" | custom-call | flops 2000000000 | bytes 10000000 | tf_op jit(solution)/shard_map/pallas_call | solution.py:60
  101.8 0.0 copy-start
  101.8 0.8 copy-done
  102.7 2.2 %shard_map.201 = bf16[64,48,128]{2,1,0:T(8,128)(2,1)} custom-call(s32[1]{0:T(128)} %bitcast.refs_0_, s32[8,128]{1,0:T(8,128)S(1)} %get-tuple-element.36.refs_1_, bf16[384,128]{1,0:T(8,128)(2,1)S(1)} %get-tuple-element.43.refs_2_, bf16[384,128]{1,0:T(8,128)(2,1)S(1)} %collective-permute-done.6.refs_4_.refs_3_, ...), custom_call_target="tpu_custom_call" | custom-call | flops 1000000000 | bytes 2000000 | tf_op jit(solution)/shard_map/pallas_call | solution.py:60
  104.9 6.6 %all-to-all-start.2 = ((bf16[64,48,128]{2,1,0:T(8,128)(2,1)}), bf16[64,48,128]{2,1,0:T(8,128)(2,1)S(1)}, u32[]{:S(2)}, u32[]{:S(2)}) async-start(bf16[64,48,128]{2,1,0:T(8,128)(2,1)} %shard_map.201), calls=%async_computation.2 | async-start | bytes 1572864 | tf_op jit(solution)/shard_map/all_to_all | solution.py:511
  111.6 0.7 collective-permute-start.10
  112.2 3.0 %collective-permute-start.11 = (bf16[32,80,128]{2,1,0:T(8,128)(2,1)}, bf16[32,80,128]{2,1,0:T(8,128)(2,1)S(1)}, u32[]{:S(2)}, u32[]{:S(2)}) collective-permute-start(bf16[32,80,128]{2,1,0:T(8,128)(2,1)} %get-tuple-element.53), channel_id=1, source_target_pairs={{0,2},{1,3},{2,0},{3,1},{4,6},{5,7},{6,4},{7,5},{8,10},{9,11},{10,... | collective-permute-start | bytes 1966088 | tf_op jit(solution)/shard_map/ppermute | solution.py:72
  115.2 0.0 collective-permute-start.12
  115.2 13.7 %collective-permute-done.10.refs_1_ = bf16[32,80,128]{2,1,0:T(8,128)(2,1)S(1)} collective-permute-done((bf16[32,80,128]{2,1,0:T(8,128)(2,1)}, bf16[32,80,128]{2,1,0:T(8,128)(2,1)S(1)}, u32[]{:S(2)}, u32[]{:S(2)}) %collective-permute-start.10) | collective-permute-done | bytes 655392 | tf_op jit(solution)/shard_map/ppermute | solution.py:72
  128.9 14.9 %collective-permute-done.11.refs_2_ = bf16[32,80,128]{2,1,0:T(8,128)(2,1)S(1)} collective-permute-done((bf16[32,80,128]{2,1,0:T(8,128)(2,1)}, bf16[32,80,128]{2,1,0:T(8,128)(2,1)S(1)}, u32[]{:S(2)}, u32[]{:S(2)}) %collective-permute-start.11) | collective-permute-done | bytes 655392 | tf_op jit(solution)/shard_map/ppermute | solution.py:72
  143.9 0.0 collective-permute-done.12.refs_3_
  143.9 0.0 all-to-all-done.2.refs_1_.refs_4_
  143.9 1.2 shard_map.203
  145.0 9.6 %all-to-all-start.3 = ((bf16[32,80,128]{2,1,0:T(8,128)(2,1)}), bf16[32,80,128]{2,1,0:T(8,128)(2,1)S(1)}, u32[]{:S(2)}, u32[]{:S(2)}) async-start(bf16[32,80,128]{2,1,0:T(8,128)(2,1)} %shard_map.203), calls=%async_computation.3 | async-start | bytes 1310720 | tf_op jit(solution)/shard_map/all_to_all | solution.py:511
  154.7 0.6 slice_reduce_fusion
  155.3 16.2 %all-to-all-done.3.refs_0_ = bf16[32,80,128]{2,1,0:T(8,128)(2,1)S(1)} async-done(((bf16[32,80,128]{2,1,0:T(8,128)(2,1)}), bf16[32,80,128]{2,1,0:T(8,128)(2,1)S(1)}, u32[]{:S(2)}, u32[]{:S(2)}) %all-to-all-start.3) | async-done | bytes 655392 | tf_op jit(solution)/shard_map/all_to_all | solution.py:511
  171.5 0.8 shard_map.204
  172.3 8.6 %all-to-all-start.4 = ((bf16[8,80,128]{2,1,0:T(8,128)(2,1)}), bf16[8,80,128]{2,1,0:T(8,128)(2,1)S(1)}, u32[]{:S(2)}, u32[]{:S(2)}) async-start(bf16[8,80,128]{2,1,0:T(8,128)(2,1)} %shard_map.204), calls=%async_computation.4 | async-start | bytes 327680 | tf_op jit(solution)/shard_map/all_to_all | solution.py:511
  180.8 4.2 %shard_map.202 = f32[192,2048]{1,0:T(8,128)} custom-call(s32[64,32]{1,0:T(8,128)S(1)} %bitcast.10, bf16[64,48,128]{2,1,0:T(8,128)(2,1)S(1)} %all-to-all-done.2.refs_1_.refs_4_), custom_call_target="tpu_custom_call" | custom-call | flops 2000000000 | bytes 4000000 | tf_op jit(solution)/shard_map/pallas_call | solution.py:60
  185.0 1.3 all-to-all-done.4.refs_1_
  186.3 0.7 shard_map.205
  (3 shorter events, 0.0 us)
Async XLA Ops:
  0.6 6.3 %collective-permute-start.1 = (s32[2,128]{1,0:T(2,128)}, s32[2,128]{1,0:T(2,128)S(1)}, u32[]{:S(2)}, u32[]{:S(2)}) collective-permute-start(s32[2,128]{1,0:T(2,128)} %refs_1_.1), channel_id=1, source_target_pairs={{0,2},{1,3},{2,0},{3,1},{4,6},{5,7},{6,4},{7,5},{8,10},{9,11},{10,... | collective-permute-start | bytes 3080 | tf_op jit(solution)/shard_map/ppermute | solution.py:72
  4.3 4.1 %collective-permute-start = (s32[2,128]{1,0:T(2,128)}, s32[2,128]{1,0:T(2,128)S(1)}, u32[]{:S(2)}, u32[]{:S(2)}) collective-permute-start(s32[2,128]{1,0:T(2,128)} %refs_1_.1), channel_id=1, source_target_pairs={{0,1},{1,2},{2,3},{3,0},{4,5},{5,6},{6,7},{7,4},{8,9},{9,10},{10,1... | collective-permute-start | bytes 3080 | tf_op jit(solution)/shard_map/ppermute | solution.py:72
  4.6 3.8 %collective-permute-start.2 = (s32[2,128]{1,0:T(2,128)}, s32[2,128]{1,0:T(2,128)S(1)}, u32[]{:S(2)}, u32[]{:S(2)}) collective-permute-start(s32[2,128]{1,0:T(2,128)} %refs_1_.1), channel_id=1, source_target_pairs={{0,3},{1,0},{2,1},{3,2},{4,7},{5,4},{6,5},{7,6},{8,11},{9,8},{10,9... | collective-permute-start | bytes 3080 | tf_op jit(solution)/shard_map/ppermute | solution.py:72
  12.6 22.7 %all-to-all-start = ((s32[64,1,32]{2,1,0:T(1,128)}), s32[64,1,32]{2,1,0:T(1,128)S(1)}, u32[]{:S(2)}, u32[]{:S(2)}) async-start(s32[64,1,32]{2,1,0:T(1,128)} %bitcast.4), calls=%async_computation | async-start | bytes 65536 | tf_op jit(solution)/shard_map/all_to_all | solution.py:511
  64.7 6.1 %copy-start.3 = (f32[768]{0:T(1024)S(1)}, f32[768]{0:T(1024)}, u32[]{:S(2)}) copy-start(f32[768]{0:T(1024)} %param.21) | copy-start | bytes 9220
  64.7 6.1 %copy-start.4 = (f32[768]{0:T(1024)S(1)}, f32[768]{0:T(1024)}, u32[]{:S(2)}) copy-start(f32[768]{0:T(1024)} %param.22) | copy-start | bytes 9220
  64.7 6.1 %copy-start.5 = (f32[768]{0:T(1024)S(1)}, f32[768]{0:T(1024)}, u32[]{:S(2)}) copy-start(f32[768]{0:T(1024)} %param.23) | copy-start | bytes 9220
  64.7 10.7 %copy-start.1 = (bf16[2,768]{1,0:T(2,128)(2,1)S(1)}, bf16[2,768]{1,0:T(2,128)(2,1)}, u32[]{:S(2)}) copy-start(bf16[2,768]{1,0:T(2,128)(2,1)} %refs_6_.1) | copy-start | bytes 9220
  64.7 10.7 %copy-start.2 = (s32[2,128]{1,0:T(2,128)S(1)}, s32[2,128]{1,0:T(2,128)}, u32[]{:S(2)}) copy-start(s32[2,128]{1,0:T(2,128)} %refs_7_.1) | copy-start | bytes 3076
  66.6 5.9 %collective-permute-start.3 = (bf16[384,128]{1,0:T(8,128)(2,1)S(1)}, bf16[384,128]{1,0:T(8,128)(2,1)S(1)}, u32[]{:S(2)}, u32[]{:S(2)}) collective-permute-start(bf16[384,128]{1,0:T(8,128)(2,1)S(1)} %get-tuple-element.39), channel_id=1, source_target_pairs={{0,1},{1,2},{2,3},{3,0},{4,5},{5,6},{6,7},{7,4},{8,9},{9,10},{10,1... | collective-permute-start | bytes 294920 | tf_op jit(solution)/shard_map/ppermute | solution.py:72
  66.7 8.7 %collective-permute-start.4 = (bf16[384,128]{1,0:T(8,128)(2,1)S(1)}, bf16[384,128]{1,0:T(8,128)(2,1)S(1)}, u32[]{:S(2)}, u32[]{:S(2)}) collective-permute-start(bf16[384,128]{1,0:T(8,128)(2,1)S(1)} %get-tuple-element.40), channel_id=1, source_target_pairs={{0,2},{1,3},{2,0},{3,1},{4,6},{5,7},{6,4},{7,5},{8,10},{9,11},{10,... | collective-permute-start | bytes 294920 | tf_op jit(solution)/shard_map/ppermute | solution.py:72
  70.8 4.6 %collective-permute-start.5 = (bf16[384,128]{1,0:T(8,128)(2,1)S(1)}, bf16[384,128]{1,0:T(8,128)(2,1)S(1)}, u32[]{:S(2)}, u32[]{:S(2)}) collective-permute-start(bf16[384,128]{1,0:T(8,128)(2,1)S(1)} %get-tuple-element.41), channel_id=1, source_target_pairs={{0,3},{1,0},{2,1},{3,2},{4,7},{5,4},{6,5},{7,6},{8,11},{9,8},{10,9... | collective-permute-start | bytes 294920 | tf_op jit(solution)/shard_map/ppermute | solution.py:72
  88.2 9.4 %collective-permute-start.9 = (bf16[4,256,768]{2,1,0:T(8,128)(2,1)}, bf16[4,256,768]{2,1,0:T(8,128)(2,1)S(1)}, u32[]{:S(2)}, u32[]{:S(2)}) collective-permute-start(bf16[4,256,768]{2,1,0:T(8,128)(2,1)} %get-tuple-element.48), channel_id=1, source_target_pairs={{0,4},{4,0},{1,5},{5,1},{2,6},{6,2},{3,7},{7,3},{8,12},{12,8},{9,1... | collective-permute-start | bytes 4718600 | tf_op jit(solution)/shard_map/ppermute | solution.py:594
  89.5 5.6 %collective-permute-start.6 = (bf16[384,128]{1,0:T(8,128)(2,1)S(1)}, bf16[384,128]{1,0:T(8,128)(2,1)S(1)}, u32[]{:S(2)}, u32[]{:S(2)}) collective-permute-start(bf16[384,128]{1,0:T(8,128)(2,1)S(1)} %get-tuple-element.44), channel_id=1, source_target_pairs={{0,1},{1,2},{2,3},{3,0},{4,5},{5,6},{6,7},{7,4},{8,9},{9,10},{10,1... | collective-permute-start | bytes 294920 | tf_op jit(solution)/shard_map/ppermute | solution.py:72
  89.5 8.0 %collective-permute-start.7 = (bf16[384,128]{1,0:T(8,128)(2,1)S(1)}, bf16[384,128]{1,0:T(8,128)(2,1)S(1)}, u32[]{:S(2)}, u32[]{:S(2)}) collective-permute-start(bf16[384,128]{1,0:T(8,128)(2,1)S(1)} %get-tuple-element.45), channel_id=1, source_target_pairs={{0,2},{1,3},{2,0},{3,1},{4,6},{5,7},{6,4},{7,5},{8,10},{9,11},{10,... | collective-permute-start | bytes 294920 | tf_op jit(solution)/shard_map/ppermute | solution.py:72
  92.6 5.0 %collective-permute-start.8 = (bf16[384,128]{1,0:T(8,128)(2,1)S(1)}, bf16[384,128]{1,0:T(8,128)(2,1)S(1)}, u32[]{:S(2)}, u32[]{:S(2)}) collective-permute-start(bf16[384,128]{1,0:T(8,128)(2,1)S(1)} %get-tuple-element.46), channel_id=1, source_target_pairs={{0,3},{1,0},{2,1},{3,2},{4,7},{5,4},{6,5},{7,6},{8,11},{9,8},{10,9... | collective-permute-start | bytes 294920 | tf_op jit(solution)/shard_map/ppermute | solution.py:72
  101.8 0.9 copy-start
  104.9 39.0 %all-to-all-start.2 = ((bf16[64,48,128]{2,1,0:T(8,128)(2,1)}), bf16[64,48,128]{2,1,0:T(8,128)(2,1)S(1)}, u32[]{:S(2)}, u32[]{:S(2)}) async-start(bf16[64,48,128]{2,1,0:T(8,128)(2,1)} %shard_map.201), calls=%async_computation.2 | async-start | bytes 1572864 | tf_op jit(solution)/shard_map/all_to_all | solution.py:511
  111.6 17.4 %collective-permute-start.10 = (bf16[32,80,128]{2,1,0:T(8,128)(2,1)}, bf16[32,80,128]{2,1,0:T(8,128)(2,1)S(1)}, u32[]{:S(2)}, u32[]{:S(2)}) collective-permute-start(bf16[32,80,128]{2,1,0:T(8,128)(2,1)} %get-tuple-element.52), channel_id=1, source_target_pairs={{0,1},{1,2},{2,3},{3,0},{4,5},{5,6},{6,7},{7,4},{8,9},{9,10},{10,1... | collective-permute-start | bytes 1966088 | tf_op jit(solution)/shard_map/ppermute | solution.py:72
  112.2 31.6 %collective-permute-start.11 = (bf16[32,80,128]{2,1,0:T(8,128)(2,1)}, bf16[32,80,128]{2,1,0:T(8,128)(2,1)S(1)}, u32[]{:S(2)}, u32[]{:S(2)}) collective-permute-start(bf16[32,80,128]{2,1,0:T(8,128)(2,1)} %get-tuple-element.53), channel_id=1, source_target_pairs={{0,2},{1,3},{2,0},{3,1},{4,6},{5,7},{6,4},{7,5},{8,10},{9,11},{10,... | collective-permute-start | bytes 1966088 | tf_op jit(solution)/shard_map/ppermute | solution.py:72
  115.2 28.6 %collective-permute-start.12 = (bf16[32,80,128]{2,1,0:T(8,128)(2,1)}, bf16[32,80,128]{2,1,0:T(8,128)(2,1)S(1)}, u32[]{:S(2)}, u32[]{:S(2)}) collective-permute-start(bf16[32,80,128]{2,1,0:T(8,128)(2,1)} %copy-done), channel_id=1, source_target_pairs={{0,3},{1,0},{2,1},{3,2},{4,7},{5,4},{6,5},{7,6},{8,11},{9,8},{10,9... | collective-permute-start | bytes 1966088 | tf_op jit(solution)/shard_map/ppermute | solution.py:72
  145.0 26.5 %all-to-all-start.3 = ((bf16[32,80,128]{2,1,0:T(8,128)(2,1)}), bf16[32,80,128]{2,1,0:T(8,128)(2,1)S(1)}, u32[]{:S(2)}, u32[]{:S(2)}) async-start(bf16[32,80,128]{2,1,0:T(8,128)(2,1)} %shard_map.203), calls=%async_computation.3 | async-start | bytes 1310720 | tf_op jit(solution)/shard_map/all_to_all | solution.py:511
  172.3 14.1 %all-to-all-start.4 = ((bf16[8,80,128]{2,1,0:T(8,128)(2,1)}), bf16[8,80,128]{2,1,0:T(8,128)(2,1)S(1)}, u32[]{:S(2)}, u32[]{:S(2)}) async-start(bf16[8,80,128]{2,1,0:T(8,128)(2,1)} %shard_map.204), calls=%async_computation.4 | async-start | bytes 327680 | tf_op jit(solution)/shard_map/all_to_all | solution.py:511
where the time goes:
time: 188 us; the launch traced here: 187 us
  waiting for transfers between devices  65.2 us (35%)
  starting transfers between devices  56.9 us (30%)
  Pallas kernels  35.6 us (19%)
  blocking collectives  27 us (14%)
    ppermute x12, waiting for transfers between devices, shift(): return lax.ppermute(x, axis, [(i, (i + by) % 4) for i in range(4)])  39.6 us
    all_to_all x4, starting transfers between devices, swap(): return lax.all_to_all(x, axes, split_axis=0, concat_axis=0, tiled=True)  38.3 us
    pallas_call x11, Pallas kernels, call(): pl.pallas_call(run, out_shape=out_shape, in_specs=in_specs, out_specs=spe...  35.6 us
    all_to_all x1, blocking collectives, swap(): return lax.all_to_all(x, axes, split_axis=0, concat_axis=0, tiled=True)  27 us
    all_to_all x4, waiting for transfers between devices, swap(): return lax.all_to_all(x, axes, split_axis=0, concat_axis=0, tiled=True)  25.5 us
    ppermute x12, starting transfers between devices, shift(): return lax.ppermute(x, axis, [(i, (i + by) % 4) for i in range(4)])  17.3 us
  transfers between devices with their start and end apart: 17, of which 10 were waited for; matrix products, arithmetic and copies ran while one was open for 0% of the time, Pallas kernels for 3%

commit v1 on v0

--- a/solution.py
+++ b/solution.py
@@ -68,6 +68,16 @@
     )(*args, *awaited)
 
 
+def after(x, awaited):
+    return pl.pallas_call(
+        lambda *refs: None,
+        out_shape=shape(x.shape, x.dtype),
+        in_specs=[pl.BlockSpec(memory_space=pl.ANY)] * 2,
+        out_specs=pl.BlockSpec(memory_space=pl.ANY),
+        input_output_aliases={0: 0},
+    )(x, awaited)
+
+
 def shift(x, axis, by):
     return lax.ppermute(x, axis, [(i, (i + by) % 4) for i in range(4)])
 
@@ -115,26 +125,29 @@
     return jnp.transpose(jnp.broadcast_to(row, (128, 128)))
 
 
-def routing_kernel(me_ref, a_ref, b_ref, c_ref, d_ref, place_hbm, request_ref, slot_ref, held, place_ref, sem):
-    me = me_ref[0]
+def lookup_kernel(place_hbm, ids_hbm, lookup_ref, ids_ref, place_ref, sem):
     copies = [
         pltpu.make_async_copy(place_hbm, place_ref, sem.at[0]),
-        pltpu.make_async_copy(a_ref, held.at[me], sem.at[1]),
+        pltpu.make_async_copy(ids_hbm, ids_ref, sem.at[1]),
     ]
     for c in copies:
         c.start()
-    for k, ref in ((1, b_ref), (2, c_ref), (3, d_ref)):
-        held[(me - k) & 3] = ref[...]
     for c in copies:
         c.wait()
     place = place_ref[...]
     lists = place.shape[1]
-    lane = iota((128, 128), 1)
     owner_of_list = jnp.broadcast_to(place >> 3, (128, lists))
     row = iota((128, lists), 0)
     lookup = jnp.where(owner_of_list == row, 1.0, 0.0)
     lookup = jnp.where(row == 64, jnp.broadcast_to(place & 7, (128, lists)).astype(F32), lookup)
-    lookup = lookup.astype(BF)
+    lookup_ref[...] = lookup.astype(BF)
+
+
+def routing_kernel(me_ref, a_ref, b_ref, c_ref, d_ref, lookup_ref, request_ref, slot_ref, held):
+    collect(me_ref[0], (a_ref, b_ref, c_ref, d_ref), held)
+    lookup = lookup_ref[...]
+    lists = lookup.shape[1]
+    lane = iota((128, 128), 1)
     before = (iota((128, 128), 1) < iota((128, 128), 0)).astype(F32).astype(BF)
     carry = jnp.zeros((1, 128), F32)
     request = jnp.zeros((128, 128), F32)
@@ -235,7 +248,7 @@
             out_ref[r // CAP + i] = pack(rows[CAP * i : CAP * (i + 1)], CAP // 2)
 
 
-def landing_kernel(asked_ref, arrived_ref, out_ref):
+def landing_kernel(asked_ref, arrived_ref, out_hbm, out_ref, sem):
     arrived = unpack(arrived_ref[...])
     stored = out_ref.shape[1]
     slots = arrived.shape[0]
@@ -246,12 +259,18 @@
         [columns[g % part][CAP * (g // part) : CAP * (g // part + 1)] for g in range(4 * part)], axis=0
     )
     step = 512
+    copies = []
     lane = iota((slots, 128), 1)
     for r in range(0, stored, step):
         chosen = jnp.concatenate(
             [(column == lane + (r + 128 * t)).astype(F32).astype(BF) for t in range(step // 128)], axis=1
         )
         out_ref[:, r : r + step] = dot(arrived, chosen, 0, 0)[:SLAB]
+        at = pl.ds(r, step)
+        copies.append(pltpu.make_async_copy(out_ref.at[:, at], out_hbm.at[:, at], sem.at[r // step]))
+        copies[-1].start()
+    for c in copies:
+        c.wait()
 
 
 def lane_mean(x):
@@ -441,15 +460,16 @@
         c.wait()
 
 
-def gradients_kernel(me_ref, keep_hbm, other_ref, vectors_ref, *refs):
-    out_refs, (grads, held, keep_ref, sem) = refs[:4], refs[4:]
-    copy = pltpu.make_async_copy(keep_hbm, keep_ref, sem.at[0])
-    copy.start()
+def gradients_kernel(keep_hbm, other_ref, vectors_ref, out_ref, grads, keep_ref, sem):
+    copies = [pltpu.make_async_copy(keep_hbm.at[i], keep_ref.at[i], sem.at[i]) for i in (0, 2, 1, 3)]
+    for c in copies:
+        c.start()
     for j in (0, 1):
-        grads[j] = dot(other_ref[j], other_ref[2 + j], 0, 0)
-    copy.wait()
-    for j in (0, 1):
-        grads[j] = grads[j] + dot(keep_ref[j], keep_ref[2 + j], 0, 0)
+        copies[2 * j].wait()
+        copies[2 * j + 1].wait()
+        left = jnp.concatenate([keep_ref[j], other_ref[j]], axis=0)
+        right = jnp.concatenate([keep_ref[2 + j], other_ref[2 + j]], axis=0)
+        grads[j] = dot(left, right, 0, 0)
 
     def assemble(at, carry):
         rows48 = jnp.concatenate([grads[j, pl.ds(pl.multiple_of(24 * at, 8), 24), :] for j in (0, 1)], axis=0)
@@ -459,12 +479,10 @@
                 rb, t = h // 6, h % 6
                 tiles.append(rows48[8 * rb : 8 * rb + 8, 128 * t : 128 * (t + 1)])
             tiles.append(vectors_ref[8 * m : 8 * m + 8, :])
-            held[m, at] = jnp.concatenate(tiles, axis=0).astype(BF)
+            out_ref[m, at] = jnp.concatenate(tiles, axis=0).astype(BF)
         return carry
 
-    lax.fori_loop(0, held.shape[1], assemble, 0)
-    for k, ref in enumerate(out_refs):
-        ref[...] = held[(me_ref[0] + k) & 3]
+    lax.fori_loop(0, out_ref.shape[1], assemble, 0)
 
 
 def plus(*refs):
@@ -472,10 +490,6 @@
     for r in refs[1:]:
         total = total + r.astype(F32)
     return total.astype(BF)
-
-
-def sum_kernel(*refs):
-    refs[-1][...] = plus(*[r[...] for r in refs[:-1]])
 
 
 def last_kernel(parts_ref, out_ref):
@@ -537,17 +551,17 @@
     core = lax.axis_index("c").astype(jnp.int32).reshape(1)
 
     ids = exchange([cand_item] * 4, "x")
+    lookup, own_ids = call(
+        lookup_kernel,
+        [pltpu.VMEM((128, list_place.shape[0]), BF), pltpu.VMEM((queries, size), jnp.int32)],
+        (list_place.reshape(1, -1), cand_item), 4, 10**6, 10**6,
+        [pltpu.VMEM((1, list_place.shape[0]), jnp.int32), pltpu.SemaphoreType.DMA((2,))], 0, (0, 1),
+    )
     request, slot = call(
         routing_kernel,
         [shape((n_dp, CAP), jnp.int32), shape((n_mp * queries, size), jnp.int32)],
-        (along_x, *ids, list_place.reshape(1, -1)),
-        8, 3 * 10**8, 10**6,
-        [
-            pltpu.VMEM((n_mp, queries, size), jnp.int32),
-            pltpu.VMEM((1, list_place.shape[0]), jnp.int32),
-            pltpu.SemaphoreType.DMA((2,)),
-        ],
-        1, (1, 5),
+        (along_x, own_ids, *ids[1:], lookup),
+        8, 3 * 10**8, 10**6, [pltpu.VMEM((n_mp, queries, size), jnp.int32)], 1,
     )
     asked = swap(request, ROWS)
     table = call(
@@ -592,33 +606,32 @@
     column_grads = exchange(diff_base, "x")
 
     other = lax.ppermute(send, "c", [(0, 1), (1, 0)])
-    block = shape((n_yz, 80, 128))
     blocks = call(
-        gradients_kernel, [block] * n_mp, (along_x, keep, other, vectors), 32, 2 * 10**9, 10**7,
+        gradients_kernel, shape((n_mp, n_yz, 80, 128)), (keep, other, vectors), 32, 2 * 10**9, 10**7,
         [
             pltpu.VMEM((2, width, width), F32),
-            pltpu.VMEM((n_mp, n_yz, 80, 128), BF),
             pltpu.VMEM((4, queries * size, width), BF),
-            pltpu.SemaphoreType.DMA((1,)),
+            pltpu.SemaphoreType.DMA((4,)),
         ],
-        1, (1,), column_grads[1:],
-    )
-    blocks = exchange(blocks, "x")
+        0, (0,), (column_grads[2],),
+    )
+    over_x = lax.psum_scatter(blocks.reshape(-1, 128), "x", scatter_dimension=0, tiled=True)
 
     outgoing = call(
         slots_kernel, shape((n_dp, 48, 128)), (along_x, slot, *column_grads), 16, 10**9, 2 * 10**6,
-        [pltpu.VMEM((n_mp, 384, 128), BF)], 1, awaited=(blocks[0],),
+        [pltpu.VMEM((n_mp, 384, 128), BF)], 1, awaited=(blocks,),
     )
     arrived = swap(outgoing, ROWS)
-    table_grad = call(
+    landed = call(
         landing_kernel,
-        shape((slab, stored), F32),
+        pltpu.HBM((slab, stored), F32),
         (asked, arrived),
-        20, 2 * 10**9, 4 * 10**6,
-    ).T
-
-    over_x = call(sum_kernel, block, tuple(blocks), 8, 10**6, 10**7, awaited=(arrived,))
-    copies = call(last_kernel, shape((2 * n_mp, 80, 128)), (swap(over_x, ("y", "z")),), 4, 10**6, 10**6)
+        20, 2 * 10**9, 4 * 10**6, [pltpu.VMEM((slab, stored), F32), pltpu.SemaphoreType.DMA((4,))],
+    )
+    table_grad = landed.T
+
+    parts = swap(after(over_x, arrived).reshape(n_yz, 80, 128), ("y", "z"))
+    copies = call(last_kernel, shape((2 * n_mp, 80, 128)), (parts,), 4, 10**6, 10**6, awaited=(landed,))
     blocks = swap(copies, ("c", "x"))
     rows = width // n_dp
     finished = call(

time: 188 us -> 189 us (level)
  blocking collectives: 27 us -> 57.5 us
  waiting for transfers between devices: 65.2 us -> 37.2 us
  between operations: 0.8 us -> 14.2 us
  starting transfers between devices: 56.9 us -> 43.6 us
    all_to_all x1 -> x2, blocking collectives: 27 us -> 57.5 us  [swap(): return lax.all_to_all(x, axes, split_axis=0, concat_axis=0, tiled=True)]
    ppermute x12 -> x9, waiting for transfers between devices: 39.6 us -> 11.9 us  [shift(): return lax.ppermute(x, axis, [(i, (i + by) % 4) for i in range(4)])]
    all_to_all x4 -> x3, starting transfers between devices: 38.3 us -> 28.8 us  [swap(): return lax.all_to_all(x, axes, split_axis=0, concat_axis=0, tiled=True)]
    ppermute x12 -> x9, starting transfers between devices: 17.3 us -> 13.1 us  [shift(): return lax.ppermute(x, axis, [(i, (i + by) % 4) for i in range(4)])]
    all_to_all x4 -> x3, waiting for transfers between devices: 25.5 us -> 25.3 us  [swap(): return lax.all_to_all(x, axes, split_axis=0, concat_axis=0, tiled=True)]
  transfers between devices with their start and end apart: 17 -> 14, of which waited for: 10 -> 9; matrix products, arithmetic and copies ran while one was open for 0% -> 0% of each run, Pallas kernels for 3% -> 4%
where the time goes in v1:
time: 189 us
  blocking collectives  57.5 us (30%)
  starting transfers between devices  43.6 us (23%)
  waiting for transfers between devices  37.2 us (20%)
  Pallas kernels  34.1 us (18%)
  between operations  14.2 us (8%)
  local copies, waits for them, and re-layouts  2.07 us (1%)
    all_to_all x2, blocking collectives, swap(): return lax.all_to_all(x, axes, split_axis=0, concat_axis=0, tiled=True)  57.5 us
    pallas_call x11, Pallas kernels, call(): pl.pallas_call(run, out_shape=out_shape, in_specs=in_specs, out_specs=spe...  34.1 us
    all_to_all x3, starting transfers between devices, swap(): return lax.all_to_all(x, axes, split_axis=0, concat_axis=0, tiled=True)  28.8 us
    all_to_all x3, waiting for transfers between devices, swap(): return lax.all_to_all(x, axes, split_axis=0, concat_axis=0, tiled=True)  25.3 us
    ppermute x9, starting transfers between devices, shift(): return lax.ppermute(x, axis, [(i, (i + by) % 4) for i in range(4)])  13.1 us
    ppermute x9, waiting for transfers between devices, shift(): return lax.ppermute(x, axis, [(i, (i + by) % 4) for i in range(4)])  11.9 us
  transfers between devices with their start and end apart: 14, of which 9 were waited for; matrix products, arithmetic and copies ran while one was open for 0% of the time, Pallas kernels for 4%

profile of v1, /device:TPU:1, one launch (start us, length us, event | category | flops | bytes accessed | tf_op | source)
XLA Modules:
  0.0 188.7 jit_solution(1743181025768090744)
XLA Ops:
  7.2 2.1 %collective-permute-start = (s32[2,128]{1,0:T(2,128)}, s32[2,128]{1,0:T(2,128)S(1)}, u32[]{:S(2)}, u32[]{:S(2)}) collective-permute-start(s32[2,128]{1,0:T(2,128)} %refs_1_.1), channel_id=1, source_target_pairs={{0,1},{1,2},{2,3},{3,0},{4,5},{5,6},{6,7},{7,4},{8,9},{9,10},{10,1... | collective-permute-start | bytes 3080 | tf_op jit(solution)/shard_map/ppermute | solution.py:82
  9.3 1.4 collective-permute-start.2
  10.7 1.6 collective-permute-start.1
  12.3 0.8 shard_map.195
  13.1 0.0 collective-permute-done.refs_2_
  13.1 0.0 collective-permute-done.2.refs_4_
  13.1 1.7 collective-permute-done.1.refs_3_
  14.8 3.4 %shard_map.196 = (s32[64,32]{1,0:T(8,128)}, s32[8,128]{1,0:T(8,128)S(1)}) custom-call(s32[1]{0:T(128)} %bitcast.refs_0_, s32[2,128]{1,0:T(2,128)S(1)} %get-tuple-element.34.refs_1_, s32[2,128]{1,0:T(2,128)S(1)} %collective-permute-done.refs_2_, s32[2,128]{1,0:T(2,128)S(1)} %collective-permute-done.1.refs_3_, s32[2,128]{1,0:T(2,128)S(1)} %collective-permute-done.2.refs_4_, ...), custom_call_target="tpu_custom_call" | custom-call | flops 300000000 | bytes 1000000 | tf_op jit(solution)/shard_map/pallas_call | solution.py:60
  18.2 14.1 %all-to-all-start = ((s32[64,1,32]{2,1,0:T(1,128)}), s32[64,1,32]{2,1,0:T(1,128)S(1)}, u32[]{:S(2)}, u32[]{:S(2)}) async-start(s32[64,1,32]{2,1,0:T(1,128)} %bitcast.4), calls=%async_computation | async-start | bytes 65536 | tf_op jit(solution)/shard_map/all_to_all | solution.py:525
  32.4 0.0 reduce-scatter.2.cloned.1.call-start
  32.4 1.2 shard_map.197.refs_1_
  33.6 7.9 %all-to-all-done = s32[64,1,32]{2,1,0:T(1,128)S(1)} async-done(((s32[64,1,32]{2,1,0:T(1,128)}), s32[64,1,32]{2,1,0:T(1,128)S(1)}, u32[]{:S(2)}, u32[]{:S(2)}) %all-to-all-start) | async-done | bytes 8224 | tf_op jit(solution)/shard_map/all_to_all | solution.py:525
  41.6 2.4 %shard_map.198 = bf16[64,48,128]{2,1,0:T(8,128)(2,1)S(1)} custom-call(s32[64,32]{1,0:T(8,128)S(1)} %bitcast.12, bf16[256,2048]{1,0:T(8,128)(2,1)S(1)} %shard_map.197.refs_1_), custom_call_target="tpu_custom_call" | custom-call | flops 2000000000 | bytes 2000000 | tf_op jit(solution)/shard_map/pallas_call | solution.py:60
  44.0 27.0 %all_to_all.31.refs_2_ = bf16[64,48,128]{2,1,0:T(8,128)(2,1)S(1)} all-to-all(bf16[64,48,128]{2,1,0:T(8,128)(2,1)S(1)} %shard_map.198), channel_id=1, replica_groups=mesh['y'=4,'z'=8,'c'=2,'x'=4] {'y','z','c'}, dimensions={0} | all-to-all | bytes 1572864 | tf_op jit(solution)/shard_map/all_to_all | solution.py:525
  71.1 0.0 copy-start.4
  71.1 0.0 copy-start.5
  71.1 0.0 copy-start.6
  71.1 0.0 copy-start.2
  71.1 0.0 copy-start.3
  71.1 1.8 shard_map.199
  72.9 0.1 collective-permute-start.3
  73.0 2.4 %collective-permute-start.4 = (bf16[384,128]{1,0:T(8,128)(2,1)S(1)}, bf16[384,128]{1,0:T(8,128)(2,1)S(1)}, u32[]{:S(2)}, u32[]{:S(2)}) collective-permute-start(bf16[384,128]{1,0:T(8,128)(2,1)S(1)} %get-tuple-element.40), channel_id=1, source_target_pairs={{0,2},{1,3},{2,0},{3,1},{4,6},{5,7},{6,4},{7,5},{8,10},{9,11},{10,... | collective-permute-start | bytes 294920 | tf_op jit(solution)/shard_map/ppermute | solution.py:82
  75.5 1.1 collective-permute-start.5
  76.6 0.0 copy-done.4
  76.6 0.0 copy-done.5
  76.6 0.0 copy-done.6
  76.7 1.8 collective-permute-done.3.refs_3_
  78.4 1.7 collective-permute-done.4.refs_4_
  80.1 0.5 collective-permute-done.5.refs_5_
  80.6 0.0 copy-done.2
  80.6 0.0 copy-done.3
  80.6 12.7 %shard_map.200 = (f32[2,128]{1,0:T(2,128)S(1)}, f32[2,768]{1,0:T(2,128)}, bf16[384,128]{1,0:T(8,128)(2,1)S(1)}, bf16[384,128]{1,0:T(8,128)(2,1)S(1)}, bf16[384,1...) custom-call(s32[1]{0:T(128)} %bitcast.refs_0_, ...), custom_call_target="tpu_custom_call" | custom-call | flops 4000000000 | bytes 10000000 | tf_op jit(solution)/shard_map/pallas_call | solution.py:60
  93.3 1.6 collective-permute-start.9
  95.0 1.6 collective-permute-start.7
  96.5 4.3 %collective-permute-done.7.refs_3_.refs_4_ = bf16[384,128]{1,0:T(8,128)(2,1)S(1)} collective-permute-done((bf16[384,128]{1,0:T(8,128)(2,1)S(1)}, bf16[384,128]{1,0:T(8,128)(2,1)S(1)}, u32[]{:S(2)}, u32[]{:S(2)}) %collective-permute-start.7) | collective-permute-done | bytes 98336 | tf_op jit(solution)/shard_map/ppermute | solution.py:82
  100.8 0.0 collective-permute-done.9.refs_1_
  100.8 5.1 %shard_map.201.refs_6_ = bf16[4,32,80,128]{3,2,1,0:T(8,128)(2,1)} custom-call(bf16[4,256,768]{2,1,0:T(8,128)(2,1)} %get-tuple-element.47.refs_0_, bf16[4,256,768]{2,1,0:T(8,128)(2,1)S(1)} %collective-permute-done.9.refs_1_, f32[32,128]{1,0:T(8,128)S(1)} %get-tuple-element.49.refs_2_, bf16[384,128]{1,0:T(8,128)(2,1)S(1)} %collective-permute-done.7.refs_3_.refs_4_), custom_call_target="tpu_custom_call" | custom-call | flops 2000000000 | bytes 10000000 | tf_op jit(solution)/shard_map/pallas_call | solution.py:60
  105.9 0.0 reduce-scatter.2.cloned.1.call-update
  105.9 1.0 collective-permute-start.6
  106.9 1.8 collective-permute-start.8
  108.7 2.0 %collective-permute-done.6.refs_3_ = bf16[384,128]{1,0:T(8,128)(2,1)S(1)} collective-permute-done((bf16[384,128]{1,0:T(8,128)(2,1)S(1)}, bf16[384,128]{1,0:T(8,128)(2,1)S(1)}, u32[]{:S(2)}, u32[]{:S(2)}) %collective-permute-start.6) | collective-permute-done | bytes 98336 | tf_op jit(solution)/shard_map/ppermute | solution.py:82
  110.7 0.0 collective-permute-done.8.refs_5_
  110.7 1.4 shard_map.202
  112.0 30.5 %all_to_all.32.refs_1_ = bf16[64,48,128]{2,1,0:T(8,128)(2,1)} all-to-all(bf16[64,48,128]{2,1,0:T(8,128)(2,1)S(1)} %shard_map.202), channel_id=1, replica_groups=mesh['y'=4,'z'=8,'c'=2,'x'=4] {'y','z','c'}, dimensions={0} | all-to-all | bytes 1572864 | tf_op jit(solution)/shard_map/all_to_all | solution.py:525
  142.5 0.0 copy-start
  142.5 0.0 reduce-scatter.2.cloned.1.call-done.refs_0_
  142.5 6.4 %all-to-all-start.3 = ((bf16[32,80,128]{2,1,0:T(8,128)(2,1)}), bf16[32,80,128]{2,1,0:T(8,128)(2,1)S(1)}, u32[]{:S(2)}, u32[]{:S(2)}) async-start(bf16[32,80,128]{2,1,0:T(8,128)(2,1)} %bitcast.14), calls=%async_computation.4 | async-start | bytes 1310720 | tf_op jit(solution)/shard_map/all_to_all | solution.py:525
  148.9 0.0 copy-done
  149.0 3.8 %shard_map.203.refs_1_ = f32[192,2048]{1,0:T(8,128)} custom-call(s32[64,32]{1,0:T(8,128)S(1)} %bitcast.13, bf16[64,48,128]{2,1,0:T(8,128)(2,1)S(1)} %copy-done), custom_call_target="tpu_custom_call" | custom-call | flops 2000000000 | bytes 4000000 | tf_op jit(solution)/shard_map/pallas_call | solution.py:60
  152.8 12.5 %all-to-all-done.3.refs_0_ = bf16[32,80,128]{2,1,0:T(8,128)(2,1)S(1)} async-done(((bf16[32,80,128]{2,1,0:T(8,128)(2,1)}), bf16[32,80,128]{2,1,0:T(8,128)(2,1)S(1)}, u32[]{:S(2)}, u32[]{:S(2)}) %all-to-all-start.3) | async-done | bytes 655392 | tf_op jit(solution)/shard_map/all_to_all | solution.py:525
  165.3 0.0 copy-start.1
  165.3 1.4 copy-done.1
  166.7 0.8 shard_map.205
  167.5 8.2 %all-to-all-start.4 = ((bf16[8,80,128]{2,1,0:T(8,128)(2,1)}), bf16[8,80,128]{2,1,0:T(8,128)(2,1)S(1)}, u32[]{:S(2)}, u32[]{:S(2)}) async-start(bf16[8,80,128]{2,1,0:T(8,128)(2,1)} %shard_map.205), calls=%async_computation.5 | async-start | bytes 327680 | tf_op jit(solution)/shard_map/all_to_all | solution.py:525
  175.7 0.6 slice_reduce_fusion
  176.3 4.9 %all-to-all-done.4.refs_1_ = bf16[8,80,128]{2,1,0:T(8,128)(2,1)S(1)} async-done(((bf16[8,80,128]{2,1,0:T(8,128)(2,1)}), bf16[8,80,128]{2,1,0:T(8,128)(2,1)S(1)}, u32[]{:S(2)}, u32[]{:S(2)}) %all-to-all-start.4) | async-done | bytes 163872 | tf_op jit(solution)/shard_map/all_to_all | solution.py:525
  181.2 0.7 shard_map.206
  (4 shorter events, 0.0 us)
Async XLA Ops:
  7.2 5.9 %collective-permute-start = (s32[2,128]{1,0:T(2,128)}, s32[2,128]{1,0:T(2,128)S(1)}, u32[]{:S(2)}, u32[]{:S(2)}) collective-permute-start(s32[2,128]{1,0:T(2,128)} %refs_1_.1), channel_id=1, source_target_pairs={{0,1},{1,2},{2,3},{3,0},{4,5},{5,6},{6,7},{7,4},{8,9},{9,10},{10,1... | collective-permute-start | bytes 3080 | tf_op jit(solution)/shard_map/ppermute | solution.py:82
  9.3 3.8 %collective-permute-start.2 = (s32[2,128]{1,0:T(2,128)}, s32[2,128]{1,0:T(2,128)S(1)}, u32[]{:S(2)}, u32[]{:S(2)}) collective-permute-start(s32[2,128]{1,0:T(2,128)} %refs_1_.1), channel_id=1, source_target_pairs={{0,3},{1,0},{2,1},{3,2},{4,7},{5,4},{6,5},{7,6},{8,11},{9,8},{10,9... | collective-permute-start | bytes 3080 | tf_op jit(solution)/shard_map/ppermute | solution.py:82
  10.7 4.1 %collective-permute-start.1 = (s32[2,128]{1,0:T(2,128)}, s32[2,128]{1,0:T(2,128)S(1)}, u32[]{:S(2)}, u32[]{:S(2)}) collective-permute-start(s32[2,128]{1,0:T(2,128)} %refs_1_.1), channel_id=1, source_target_pairs={{0,2},{1,3},{2,0},{3,1},{4,6},{5,7},{6,4},{7,5},{8,10},{9,11},{10,... | collective-permute-start | bytes 3080 | tf_op jit(solution)/shard_map/ppermute | solution.py:82
  18.2 23.4 %all-to-all-start = ((s32[64,1,32]{2,1,0:T(1,128)}), s32[64,1,32]{2,1,0:T(1,128)S(1)}, u32[]{:S(2)}, u32[]{:S(2)}) async-start(s32[64,1,32]{2,1,0:T(1,128)} %bitcast.4), calls=%async_computation | async-start | bytes 65536 | tf_op jit(solution)/shard_map/all_to_all | solution.py:525
  32.4 110.1 %reduce-scatter.2.cloned.1.call-start = ((), (), s32[]{:S(2)}) async-start(), calls=%async_computation.6 | async-start | bytes 3276800 | tf_op jit(solution)/shard_map/reduce_scatter | solution.py:618
  71.1 5.5 %copy-start.4 = (f32[768]{0:T(1024)S(1)}, f32[768]{0:T(1024)}, u32[]{:S(2)}) copy-start(f32[768]{0:T(1024)} %param.21) | copy-start | bytes 9220
  71.1 5.5 %copy-start.5 = (f32[768]{0:T(1024)S(1)}, f32[768]{0:T(1024)}, u32[]{:S(2)}) copy-start(f32[768]{0:T(1024)} %param.22) | copy-start | bytes 9220
  71.1 5.6 %copy-start.6 = (f32[768]{0:T(1024)S(1)}, f32[768]{0:T(1024)}, u32[]{:S(2)}) copy-start(f32[768]{0:T(1024)} %param.23) | copy-start | bytes 9220
  71.1 9.5 %copy-start.2 = (bf16[2,768]{1,0:T(2,128)(2,1)S(1)}, bf16[2,768]{1,0:T(2,128)(2,1)}, u32[]{:S(2)}) copy-start(bf16[2,768]{1,0:T(2,128)(2,1)} %refs_6_.1) | copy-start | bytes 9220
  71.1 9.5 %copy-start.3 = (s32[2,128]{1,0:T(2,128)S(1)}, s32[2,128]{1,0:T(2,128)}, u32[]{:S(2)}) copy-start(s32[2,128]{1,0:T(2,128)} %refs_7_.1) | copy-start | bytes 3076
  72.9 5.5 %collective-permute-start.3 = (bf16[384,128]{1,0:T(8,128)(2,1)S(1)}, bf16[384,128]{1,0:T(8,128)(2,1)S(1)}, u32[]{:S(2)}, u32[]{:S(2)}) collective-permute-start(bf16[384,128]{1,0:T(8,128)(2,1)S(1)} %get-tuple-element.39), channel_id=1, source_target_pairs={{0,1},{1,2},{2,3},{3,0},{4,5},{5,6},{6,7},{7,4},{8,9},{9,10},{10,1... | collective-permute-start | bytes 294920 | tf_op jit(solution)/shard_map/ppermute | solution.py:82
  73.0 7.1 %collective-permute-start.4 = (bf16[384,128]{1,0:T(8,128)(2,1)S(1)}, bf16[384,128]{1,0:T(8,128)(2,1)S(1)}, u32[]{:S(2)}, u32[]{:S(2)}) collective-permute-start(bf16[384,128]{1,0:T(8,128)(2,1)S(1)} %get-tuple-element.40), channel_id=1, source_target_pairs={{0,2},{1,3},{2,0},{3,1},{4,6},{5,7},{6,4},{7,5},{8,10},{9,11},{10,... | collective-permute-start | bytes 294920 | tf_op jit(solution)/shard_map/ppermute | solution.py:82
  75.5 5.1 %collective-permute-start.5 = (bf16[384,128]{1,0:T(8,128)(2,1)S(1)}, bf16[384,128]{1,0:T(8,128)(2,1)S(1)}, u32[]{:S(2)}, u32[]{:S(2)}) collective-permute-start(bf16[384,128]{1,0:T(8,128)(2,1)S(1)} %get-tuple-element.41), channel_id=1, source_target_pairs={{0,3},{1,0},{2,1},{3,2},{4,7},{5,4},{6,5},{7,6},{8,11},{9,8},{10,9... | collective-permute-start | bytes 294920 | tf_op jit(solution)/shard_map/ppermute | solution.py:82
  93.3 7.5 %collective-permute-start.9 = (bf16[4,256,768]{2,1,0:T(8,128)(2,1)}, bf16[4,256,768]{2,1,0:T(8,128)(2,1)S(1)}, u32[]{:S(2)}, u32[]{:S(2)}) collective-permute-start(bf16[4,256,768]{2,1,0:T(8,128)(2,1)} %get-tuple-element.48), channel_id=1, source_target_pairs={{0,4},{4,0},{1,5},{5,1},{2,6},{6,2},{3,7},{7,3},{8,12},{12,8},{9,1... | collective-permute-start | bytes 4718600 | tf_op jit(solution)/shard_map/ppermute | solution.py:608
  95.0 5.9 %collective-permute-start.7 = (bf16[384,128]{1,0:T(8,128)(2,1)S(1)}, bf16[384,128]{1,0:T(8,128)(2,1)S(1)}, u32[]{:S(2)}, u32[]{:S(2)}) collective-permute-start(bf16[384,128]{1,0:T(8,128)(2,1)S(1)} %get-tuple-element.45), channel_id=1, source_target_pairs={{0,2},{1,3},{2,0},{3,1},{4,6},{5,7},{6,4},{7,5},{8,10},{9,11},{10,... | collective-permute-start | bytes 294920 | tf_op jit(solution)/shard_map/ppermute | solution.py:82
  105.9 4.8 %collective-permute-start.6 = (bf16[384,128]{1,0:T(8,128)(2,1)S(1)}, bf16[384,128]{1,0:T(8,128)(2,1)S(1)}, u32[]{:S(2)}, u32[]{:S(2)}) collective-permute-start(bf16[384,128]{1,0:T(8,128)(2,1)S(1)} %get-tuple-element.44), channel_id=1, source_target_pairs={{0,1},{1,2},{2,3},{3,0},{4,5},{5,6},{6,7},{7,4},{8,9},{9,10},{10,1... | collective-permute-start | bytes 294920 | tf_op jit(solution)/shard_map/ppermute | solution.py:82
  106.9 3.8 %collective-permute-start.8 = (bf16[384,128]{1,0:T(8,128)(2,1)S(1)}, bf16[384,128]{1,0:T(8,128)(2,1)S(1)}, u32[]{:S(2)}, u32[]{:S(2)}) collective-permute-start(bf16[384,128]{1,0:T(8,128)(2,1)S(1)} %get-tuple-element.46), channel_id=1, source_target_pairs={{0,3},{1,0},{2,1},{3,2},{4,7},{5,4},{6,5},{7,6},{8,11},{9,8},{10,9... | collective-permute-start | bytes 294920 | tf_op jit(solution)/shard_map/ppermute | solution.py:82
  142.5 6.4 %copy-start = (bf16[64,48,128]{2,1,0:T(8,128)(2,1)S(1)}, bf16[64,48,128]{2,1,0:T(8,128)(2,1)}, u32[]{:S(2)}) copy-start(bf16[64,48,128]{2,1,0:T(8,128)(2,1)} %all_to_all.32.refs_1_) | copy-start | bytes 2359300
  142.5 22.8 %all-to-all-start.3 = ((bf16[32,80,128]{2,1,0:T(8,128)(2,1)}), bf16[32,80,128]{2,1,0:T(8,128)(2,1)S(1)}, u32[]{:S(2)}, u32[]{:S(2)}) async-start(bf16[32,80,128]{2,1,0:T(8,128)(2,1)} %bitcast.14), calls=%async_computation.4 | async-start | bytes 1310720 | tf_op jit(solution)/shard_map/all_to_all | solution.py:525
  165.3 1.4 copy-start.1
  167.5 13.7 %all-to-all-start.4 = ((bf16[8,80,128]{2,1,0:T(8,128)(2,1)}), bf16[8,80,128]{2,1,0:T(8,128)(2,1)S(1)}, u32[]{:S(2)}, u32[]{:S(2)}) async-start(bf16[8,80,128]{2,1,0:T(8,128)(2,1)} %shard_map.205), calls=%async_computation.5 | async-start | bytes 327680 | tf_op jit(solution)/shard_map/all_to_all | solution.py:525
Sparse Core Ops, SparseCore 0:
  106.0 33.2 reduce-scatter.1

commit v2 on v1

--- a/solution.py
+++ b/solution.py
@@ -248,7 +248,8 @@
             out_ref[r // CAP + i] = pack(rows[CAP * i : CAP * (i + 1)], CAP // 2)
 
 
-def landing_kernel(asked_ref, arrived_ref, out_hbm, out_ref, sem):
+def landing_kernel(asked_ref, arrived_ref, out_hbm, token_ref, out_ref, sem):
+    token_ref[...] = jnp.zeros_like(token_ref)
     arrived = unpack(arrived_ref[...])
     stored = out_ref.shape[1]
     slots = arrived.shape[0]
@@ -460,7 +461,9 @@
         c.wait()
 
 
-def gradients_kernel(keep_hbm, other_ref, vectors_ref, out_ref, grads, keep_ref, sem):
+def gradients_kernel(me_ref, keep_hbm, other_ref, vectors_ref, *refs):
+    out_refs, (token_ref, grads, held, keep_ref, sem) = refs[:4], refs[4:]
+    token_ref[...] = jnp.zeros_like(token_ref)
     copies = [pltpu.make_async_copy(keep_hbm.at[i], keep_ref.at[i], sem.at[i]) for i in (0, 2, 1, 3)]
     for c in copies:
         c.start()
@@ -479,10 +482,16 @@
                 rb, t = h // 6, h % 6
                 tiles.append(rows48[8 * rb : 8 * rb + 8, 128 * t : 128 * (t + 1)])
             tiles.append(vectors_ref[8 * m : 8 * m + 8, :])
-            out_ref[m, at] = jnp.concatenate(tiles, axis=0).astype(BF)
+            held[m, at] = jnp.concatenate(tiles, axis=0).astype(BF)
         return carry
 
-    lax.fori_loop(0, out_ref.shape[1], assemble, 0)
+    lax.fori_loop(0, held.shape[1], assemble, 0)
+    copies = []
+    for k, ref in enumerate(out_refs):
+        copies.append(pltpu.make_async_copy(held.at[(me_ref[0] + k) & 3], ref, sem.at[4 + k]))
+        copies[-1].start()
+    for c in copies:
+        c.wait()
 
 
 def plus(*refs):
@@ -490,6 +499,21 @@
     for r in refs[1:]:
         total = total + r.astype(F32)
     return total.astype(BF)
+
+
+def sum_kernel(own_hbm, b_ref, c_ref, d_ref, out_hbm, own_ref, out_ref, sem):
+    copy = pltpu.make_async_copy(own_hbm, own_ref, sem.at[0])
+    copy.start()
+    copy.wait()
+    n = own_ref.shape[0] // 2
+    copies = []
+    for i in (0, 1):
+        at = pl.ds(n * i, n)
+        out_ref[n * i : n * (i + 1)] = plus(*[r[n * i : n * (i + 1)] for r in (own_ref, b_ref, c_ref, d_ref)])
+        copies.append(pltpu.make_async_copy(out_ref.at[at], out_hbm.at[at], sem.at[1 + i]))
+        copies[-1].start()
+    for c in copies:
+        c.wait()
 
 
 def last_kernel(parts_ref, out_ref):
@@ -606,32 +630,38 @@
     column_grads = exchange(diff_base, "x")
 
     other = lax.ppermute(send, "c", [(0, 1), (1, 0)])
-    blocks = call(
-        gradients_kernel, shape((n_mp, n_yz, 80, 128)), (keep, other, vectors), 32, 2 * 10**9, 10**7,
+    block = shape((n_yz, 80, 128))
+    *blocks, made = call(
+        gradients_kernel, [pltpu.HBM(block.shape, BF)] * n_mp + [shape((8, 128), F32)], (along_x, keep, other, vectors), 32, 2 * 10**9, 10**7,
         [
             pltpu.VMEM((2, width, width), F32),
+            pltpu.VMEM((n_mp, n_yz, 80, 128), BF),
             pltpu.VMEM((4, queries * size, width), BF),
-            pltpu.SemaphoreType.DMA((4,)),
+            pltpu.SemaphoreType.DMA((8,)),
         ],
-        0, (0,), (column_grads[2],),
-    )
-    over_x = lax.psum_scatter(blocks.reshape(-1, 128), "x", scatter_dimension=0, tiled=True)
+        1, (1,), column_grads[1:],
+    )
+    arrive = exchange(blocks, "x")
 
     outgoing = call(
         slots_kernel, shape((n_dp, 48, 128)), (along_x, slot, *column_grads), 16, 10**9, 2 * 10**6,
-        [pltpu.VMEM((n_mp, 384, 128), BF)], 1, awaited=(blocks,),
+        [pltpu.VMEM((n_mp, 384, 128), BF)], 1, awaited=(made,),
     )
     arrived = swap(outgoing, ROWS)
-    landed = call(
+    landed, token = call(
         landing_kernel,
-        pltpu.HBM((slab, stored), F32),
+        [pltpu.HBM((slab, stored), F32), shape((8, 128), F32)],
         (asked, arrived),
         20, 2 * 10**9, 4 * 10**6, [pltpu.VMEM((slab, stored), F32), pltpu.SemaphoreType.DMA((4,))],
     )
     table_grad = landed.T
 
-    parts = swap(after(over_x, arrived).reshape(n_yz, 80, 128), ("y", "z"))
-    copies = call(last_kernel, shape((2 * n_mp, 80, 128)), (parts,), 4, 10**6, 10**6, awaited=(landed,))
+    over_x = call(
+        sum_kernel, pltpu.HBM(block.shape, BF), tuple(arrive), 8, 10**12, 10**7,
+        [pltpu.VMEM(block.shape, BF), pltpu.VMEM(block.shape, BF), pltpu.SemaphoreType.DMA((3,))], 0, (0,),
+    )
+    parts = swap(after(over_x, arrived), ("y", "z"))
+    copies = call(last_kernel, shape((2 * n_mp, 80, 128)), (parts,), 4, 10**6, 10**6, awaited=(token,))
     blocks = swap(copies, ("c", "x"))
     rows = width // n_dp
     finished = call(

time: 189 us -> 176 us (0.931)
  blocking collectives: 57.5 us -> 27 us
  waiting for transfers between devices: 37.2 us -> 55.5 us
  between operations: 14.2 us -> 0.81 us
  starting transfers between devices: 43.6 us -> 52.5 us
  Pallas kernels: 34.1 us -> 38.3 us
    all_to_all x2 -> x1, blocking collectives: 57.5 us -> 27 us  [swap(): return lax.all_to_all(x, axes, split_axis=0, concat_axis=0, tiled=True)]
    ppermute x9 -> x12, waiting for transfers between devices: 11.9 us -> 29.9 us  [shift(): return lax.ppermute(x, axis, [(i, (i + by) % 4) for i in range(4)])]
    all_to_all x3 -> x4, starting transfers between devices: 28.8 us -> 34.6 us  [swap(): return lax.all_to_all(x, axes, split_axis=0, concat_axis=0, tiled=True)]
    pallas_call x11 -> x12, Pallas kernels: 34.1 us -> 38.3 us  [call(): pl.pallas_call(run, out_shape=out_shape, in_specs=in_specs, out_specs=spe...]
    ppermute x9 -> x12, starting transfers between devices: 13.1 us -> 16.3 us  [shift(): return lax.ppermute(x, axis, [(i, (i + by) % 4) for i in range(4)])]
    all_to_all x3 -> x4, waiting for transfers between devices: 25.3 us -> 25.6 us  [swap(): return lax.all_to_all(x, axes, split_axis=0, concat_axis=0, tiled=True)]
  transfers between devices with their start and end apart: 14 -> 17, of which waited for: 9 -> 12; matrix products, arithmetic and copies ran while one was open for 0% -> 0% of each run, Pallas kernels for 4% -> 6%
where the time goes in v2:
time: 176 us; the launch traced here: 175 us
  waiting for transfers between devices  55.5 us (32%)
  starting transfers between devices  52.5 us (30%)
  Pallas kernels  38.3 us (22%)
  blocking collectives  27 us (15%)
    pallas_call x12, Pallas kernels, call(): pl.pallas_call(run, out_shape=out_shape, in_specs=in_specs, out_specs=spe...  38.3 us
    all_to_all x4, starting transfers between devices, swap(): return lax.all_to_all(x, axes, split_axis=0, concat_axis=0, tiled=True)  34.6 us
    ppermute x12, waiting for transfers between devices, shift(): return lax.ppermute(x, axis, [(i, (i + by) % 4) for i in range(4)])  29.9 us
    all_to_all x1, blocking collectives, swap(): return lax.all_to_all(x, axes, split_axis=0, concat_axis=0, tiled=True)  27 us
    all_to_all x4, waiting for transfers between devices, swap(): return lax.all_to_all(x, axes, split_axis=0, concat_axis=0, tiled=True)  25.6 us
    ppermute x12, starting transfers between devices, shift(): return lax.ppermute(x, axis, [(i, (i + by) % 4) for i in range(4)])  16.3 us
  transfers between devices with their start and end apart: 17, of which 12 were waited for; matrix products, arithmetic and copies ran while one was open for 0% of the time, Pallas kernels for 6%

profile of v2, /device:TPU:1, one launch (start us, length us, event | category | flops | bytes accessed | tf_op | source)
XLA Modules:
  0.0 174.9 jit_solution(3189643862838282020)
XLA Ops:
  0.6 2.1 %collective-permute-start = (s32[2,128]{1,0:T(2,128)}, s32[2,128]{1,0:T(2,128)S(1)}, u32[]{:S(2)}, u32[]{:S(2)}) collective-permute-start(s32[2,128]{1,0:T(2,128)} %refs_1_.1), channel_id=1, source_target_pairs={{0,1},{1,2},{2,3},{3,0},{4,5},{5,6},{6,7},{7,4},{8,9},{9,10},{10,1... | collective-permute-start | bytes 3080 | tf_op jit(solution)/shard_map/ppermute | solution.py:82
  2.8 1.4 collective-permute-start.2
  4.1 1.6 collective-permute-start.1
  5.8 0.8 shard_map.195
  6.5 0.0 collective-permute-done.refs_2_
  6.5 0.0 collective-permute-done.2.refs_4_
  6.5 1.7 collective-permute-done.1.refs_3_
  8.3 3.4 %shard_map.196 = (s32[64,32]{1,0:T(8,128)}, s32[8,128]{1,0:T(8,128)S(1)}) custom-call(s32[1]{0:T(128)} %bitcast.refs_0_, s32[2,128]{1,0:T(2,128)S(1)} %get-tuple-element.41.refs_1_, s32[2,128]{1,0:T(2,128)S(1)} %collective-permute-done.refs_2_, s32[2,128]{1,0:T(2,128)S(1)} %collective-permute-done.1.refs_3_, s32[2,128]{1,0:T(2,128)S(1)} %collective-permute-done.2.refs_4_, ...), custom_call_target="tpu_custom_call" | custom-call | flops 300000000 | bytes 1000000 | tf_op jit(solution)/shard_map/pallas_call | solution.py:60
  11.7 14.1 %all-to-all-start = ((s32[64,1,32]{2,1,0:T(1,128)}), s32[64,1,32]{2,1,0:T(1,128)S(1)}, u32[]{:S(2)}, u32[]{:S(2)}) async-start(s32[64,1,32]{2,1,0:T(1,128)} %bitcast.4), calls=%async_computation | async-start | bytes 65536 | tf_op jit(solution)/shard_map/all_to_all | solution.py:549
  25.8 1.2 shard_map.197.refs_1_
  27.1 8.0 %all-to-all-done = s32[64,1,32]{2,1,0:T(1,128)S(1)} async-done(((s32[64,1,32]{2,1,0:T(1,128)}), s32[64,1,32]{2,1,0:T(1,128)S(1)}, u32[]{:S(2)}, u32[]{:S(2)}) %all-to-all-start) | async-done | bytes 8224 | tf_op jit(solution)/shard_map/all_to_all | solution.py:549
  35.1 2.4 %shard_map.198 = bf16[64,48,128]{2,1,0:T(8,128)(2,1)S(1)} custom-call(s32[64,32]{1,0:T(8,128)S(1)} %bitcast.9, bf16[256,2048]{1,0:T(8,128)(2,1)S(1)} %shard_map.197.refs_1_), custom_call_target="tpu_custom_call" | custom-call | flops 2000000000 | bytes 2000000 | tf_op jit(solution)/shard_map/pallas_call | solution.py:60
  37.5 27.0 %all_to_all.31.refs_2_ = bf16[64,48,128]{2,1,0:T(8,128)(2,1)S(1)} all-to-all(bf16[64,48,128]{2,1,0:T(8,128)(2,1)S(1)} %shard_map.198), channel_id=1, replica_groups=mesh['y'=4,'z'=8,'c'=2,'x'=4] {'y','z','c'}, dimensions={0} | all-to-all | bytes 1572864 | tf_op jit(solution)/shard_map/all_to_all | solution.py:549
  64.5 0.0 copy-start.2
  64.5 0.0 copy-start.3
  64.5 0.0 copy-start.4
  64.5 0.0 copy-start
  64.5 0.0 copy-start.1
  64.6 1.8 %shard_map.199 = (bf16[384,128]{1,0:T(8,128)(2,1)}, bf16[384,128]{1,0:T(8,128)(2,1)S(1)}, bf16[384,128]{1,0:T(8,128)(2,1)S(1)}, bf16[384,128]{1,0:T(8,128)(2,1)S(1)}) custom-call(s32[1]{0:T(128)} %bitcast.refs_0_, s32[8,128]{1,0:T(8,128)S(1)} %get-tuple-element.43.refs_1_, bf16[64,48,128]{2,1,0:T(8,128)(2,1)S(1)} %all_to_all.31.refs_2_), custom_call_target="tpu_custom_call" | custom-call | flops 1000000000 | bytes 2000000 | tf_op jit(solution)/shard_map/pallas_call | solution.py:60
  66.4 0.1 collective-permute-start.3
  66.5 2.4 %collective-permute-start.4 = (bf16[384,128]{1,0:T(8,128)(2,1)S(1)}, bf16[384,128]{1,0:T(8,128)(2,1)S(1)}, u32[]{:S(2)}, u32[]{:S(2)}) collective-permute-start(bf16[384,128]{1,0:T(8,128)(2,1)S(1)} %get-tuple-element.47), channel_id=1, source_target_pairs={{0,2},{1,3},{2,0},{3,1},{4,6},{5,7},{6,4},{7,5},{8,10},{9,11},{10,... | collective-permute-start | bytes 294920 | tf_op jit(solution)/shard_map/ppermute | solution.py:82
  68.9 1.2 collective-permute-start.5
  70.1 0.0 copy-done.2
  70.1 0.0 copy-done.3
  70.1 0.0 copy-done.4
  70.1 1.7 collective-permute-done.3.refs_3_
  71.9 1.7 collective-permute-done.4.refs_4_
  73.6 0.5 collective-permute-done.5.refs_5_
  74.0 0.0 copy-done
  74.0 0.0 copy-done.1
  74.0 12.7 %shard_map.200 = (f32[2,128]{1,0:T(2,128)S(1)}, f32[2,768]{1,0:T(2,128)}, bf16[384,128]{1,0:T(8,128)(2,1)S(1)}, bf16[384,128]{1,0:T(8,128)(2,1)S(1)}, bf16[384,1...) custom-call(s32[1]{0:T(128)} %bitcast.refs_0_, ...), custom_call_target="tpu_custom_call" | custom-call | flops 4000000000 | bytes 10000000 | tf_op jit(solution)/shard_map/pallas_call | solution.py:60
  86.8 1.6 collective-permute-start.9
  88.4 0.9 collective-permute-start.6
  89.4 2.7 %collective-permute-start.7 = (bf16[384,128]{1,0:T(8,128)(2,1)S(1)}, bf16[384,128]{1,0:T(8,128)(2,1)S(1)}, u32[]{:S(2)}, u32[]{:S(2)}) collective-permute-start(bf16[384,128]{1,0:T(8,128)(2,1)S(1)} %get-tuple-element.52), channel_id=1, source_target_pairs={{0,2},{1,3},{2,0},{3,1},{4,6},{5,7},{6,4},{7,5},{8,10},{9,11},{10,... | collective-permute-start | bytes 294920 | tf_op jit(solution)/shard_map/ppermute | solution.py:82
  92.0 0.0 collective-permute-start.8
  92.1 1.9 %collective-permute-done.6.refs_4_.refs_3_ = bf16[384,128]{1,0:T(8,128)(2,1)S(1)} collective-permute-done((bf16[384,128]{1,0:T(8,128)(2,1)S(1)}, bf16[384,128]{1,0:T(8,128)(2,1)S(1)}, u32[]{:S(2)}, u32[]{:S(2)}) %collective-permute-start.6) | collective-permute-done | bytes 98336 | tf_op jit(solution)/shard_map/ppermute | solution.py:82
  94.0 3.0 %collective-permute-done.7.refs_5_.refs_4_ = bf16[384,128]{1,0:T(8,128)(2,1)S(1)} collective-permute-done((bf16[384,128]{1,0:T(8,128)(2,1)S(1)}, bf16[384,128]{1,0:T(8,128)(2,1)S(1)}, u32[]{:S(2)}, u32[]{:S(2)}) %collective-permute-start.7) | collective-permute-done | bytes 98336 | tf_op jit(solution)/shard_map/ppermute | solution.py:82
  97.0 0.0 collective-permute-done.8.refs_6_.refs_5_
  97.0 0.0 collective-permute-done.9.refs_2_
  97.0 5.1 %shard_map.201 = (bf16[32,80,128]{2,1,0:T(8,128)(2,1)}, bf16[32,80,128]{2,1,0:T(8,128)(2,1)}, bf16[32,80,128]{2,1,0:T(8,128)(2,1)}, bf16[32,80,128]{2,1,0:T(8,128)(2,1)}, f32[8,128]{1,0:T(8,128)S(1)}) custom-call(s32[1]{0:T(128)} %bitcast.refs_0_, bf16[4,256,768]{2,1,0:T(8,128)(2,1)} %get-tuple-element.54.refs_1_, ...), custom_call_target="tpu_custom_call" | custom-call | flops 2000000000 | bytes 10000000 | tf_op jit(solution)/shard_map/pallas_call | solution.py:60
  102.1 1.2 collective-permute-start.10
  103.3 2.7 %collective-permute-start.11 = (bf16[32,80,128]{2,1,0:T(8,128)(2,1)}, bf16[32,80,128]{2,1,0:T(8,128)(2,1)S(1)}, u32[]{:S(2)}, u32[]{:S(2)}) collective-permute-start(bf16[32,80,128]{2,1,0:T(8,128)(2,1)} %get-tuple-element.62), channel_id=1, source_target_pairs={{0,2},{1,3},{2,0},{3,1},{4,6},{5,7},{6,4},{7,5},{8,10},{9,11},{10,... | collective-permute-start | bytes 1966088 | tf_op jit(solution)/shard_map/ppermute | solution.py:82
  106.0 0.0 collective-permute-start.12
  106.0 2.2 %shard_map.202 = bf16[64,48,128]{2,1,0:T(8,128)(2,1)} custom-call(s32[1]{0:T(128)} %bitcast.refs_0_, s32[8,128]{1,0:T(8,128)S(1)} %get-tuple-element.43.refs_1_, bf16[384,128]{1,0:T(8,128)(2,1)S(1)} %get-tuple-element.50.refs_2_, bf16[384,128]{1,0:T(8,128)(2,1)S(1)} %collective-permute-done.6.refs_4_.refs_3_, ...), custom_call_target="tpu_custom_call" | custom-call | flops 1000000000 | bytes 2000000 | tf_op jit(solution)/shard_map/pallas_call | solution.py:60
  108.2 7.1 %all-to-all-start.2 = ((bf16[64,48,128]{2,1,0:T(8,128)(2,1)}), bf16[64,48,128]{2,1,0:T(8,128)(2,1)}, u32[]{:S(2)}, u32[]{:S(2)}) async-start(bf16[64,48,128]{2,1,0:T(8,128)(2,1)} %shard_map.202), calls=%async_computation.2 | async-start | bytes 1572864 | tf_op jit(solution)/shard_map/all_to_all | solution.py:549
  115.4 3.8 %collective-permute-done.10.refs_1_ = bf16[32,80,128]{2,1,0:T(8,128)(2,1)S(1)} collective-permute-done((bf16[32,80,128]{2,1,0:T(8,128)(2,1)}, bf16[32,80,128]{2,1,0:T(8,128)(2,1)S(1)}, u32[]{:S(2)}, u32[]{:S(2)}) %collective-permute-start.10) | collective-permute-done | bytes 655392 | tf_op jit(solution)/shard_map/ppermute | solution.py:82
  119.2 15.5 %collective-permute-done.11.refs_2_ = bf16[32,80,128]{2,1,0:T(8,128)(2,1)S(1)} collective-permute-done((bf16[32,80,128]{2,1,0:T(8,128)(2,1)}, bf16[32,80,128]{2,1,0:T(8,128)(2,1)S(1)}, u32[]{:S(2)}, u32[]{:S(2)}) %collective-permute-start.11) | collective-permute-done | bytes 655392 | tf_op jit(solution)/shard_map/ppermute | solution.py:82
  134.7 0.0 collective-permute-done.12.refs_3_
  134.7 2.2 %shard_map.204.refs_0_ = bf16[32,80,128]{2,1,0:T(8,128)(2,1)} custom-call(bf16[32,80,128]{2,1,0:T(8,128)(2,1)} %get-tuple-element.60.refs_0_, bf16[32,80,128]{2,1,0:T(8,128)(2,1)S(1)} %collective-permute-done.10.refs_1_, bf16[32,80,128]{2,1,0:T(8,128)(2,1)S(1)} %collective-permute-done.11.refs_2_, bf16[32,80,128]{2,1,0:T(8,128)(2,1)S(1)} %collective-permute-done.12.refs_3_), custom_call_target="tpu_custom_call" | custom-call | flops 999999995904 | bytes 10000000 | tf_op jit(solution)/shard_map/pallas_call | solution.py:60
  136.9 1.4 all-to-all-done.2.refs_1_
  138.3 5.1 %all-to-all-start.3 = ((bf16[32,80,128]{2,1,0:T(8,128)(2,1)}), bf16[32,80,128]{2,1,0:T(8,128)(2,1)S(1)}, u32[]{:S(2)}, u32[]{:S(2)}) async-start(bf16[32,80,128]{2,1,0:T(8,128)(2,1)} %shard_map.205), calls=%async_computation.3 | async-start | bytes 1310720 | tf_op jit(solution)/shard_map/all_to_all | solution.py:549
  143.4 5.0 %shard_map.203 = (f32[192,2048]{1,0:T(8,128)}, f32[8,128]{1,0:T(8,128)S(1)}) custom-call(s32[64,32]{1,0:T(8,128)S(1)} %bitcast.10, bf16[64,48,128]{2,1,0:T(8,128)(2,1)} %all-to-all-done.2.refs_1_), custom_call_target="tpu_custom_call" | custom-call | flops 2000000000 | bytes 4000000 | tf_op jit(solution)/shard_map/pallas_call | solution.py:60
  148.4 11.4 %all-to-all-done.3.refs_0_ = bf16[32,80,128]{2,1,0:T(8,128)(2,1)S(1)} async-done(((bf16[32,80,128]{2,1,0:T(8,128)(2,1)}), bf16[32,80,128]{2,1,0:T(8,128)(2,1)S(1)}, u32[]{:S(2)}, u32[]{:S(2)}) %all-to-all-start.3) | async-done | bytes 655392 | tf_op jit(solution)/shard_map/all_to_all | solution.py:549
  159.8 0.8 shard_map.206
  160.6 8.2 %all-to-all-start.4 = ((bf16[8,80,128]{2,1,0:T(8,128)(2,1)}), bf16[8,80,128]{2,1,0:T(8,128)(2,1)S(1)}, u32[]{:S(2)}, u32[]{:S(2)}) async-start(bf16[8,80,128]{2,1,0:T(8,128)(2,1)} %shard_map.206), calls=%async_computation.4 | async-start | bytes 327680 | tf_op jit(solution)/shard_map/all_to_all | solution.py:549
  168.7 0.6 slice_reduce_fusion
  169.4 4.9 %all-to-all-done.4.refs_1_ = bf16[8,80,128]{2,1,0:T(8,128)(2,1)S(1)} async-done(((bf16[8,80,128]{2,1,0:T(8,128)(2,1)}), bf16[8,80,128]{2,1,0:T(8,128)(2,1)S(1)}, u32[]{:S(2)}, u32[]{:S(2)}) %all-to-all-start.4) | async-done | bytes 163872 | tf_op jit(solution)/shard_map/all_to_all | solution.py:549
  174.2 0.7 shard_map.207
  (4 shorter events, 0.0 us)
Async XLA Ops:
  0.6 5.9 %collective-permute-start = (s32[2,128]{1,0:T(2,128)}, s32[2,128]{1,0:T(2,128)S(1)}, u32[]{:S(2)}, u32[]{:S(2)}) collective-permute-start(s32[2,128]{1,0:T(2,128)} %refs_1_.1), channel_id=1, source_target_pairs={{0,1},{1,2},{2,3},{3,0},{4,5},{5,6},{6,7},{7,4},{8,9},{9,10},{10,1... | collective-permute-start | bytes 3080 | tf_op jit(solution)/shard_map/ppermute | solution.py:82
  2.8 3.8 %collective-permute-start.2 = (s32[2,128]{1,0:T(2,128)}, s32[2,128]{1,0:T(2,128)S(1)}, u32[]{:S(2)}, u32[]{:S(2)}) collective-permute-start(s32[2,128]{1,0:T(2,128)} %refs_1_.1), channel_id=1, source_target_pairs={{0,3},{1,0},{2,1},{3,2},{4,7},{5,4},{6,5},{7,6},{8,11},{9,8},{10,9... | collective-permute-start | bytes 3080 | tf_op jit(solution)/shard_map/ppermute | solution.py:82
  4.1 4.1 %collective-permute-start.1 = (s32[2,128]{1,0:T(2,128)}, s32[2,128]{1,0:T(2,128)S(1)}, u32[]{:S(2)}, u32[]{:S(2)}) collective-permute-start(s32[2,128]{1,0:T(2,128)} %refs_1_.1), channel_id=1, source_target_pairs={{0,2},{1,3},{2,0},{3,1},{4,6},{5,7},{6,4},{7,5},{8,10},{9,11},{10,... | collective-permute-start | bytes 3080 | tf_op jit(solution)/shard_map/ppermute | solution.py:82
  11.7 23.4 %all-to-all-start = ((s32[64,1,32]{2,1,0:T(1,128)}), s32[64,1,32]{2,1,0:T(1,128)S(1)}, u32[]{:S(2)}, u32[]{:S(2)}) async-start(s32[64,1,32]{2,1,0:T(1,128)} %bitcast.4), calls=%async_computation | async-start | bytes 65536 | tf_op jit(solution)/shard_map/all_to_all | solution.py:549
  64.5 5.6 %copy-start.2 = (f32[768]{0:T(1024)S(1)}, f32[768]{0:T(1024)}, u32[]{:S(2)}) copy-start(f32[768]{0:T(1024)} %param.21) | copy-start | bytes 9220
  64.5 5.6 %copy-start.3 = (f32[768]{0:T(1024)S(1)}, f32[768]{0:T(1024)}, u32[]{:S(2)}) copy-start(f32[768]{0:T(1024)} %param.22) | copy-start | bytes 9220
  64.5 5.6 %copy-start.4 = (f32[768]{0:T(1024)S(1)}, f32[768]{0:T(1024)}, u32[]{:S(2)}) copy-start(f32[768]{0:T(1024)} %param.23) | copy-start | bytes 9220
  64.5 9.5 %copy-start = (bf16[2,768]{1,0:T(2,128)(2,1)S(1)}, bf16[2,768]{1,0:T(2,128)(2,1)}, u32[]{:S(2)}) copy-start(bf16[2,768]{1,0:T(2,128)(2,1)} %refs_6_.1) | copy-start | bytes 9220
  64.5 9.5 %copy-start.1 = (s32[2,128]{1,0:T(2,128)S(1)}, s32[2,128]{1,0:T(2,128)}, u32[]{:S(2)}) copy-start(s32[2,128]{1,0:T(2,128)} %refs_7_.1) | copy-start | bytes 3076
  66.4 5.5 %collective-permute-start.3 = (bf16[384,128]{1,0:T(8,128)(2,1)S(1)}, bf16[384,128]{1,0:T(8,128)(2,1)S(1)}, u32[]{:S(2)}, u32[]{:S(2)}) collective-permute-start(bf16[384,128]{1,0:T(8,128)(2,1)S(1)} %get-tuple-element.46), channel_id=1, source_target_pairs={{0,1},{1,2},{2,3},{3,0},{4,5},{5,6},{6,7},{7,4},{8,9},{9,10},{10,1... | collective-permute-start | bytes 294920 | tf_op jit(solution)/shard_map/ppermute | solution.py:82
  66.5 7.1 %collective-permute-start.4 = (bf16[384,128]{1,0:T(8,128)(2,1)S(1)}, bf16[384,128]{1,0:T(8,128)(2,1)S(1)}, u32[]{:S(2)}, u32[]{:S(2)}) collective-permute-start(bf16[384,128]{1,0:T(8,128)(2,1)S(1)} %get-tuple-element.47), channel_id=1, source_target_pairs={{0,2},{1,3},{2,0},{3,1},{4,6},{5,7},{6,4},{7,5},{8,10},{9,11},{10,... | collective-permute-start | bytes 294920 | tf_op jit(solution)/shard_map/ppermute | solution.py:82
  68.9 5.1 %collective-permute-start.5 = (bf16[384,128]{1,0:T(8,128)(2,1)S(1)}, bf16[384,128]{1,0:T(8,128)(2,1)S(1)}, u32[]{:S(2)}, u32[]{:S(2)}) collective-permute-start(bf16[384,128]{1,0:T(8,128)(2,1)S(1)} %get-tuple-element.48), channel_id=1, source_target_pairs={{0,3},{1,0},{2,1},{3,2},{4,7},{5,4},{6,5},{7,6},{8,11},{9,8},{10,9... | collective-permute-start | bytes 294920 | tf_op jit(solution)/shard_map/ppermute | solution.py:82
  86.8 10.2 %collective-permute-start.9 = (bf16[4,256,768]{2,1,0:T(8,128)(2,1)}, bf16[4,256,768]{2,1,0:T(8,128)(2,1)S(1)}, u32[]{:S(2)}, u32[]{:S(2)}) collective-permute-start(bf16[4,256,768]{2,1,0:T(8,128)(2,1)} %get-tuple-element.55), channel_id=1, source_target_pairs={{0,4},{4,0},{1,5},{5,1},{2,6},{6,2},{3,7},{7,3},{8,12},{12,8},{9,1... | collective-permute-start | bytes 4718600 | tf_op jit(solution)/shard_map/ppermute | solution.py:632
  88.4 5.6 %collective-permute-start.6 = (bf16[384,128]{1,0:T(8,128)(2,1)S(1)}, bf16[384,128]{1,0:T(8,128)(2,1)S(1)}, u32[]{:S(2)}, u32[]{:S(2)}) collective-permute-start(bf16[384,128]{1,0:T(8,128)(2,1)S(1)} %get-tuple-element.51), channel_id=1, source_target_pairs={{0,1},{1,2},{2,3},{3,0},{4,5},{5,6},{6,7},{7,4},{8,9},{9,10},{10,1... | collective-permute-start | bytes 294920 | tf_op jit(solution)/shard_map/ppermute | solution.py:82
  89.4 7.6 %collective-permute-start.7 = (bf16[384,128]{1,0:T(8,128)(2,1)S(1)}, bf16[384,128]{1,0:T(8,128)(2,1)S(1)}, u32[]{:S(2)}, u32[]{:S(2)}) collective-permute-start(bf16[384,128]{1,0:T(8,128)(2,1)S(1)} %get-tuple-element.52), channel_id=1, source_target_pairs={{0,2},{1,3},{2,0},{3,1},{4,6},{5,7},{6,4},{7,5},{8,10},{9,11},{10,... | collective-permute-start | bytes 294920 | tf_op jit(solution)/shard_map/ppermute | solution.py:82
  92.0 5.0 %collective-permute-start.8 = (bf16[384,128]{1,0:T(8,128)(2,1)S(1)}, bf16[384,128]{1,0:T(8,128)(2,1)S(1)}, u32[]{:S(2)}, u32[]{:S(2)}) collective-permute-start(bf16[384,128]{1,0:T(8,128)(2,1)S(1)} %get-tuple-element.53), channel_id=1, source_target_pairs={{0,3},{1,0},{2,1},{3,2},{4,7},{5,4},{6,5},{7,6},{8,11},{9,8},{10,9... | collective-permute-start | bytes 294920 | tf_op jit(solution)/shard_map/ppermute | solution.py:82
  102.1 17.1 %collective-permute-start.10 = (bf16[32,80,128]{2,1,0:T(8,128)(2,1)}, bf16[32,80,128]{2,1,0:T(8,128)(2,1)S(1)}, u32[]{:S(2)}, u32[]{:S(2)}) collective-permute-start(bf16[32,80,128]{2,1,0:T(8,128)(2,1)} %get-tuple-element.61), channel_id=1, source_target_pairs={{0,1},{1,2},{2,3},{3,0},{4,5},{5,6},{6,7},{7,4},{8,9},{9,10},{10,1... | collective-permute-start | bytes 1966088 | tf_op jit(solution)/shard_map/ppermute | solution.py:82
  103.3 31.4 %collective-permute-start.11 = (bf16[32,80,128]{2,1,0:T(8,128)(2,1)}, bf16[32,80,128]{2,1,0:T(8,128)(2,1)S(1)}, u32[]{:S(2)}, u32[]{:S(2)}) collective-permute-start(bf16[32,80,128]{2,1,0:T(8,128)(2,1)} %get-tuple-element.62), channel_id=1, source_target_pairs={{0,2},{1,3},{2,0},{3,1},{4,6},{5,7},{6,4},{7,5},{8,10},{9,11},{10,... | collective-permute-start | bytes 1966088 | tf_op jit(solution)/shard_map/ppermute | solution.py:82
  106.0 28.7 %collective-permute-start.12 = (bf16[32,80,128]{2,1,0:T(8,128)(2,1)}, bf16[32,80,128]{2,1,0:T(8,128)(2,1)S(1)}, u32[]{:S(2)}, u32[]{:S(2)}) collective-permute-start(bf16[32,80,128]{2,1,0:T(8,128)(2,1)} %get-tuple-element.63), channel_id=1, source_target_pairs={{0,3},{1,0},{2,1},{3,2},{4,7},{5,4},{6,5},{7,6},{8,11},{9,8},{10,9... | collective-permute-start | bytes 1966088 | tf_op jit(solution)/shard_map/ppermute | solution.py:82
  108.2 30.0 %all-to-all-start.2 = ((bf16[64,48,128]{2,1,0:T(8,128)(2,1)}), bf16[64,48,128]{2,1,0:T(8,128)(2,1)}, u32[]{:S(2)}, u32[]{:S(2)}) async-start(bf16[64,48,128]{2,1,0:T(8,128)(2,1)} %shard_map.202), calls=%async_computation.2 | async-start | bytes 1572864 | tf_op jit(solution)/shard_map/all_to_all | solution.py:549
  138.3 21.5 %all-to-all-start.3 = ((bf16[32,80,128]{2,1,0:T(8,128)(2,1)}), bf16[32,80,128]{2,1,0:T(8,128)(2,1)S(1)}, u32[]{:S(2)}, u32[]{:S(2)}) async-start(bf16[32,80,128]{2,1,0:T(8,128)(2,1)} %shard_map.205), calls=%async_computation.3 | async-start | bytes 1310720 | tf_op jit(solution)/shard_map/all_to_all | solution.py:549
  160.6 13.7 %all-to-all-start.4 = ((bf16[8,80,128]{2,1,0:T(8,128)(2,1)}), bf16[8,80,128]{2,1,0:T(8,128)(2,1)S(1)}, u32[]{:S(2)}, u32[]{:S(2)}) async-start(bf16[8,80,128]{2,1,0:T(8,128)(2,1)} %shard_map.206), calls=%async_computation.4 | async-start | bytes 327680 | tf_op jit(solution)/shard_map/all_to_all | solution.py:549

commit v3 on v2

--- a/solution.py
+++ b/solution.py
@@ -229,11 +229,12 @@
     copy.wait()
 
 
-def slots_kernel(me_ref, slot_ref, a_ref, b_ref, c_ref, d_ref, out_ref, held):
+def slots_kernel(me_ref, slot_ref, a_ref, b_ref, c_ref, d_ref, out_hbm, held, out_ref, sem):
     collect(me_ref[0], (a_ref, b_ref, c_ref, d_ref), held)
     grads = unpack(held[...])
     groups = out_ref.shape[0]
     step = 16 * CAP
+    copies = []
     for r in range(0, groups * CAP, step):
         row = iota((step, 128), 0) + r
         chosen = jnp.concatenate(
@@ -246,6 +247,11 @@
         rows = dot(chosen, grads)
         for i in range(16):
             out_ref[r // CAP + i] = pack(rows[CAP * i : CAP * (i + 1)], CAP // 2)
+        at = pl.ds(r // CAP, 16)
+        copies.append(pltpu.make_async_copy(out_ref.at[at], out_hbm.at[at], sem.at[r // step]))
+        copies[-1].start()
+    for c in copies:
+        c.wait()
 
 
 def landing_kernel(asked_ref, arrived_ref, out_hbm, token_ref, out_ref, sem):
@@ -315,11 +321,16 @@
     sem,
 ):
     me = me_ref[0]
-    own = pltpu.make_async_copy(a_hbm, held.at[me], sem.at[4])
+    own = pltpu.make_async_copy(a_hbm, held.at[me], sem.at[8])
     own.start()
     sources = (wq_hbm, wk_hbm, wv_hbm, wo_hbm)
     weights = (wq_ref, wk_ref, wv_ref, wo_ref)
-    copies = [pltpu.make_async_copy(a, b, sem.at[i]) for i, (a, b) in enumerate(zip(sources, weights))]
+    half = wq_ref.shape[0] // 2
+    copies = [
+        pltpu.make_async_copy(a.at[pl.ds(half * h, half)], b.at[pl.ds(half * h, half)], sem.at[2 * i + h])
+        for i, (a, b) in enumerate(zip(sources, weights))
+        for h in (0, 1)
+    ]
     for c in copies:
         c.start()
     for k, ref in ((1, b_ref), (2, c_ref), (3, d_ref)):
@@ -345,11 +356,14 @@
     normed_one = base * inv_one
     gain_attn = gain_attn_ref[...]
     first_input = (normed_one * gain_attn).astype(BF)
-    copies[0].wait()
+    for c in copies[0 : 2]:
+        c.wait()
     q_all = dot(first_input, wq_ref[...]).astype(BF)
-    copies[1].wait()
+    for c in copies[2 : 4]:
+        c.wait()
     k_all = dot(first_input, wk_ref[...]).astype(BF)
-    copies[2].wait()
+    for c in copies[4 : 6]:
+        c.wait()
     v_all = dot(first_input, wv_ref[...]).astype(BF)
 
     def cut(x, q, p):
@@ -377,7 +391,8 @@
         context.append(jnp.concatenate(line, axis=1))
     context = jnp.concatenate(context, axis=0).astype(BF)
 
-    copies[3].wait()
+    for c in copies[6 : 8]:
+        c.wait()
     mixed = base + dot(context, wo_ref[...])
     inv_two = 1.0 / jnp.sqrt(lane_mean(mixed * mixed) + EPSILON)
     normed_two = mixed * inv_two
@@ -433,8 +448,9 @@
         keep_ref[i] = jnp.where(first_core, first_pair[i], second_pair[i])
         send_ref[i] = jnp.where(first_core, second_pair[i], first_pair[i])
     sent = [
-        pltpu.make_async_copy(send_ref, send_hbm, sem.at[5]),
-        pltpu.make_async_copy(keep_ref, keep_hbm, sem.at[6]),
+        pltpu.make_async_copy(a.at[i], b.at[i], sem.at[9 + 4 * j + i])
+        for j, (a, b) in enumerate(((send_ref, send_hbm), (keep_ref, keep_hbm)))
+        for i in range(4)
     ]
     for c in sent:
         c.start()
@@ -485,11 +501,15 @@
             held[m, at] = jnp.concatenate(tiles, axis=0).astype(BF)
         return carry
 
-    lax.fori_loop(0, held.shape[1], assemble, 0)
     copies = []
-    for k, ref in enumerate(out_refs):
-        copies.append(pltpu.make_async_copy(held.at[(me_ref[0] + k) & 3], ref, sem.at[4 + k]))
-        copies[-1].start()
+    n = held.shape[1] // 2
+    for part in (0, 1):
+        lax.fori_loop(n * part, n * (part + 1), assemble, 0)
+        at = pl.ds(n * part, n)
+        for k, ref in enumerate(out_refs):
+            source = held.at[(me_ref[0] + k) & 3, at]
+            copies.append(pltpu.make_async_copy(source, ref.at[at], sem.at[4 + 4 * part + k]))
+            copies[-1].start()
     for c in copies:
         c.wait()
 
@@ -502,15 +522,18 @@
 
 
 def sum_kernel(own_hbm, b_ref, c_ref, d_ref, out_hbm, own_ref, out_ref, sem):
-    copy = pltpu.make_async_copy(own_hbm, own_ref, sem.at[0])
-    copy.start()
-    copy.wait()
-    n = own_ref.shape[0] // 2
+    n = own_ref.shape[0] // 4
+    loads = [
+        pltpu.make_async_copy(own_hbm.at[pl.ds(n * i, n)], own_ref.at[pl.ds(n * i, n)], sem.at[i]) for i in range(4)
+    ]
+    for c in loads:
+        c.start()
     copies = []
-    for i in (0, 1):
+    for i in range(4):
         at = pl.ds(n * i, n)
+        loads[i].wait()
         out_ref[n * i : n * (i + 1)] = plus(*[r[n * i : n * (i + 1)] for r in (own_ref, b_ref, c_ref, d_ref)])
-        copies.append(pltpu.make_async_copy(out_ref.at[at], out_hbm.at[at], sem.at[1 + i]))
+        copies.append(pltpu.make_async_copy(out_ref.at[at], out_hbm.at[at], sem.at[4 + i]))
         copies[-1].start()
     for c in copies:
         c.wait()
@@ -621,7 +644,7 @@
         ]
         + [pltpu.VMEM((width, width), BF)] * 4
         + [pltpu.VMEM((4, queries * size, width), BF)] * 2
-        + [pltpu.SemaphoreType.DMA((7,))],
+        + [pltpu.SemaphoreType.DMA((17,))],
         2, (2, 8, 9, 10, 11),
     )
     losses, query_grad, diff_base = outs[0], outs[1], outs[2:6]
@@ -637,15 +660,15 @@
             pltpu.VMEM((2, width, width), F32),
             pltpu.VMEM((n_mp, n_yz, 80, 128), BF),
             pltpu.VMEM((4, queries * size, width), BF),
-            pltpu.SemaphoreType.DMA((8,)),
+            pltpu.SemaphoreType.DMA((12,)),
         ],
         1, (1,), column_grads[1:],
     )
     arrive = exchange(blocks, "x")
 
     outgoing = call(
-        slots_kernel, shape((n_dp, 48, 128)), (along_x, slot, *column_grads), 16, 10**9, 2 * 10**6,
-        [pltpu.VMEM((n_mp, 384, 128), BF)], 1, awaited=(made,),
+        slots_kernel, pltpu.HBM((n_dp, 48, 128), BF), (along_x, slot, *column_grads), 16, 10**9, 2 * 10**6,
+        [pltpu.VMEM((n_mp, 384, 128), BF), pltpu.VMEM((n_dp, 48, 128), BF), pltpu.SemaphoreType.DMA((4,))], 1, awaited=(made,),
     )
     arrived = swap(outgoing, ROWS)
     landed, token = call(
@@ -658,7 +681,7 @@
 
     over_x = call(
         sum_kernel, pltpu.HBM(block.shape, BF), tuple(arrive), 8, 10**12, 10**7,
-        [pltpu.VMEM(block.shape, BF), pltpu.VMEM(block.shape, BF), pltpu.SemaphoreType.DMA((3,))], 0, (0,),
+        [pltpu.VMEM(block.shape, BF), pltpu.VMEM(block.shape, BF), pltpu.SemaphoreType.DMA((8,))], 0, (0,),
     )
     parts = swap(after(over_x, arrived), ("y", "z"))
     copies = call(last_kernel, shape((2 * n_mp, 80, 128)), (parts,), 4, 10**6, 10**6, awaited=(token,))

time: 176 us -> 175 us (level)
  no operation moved by 1% of the time
where the time goes in v3:
time: 175 us
  waiting for transfers between devices  55.7 us (32%)
  starting transfers between devices  52.5 us (30%)
  Pallas kernels  38 us (22%)
  blocking collectives  27 us (15%)
    pallas_call x12, Pallas kernels, call(): pl.pallas_call(run, out_shape=out_shape, in_specs=in_specs, out_specs=spe...  38 us
    all_to_all x4, starting transfers between devices, swap(): return lax.all_to_all(x, axes, split_axis=0, concat_axis=0, tiled=True)  34.6 us
    ppermute x12, waiting for transfers between devices, shift(): return lax.ppermute(x, axis, [(i, (i + by) % 4) for i in range(4)])  30 us
    all_to_all x1, blocking collectives, swap(): return lax.all_to_all(x, axes, split_axis=0, concat_axis=0, tiled=True)  27 us
    all_to_all x4, waiting for transfers between devices, swap(): return lax.all_to_all(x, axes, split_axis=0, concat_axis=0, tiled=True)  25.7 us
    ppermute x12, starting transfers between devices, shift(): return lax.ppermute(x, axis, [(i, (i + by) % 4) for i in range(4)])  16.3 us
  transfers between devices with their start and end apart: 17, of which 12 were waited for; matrix products, arithmetic and copies ran while one was open for 0% of the time, Pallas kernels for 6%

profile of v3, /device:TPU:1, one launch (start us, length us, event | category | flops | bytes accessed | tf_op | source)
XLA Modules:
  0.0 174.8 jit_solution(7204668832700913523)
XLA Ops:
  0.6 2.1 %collective-permute-start = (s32[2,128]{1,0:T(2,128)}, s32[2,128]{1,0:T(2,128)S(1)}, u32[]{:S(2)}, u32[]{:S(2)}) collective-permute-start(s32[2,128]{1,0:T(2,128)} %refs_1_.1), channel_id=1, source_target_pairs={{0,1},{1,2},{2,3},{3,0},{4,5},{5,6},{6,7},{7,4},{8,9},{9,10},{10,1... | collective-permute-start | bytes 3080 | tf_op jit(solution)/shard_map/ppermute | solution.py:82
  2.8 1.4 collective-permute-start.2
  4.1 1.6 collective-permute-start.1
  5.8 0.8 shard_map.195
  6.5 0.0 collective-permute-done.refs_2_
  6.5 0.0 collective-permute-done.2.refs_4_
  6.5 1.7 collective-permute-done.1.refs_3_
  8.3 3.4 %shard_map.196 = (s32[64,32]{1,0:T(8,128)}, s32[8,128]{1,0:T(8,128)S(1)}) custom-call(s32[1]{0:T(128)} %bitcast.refs_0_, s32[2,128]{1,0:T(2,128)S(1)} %get-tuple-element.41.refs_1_, s32[2,128]{1,0:T(2,128)S(1)} %collective-permute-done.refs_2_, s32[2,128]{1,0:T(2,128)S(1)} %collective-permute-done.1.refs_3_, s32[2,128]{1,0:T(2,128)S(1)} %collective-permute-done.2.refs_4_, ...), custom_call_target="tpu_custom_call" | custom-call | flops 300000000 | bytes 1000000 | tf_op jit(solution)/shard_map/pallas_call | solution.py:60
  11.7 14.1 %all-to-all-start = ((s32[64,1,32]{2,1,0:T(1,128)}), s32[64,1,32]{2,1,0:T(1,128)S(1)}, u32[]{:S(2)}, u32[]{:S(2)}) async-start(s32[64,1,32]{2,1,0:T(1,128)} %bitcast.4), calls=%async_computation | async-start | bytes 65536 | tf_op jit(solution)/shard_map/all_to_all | solution.py:572
  25.8 1.2 shard_map.197.refs_1_
  27.1 8.0 %all-to-all-done = s32[64,1,32]{2,1,0:T(1,128)S(1)} async-done(((s32[64,1,32]{2,1,0:T(1,128)}), s32[64,1,32]{2,1,0:T(1,128)S(1)}, u32[]{:S(2)}, u32[]{:S(2)}) %all-to-all-start) | async-done | bytes 8224 | tf_op jit(solution)/shard_map/all_to_all | solution.py:572
  35.1 2.4 %shard_map.198 = bf16[64,48,128]{2,1,0:T(8,128)(2,1)S(1)} custom-call(s32[64,32]{1,0:T(8,128)S(1)} %bitcast.9, bf16[256,2048]{1,0:T(8,128)(2,1)S(1)} %shard_map.197.refs_1_), custom_call_target="tpu_custom_call" | custom-call | flops 2000000000 | bytes 2000000 | tf_op jit(solution)/shard_map/pallas_call | solution.py:60
  37.5 27.0 %all_to_all.31.refs_2_ = bf16[64,48,128]{2,1,0:T(8,128)(2,1)S(1)} all-to-all(bf16[64,48,128]{2,1,0:T(8,128)(2,1)S(1)} %shard_map.198), channel_id=1, replica_groups=mesh['y'=4,'z'=8,'c'=2,'x'=4] {'y','z','c'}, dimensions={0} | all-to-all | bytes 1572864 | tf_op jit(solution)/shard_map/all_to_all | solution.py:572
  64.5 0.0 copy-start.2
  64.5 0.0 copy-start.3
  64.5 0.0 copy-start.4
  64.5 0.0 copy-start
  64.5 0.0 copy-start.1
  64.6 1.8 %shard_map.199 = (bf16[384,128]{1,0:T(8,128)(2,1)}, bf16[384,128]{1,0:T(8,128)(2,1)S(1)}, bf16[384,128]{1,0:T(8,128)(2,1)S(1)}, bf16[384,128]{1,0:T(8,128)(2,1)S(1)}) custom-call(s32[1]{0:T(128)} %bitcast.refs_0_, s32[8,128]{1,0:T(8,128)S(1)} %get-tuple-element.43.refs_1_, bf16[64,48,128]{2,1,0:T(8,128)(2,1)S(1)} %all_to_all.31.refs_2_), custom_call_target="tpu_custom_call" | custom-call | flops 1000000000 | bytes 2000000 | tf_op jit(solution)/shard_map/pallas_call | solution.py:60
  66.4 0.1 collective-permute-start.3
  66.5 2.4 %collective-permute-start.4 = (bf16[384,128]{1,0:T(8,128)(2,1)S(1)}, bf16[384,128]{1,0:T(8,128)(2,1)S(1)}, u32[]{:S(2)}, u32[]{:S(2)}) collective-permute-start(bf16[384,128]{1,0:T(8,128)(2,1)S(1)} %get-tuple-element.47), channel_id=1, source_target_pairs={{0,2},{1,3},{2,0},{3,1},{4,6},{5,7},{6,4},{7,5},{8,10},{9,11},{10,... | collective-permute-start | bytes 294920 | tf_op jit(solution)/shard_map/ppermute | solution.py:82
  68.9 1.2 collective-permute-start.5
  70.1 0.0 copy-done.2
  70.1 0.0 copy-done.3
  70.1 0.0 copy-done.4
  70.1 1.7 collective-permute-done.3.refs_3_
  71.9 1.7 collective-permute-done.4.refs_4_
  73.6 0.5 collective-permute-done.5.refs_5_
  74.0 0.0 copy-done
  74.0 0.0 copy-done.1
  74.0 12.8 %shard_map.200 = (f32[2,128]{1,0:T(2,128)S(1)}, f32[2,768]{1,0:T(2,128)}, bf16[384,128]{1,0:T(8,128)(2,1)S(1)}, bf16[384,128]{1,0:T(8,128)(2,1)S(1)}, bf16[384,1...) custom-call(s32[1]{0:T(128)} %bitcast.refs_0_, ...), custom_call_target="tpu_custom_call" | custom-call | flops 4000000000 | bytes 10000000 | tf_op jit(solution)/shard_map/pallas_call | solution.py:60
  86.8 1.6 collective-permute-start.9
  88.5 0.9 collective-permute-start.6
  89.4 2.7 %collective-permute-start.7 = (bf16[384,128]{1,0:T(8,128)(2,1)S(1)}, bf16[384,128]{1,0:T(8,128)(2,1)S(1)}, u32[]{:S(2)}, u32[]{:S(2)}) collective-permute-start(bf16[384,128]{1,0:T(8,128)(2,1)S(1)} %get-tuple-element.52), channel_id=1, source_target_pairs={{0,2},{1,3},{2,0},{3,1},{4,6},{5,7},{6,4},{7,5},{8,10},{9,11},{10,... | collective-permute-start | bytes 294920 | tf_op jit(solution)/shard_map/ppermute | solution.py:82
  92.1 0.0 collective-permute-start.8
  92.1 1.9 %collective-permute-done.6.refs_4_.refs_3_ = bf16[384,128]{1,0:T(8,128)(2,1)S(1)} collective-permute-done((bf16[384,128]{1,0:T(8,128)(2,1)S(1)}, bf16[384,128]{1,0:T(8,128)(2,1)S(1)}, u32[]{:S(2)}, u32[]{:S(2)}) %collective-permute-start.6) | collective-permute-done | bytes 98336 | tf_op jit(solution)/shard_map/ppermute | solution.py:82
  94.1 3.0 %collective-permute-done.7.refs_5_.refs_4_ = bf16[384,128]{1,0:T(8,128)(2,1)S(1)} collective-permute-done((bf16[384,128]{1,0:T(8,128)(2,1)S(1)}, bf16[384,128]{1,0:T(8,128)(2,1)S(1)}, u32[]{:S(2)}, u32[]{:S(2)}) %collective-permute-start.7) | collective-permute-done | bytes 98336 | tf_op jit(solution)/shard_map/ppermute | solution.py:82
  97.1 0.0 collective-permute-done.8.refs_6_.refs_5_
  97.1 0.0 collective-permute-done.9.refs_2_
  97.1 4.9 %shard_map.201 = (bf16[32,80,128]{2,1,0:T(8,128)(2,1)}, bf16[32,80,128]{2,1,0:T(8,128)(2,1)}, bf16[32,80,128]{2,1,0:T(8,128)(2,1)}, bf16[32,80,128]{2,1,0:T(8,128)(2,1)}, f32[8,128]{1,0:T(8,128)S(1)}) custom-call(s32[1]{0:T(128)} %bitcast.refs_0_, bf16[4,256,768]{2,1,0:T(8,128)(2,1)} %get-tuple-element.54.refs_1_, ...), custom_call_target="tpu_custom_call" | custom-call | flops 2000000000 | bytes 10000000 | tf_op jit(solution)/shard_map/pallas_call | solution.py:60
  102.0 1.2 collective-permute-start.10
  103.2 2.7 %collective-permute-start.11 = (bf16[32,80,128]{2,1,0:T(8,128)(2,1)}, bf16[32,80,128]{2,1,0:T(8,128)(2,1)S(1)}, u32[]{:S(2)}, u32[]{:S(2)}) collective-permute-start(bf16[32,80,128]{2,1,0:T(8,128)(2,1)} %get-tuple-element.62), channel_id=1, source_target_pairs={{0,2},{1,3},{2,0},{3,1},{4,6},{5,7},{6,4},{7,5},{8,10},{9,11},{10,... | collective-permute-start | bytes 1966088 | tf_op jit(solution)/shard_map/ppermute | solution.py:82
  105.9 0.0 collective-permute-start.12
  105.9 2.2 %shard_map.202 = bf16[64,48,128]{2,1,0:T(8,128)(2,1)} custom-call(s32[1]{0:T(128)} %bitcast.refs_0_, s32[8,128]{1,0:T(8,128)S(1)} %get-tuple-element.43.refs_1_, bf16[384,128]{1,0:T(8,128)(2,1)S(1)} %get-tuple-element.50.refs_2_, bf16[384,128]{1,0:T(8,128)(2,1)S(1)} %collective-permute-done.6.refs_4_.refs_3_, ...), custom_call_target="tpu_custom_call" | custom-call | flops 1000000000 | bytes 2000000 | tf_op jit(solution)/shard_map/pallas_call | solution.py:60
  108.1 7.1 %all-to-all-start.2 = ((bf16[64,48,128]{2,1,0:T(8,128)(2,1)}), bf16[64,48,128]{2,1,0:T(8,128)(2,1)}, u32[]{:S(2)}, u32[]{:S(2)}) async-start(bf16[64,48,128]{2,1,0:T(8,128)(2,1)} %shard_map.202), calls=%async_computation.2 | async-start | bytes 1572864 | tf_op jit(solution)/shard_map/all_to_all | solution.py:572
  115.2 3.9 %collective-permute-done.10.refs_1_ = bf16[32,80,128]{2,1,0:T(8,128)(2,1)S(1)} collective-permute-done((bf16[32,80,128]{2,1,0:T(8,128)(2,1)}, bf16[32,80,128]{2,1,0:T(8,128)(2,1)S(1)}, u32[]{:S(2)}, u32[]{:S(2)}) %collective-permute-start.10) | collective-permute-done | bytes 655392 | tf_op jit(solution)/shard_map/ppermute | solution.py:82
  119.1 15.5 %collective-permute-done.11.refs_2_ = bf16[32,80,128]{2,1,0:T(8,128)(2,1)S(1)} collective-permute-done((bf16[32,80,128]{2,1,0:T(8,128)(2,1)}, bf16[32,80,128]{2,1,0:T(8,128)(2,1)S(1)}, u32[]{:S(2)}, u32[]{:S(2)}) %collective-permute-start.11) | collective-permute-done | bytes 655392 | tf_op jit(solution)/shard_map/ppermute | solution.py:82
  134.6 0.0 collective-permute-done.12.refs_3_
  134.6 2.0 %shard_map.204.refs_0_ = bf16[32,80,128]{2,1,0:T(8,128)(2,1)} custom-call(bf16[32,80,128]{2,1,0:T(8,128)(2,1)} %get-tuple-element.60.refs_0_, bf16[32,80,128]{2,1,0:T(8,128)(2,1)S(1)} %collective-permute-done.10.refs_1_, bf16[32,80,128]{2,1,0:T(8,128)(2,1)S(1)} %collective-permute-done.11.refs_2_, bf16[32,80,128]{2,1,0:T(8,128)(2,1)S(1)} %collective-permute-done.12.refs_3_), custom_call_target="tpu_custom_call" | custom-call | flops 999999995904 | bytes 10000000 | tf_op jit(solution)/shard_map/pallas_call | solution.py:60
  136.7 1.5 all-to-all-done.2.refs_1_
  138.1 5.1 %all-to-all-start.3 = ((bf16[32,80,128]{2,1,0:T(8,128)(2,1)}), bf16[32,80,128]{2,1,0:T(8,128)(2,1)S(1)}, u32[]{:S(2)}, u32[]{:S(2)}) async-start(bf16[32,80,128]{2,1,0:T(8,128)(2,1)} %shard_map.205), calls=%async_computation.3 | async-start | bytes 1310720 | tf_op jit(solution)/shard_map/all_to_all | solution.py:572
  143.3 5.0 %shard_map.203 = (f32[192,2048]{1,0:T(8,128)}, f32[8,128]{1,0:T(8,128)S(1)}) custom-call(s32[64,32]{1,0:T(8,128)S(1)} %bitcast.10, bf16[64,48,128]{2,1,0:T(8,128)(2,1)} %all-to-all-done.2.refs_1_), custom_call_target="tpu_custom_call" | custom-call | flops 2000000000 | bytes 4000000 | tf_op jit(solution)/shard_map/pallas_call | solution.py:60
  148.3 11.4 %all-to-all-done.3.refs_0_ = bf16[32,80,128]{2,1,0:T(8,128)(2,1)S(1)} async-done(((bf16[32,80,128]{2,1,0:T(8,128)(2,1)}), bf16[32,80,128]{2,1,0:T(8,128)(2,1)S(1)}, u32[]{:S(2)}, u32[]{:S(2)}) %all-to-all-start.3) | async-done | bytes 655392 | tf_op jit(solution)/shard_map/all_to_all | solution.py:572
  159.6 0.8 shard_map.206
  160.4 8.2 %all-to-all-start.4 = ((bf16[8,80,128]{2,1,0:T(8,128)(2,1)}), bf16[8,80,128]{2,1,0:T(8,128)(2,1)S(1)}, u32[]{:S(2)}, u32[]{:S(2)}) async-start(bf16[8,80,128]{2,1,0:T(8,128)(2,1)} %shard_map.206), calls=%async_computation.4 | async-start | bytes 327680 | tf_op jit(solution)/shard_map/all_to_all | solution.py:572
  168.6 0.6 slice_reduce_fusion
  169.2 4.9 %all-to-all-done.4.refs_1_ = bf16[8,80,128]{2,1,0:T(8,128)(2,1)S(1)} async-done(((bf16[8,80,128]{2,1,0:T(8,128)(2,1)}), bf16[8,80,128]{2,1,0:T(8,128)(2,1)S(1)}, u32[]{:S(2)}, u32[]{:S(2)}) %all-to-all-start.4) | async-done | bytes 163872 | tf_op jit(solution)/shard_map/all_to_all | solution.py:572
  174.1 0.7 shard_map.207
  (4 shorter events, 0.0 us)
Async XLA Ops:
  0.6 5.9 %collective-permute-start = (s32[2,128]{1,0:T(2,128)}, s32[2,128]{1,0:T(2,128)S(1)}, u32[]{:S(2)}, u32[]{:S(2)}) collective-permute-start(s32[2,128]{1,0:T(2,128)} %refs_1_.1), channel_id=1, source_target_pairs={{0,1},{1,2},{2,3},{3,0},{4,5},{5,6},{6,7},{7,4},{8,9},{9,10},{10,1... | collective-permute-start | bytes 3080 | tf_op jit(solution)/shard_map/ppermute | solution.py:82
  2.8 3.8 %collective-permute-start.2 = (s32[2,128]{1,0:T(2,128)}, s32[2,128]{1,0:T(2,128)S(1)}, u32[]{:S(2)}, u32[]{:S(2)}) collective-permute-start(s32[2,128]{1,0:T(2,128)} %refs_1_.1), channel_id=1, source_target_pairs={{0,3},{1,0},{2,1},{3,2},{4,7},{5,4},{6,5},{7,6},{8,11},{9,8},{10,9... | collective-permute-start | bytes 3080 | tf_op jit(solution)/shard_map/ppermute | solution.py:82
  4.1 4.1 %collective-permute-start.1 = (s32[2,128]{1,0:T(2,128)}, s32[2,128]{1,0:T(2,128)S(1)}, u32[]{:S(2)}, u32[]{:S(2)}) collective-permute-start(s32[2,128]{1,0:T(2,128)} %refs_1_.1), channel_id=1, source_target_pairs={{0,2},{1,3},{2,0},{3,1},{4,6},{5,7},{6,4},{7,5},{8,10},{9,11},{10,... | collective-permute-start | bytes 3080 | tf_op jit(solution)/shard_map/ppermute | solution.py:82
  11.7 23.4 %all-to-all-start = ((s32[64,1,32]{2,1,0:T(1,128)}), s32[64,1,32]{2,1,0:T(1,128)S(1)}, u32[]{:S(2)}, u32[]{:S(2)}) async-start(s32[64,1,32]{2,1,0:T(1,128)} %bitcast.4), calls=%async_computation | async-start | bytes 65536 | tf_op jit(solution)/shard_map/all_to_all | solution.py:572
  64.5 5.6 %copy-start.2 = (f32[768]{0:T(1024)S(1)}, f32[768]{0:T(1024)}, u32[]{:S(2)}) copy-start(f32[768]{0:T(1024)} %param.21) | copy-start | bytes 9220
  64.5 5.6 %copy-start.3 = (f32[768]{0:T(1024)S(1)}, f32[768]{0:T(1024)}, u32[]{:S(2)}) copy-start(f32[768]{0:T(1024)} %param.22) | copy-start | bytes 9220
  64.5 5.6 %copy-start.4 = (f32[768]{0:T(1024)S(1)}, f32[768]{0:T(1024)}, u32[]{:S(2)}) copy-start(f32[768]{0:T(1024)} %param.23) | copy-start | bytes 9220
  64.5 9.5 %copy-start = (bf16[2,768]{1,0:T(2,128)(2,1)S(1)}, bf16[2,768]{1,0:T(2,128)(2,1)}, u32[]{:S(2)}) copy-start(bf16[2,768]{1,0:T(2,128)(2,1)} %refs_6_.1) | copy-start | bytes 9220
  64.5 9.5 %copy-start.1 = (s32[2,128]{1,0:T(2,128)S(1)}, s32[2,128]{1,0:T(2,128)}, u32[]{:S(2)}) copy-start(s32[2,128]{1,0:T(2,128)} %refs_7_.1) | copy-start | bytes 3076
  66.4 5.5 %collective-permute-start.3 = (bf16[384,128]{1,0:T(8,128)(2,1)S(1)}, bf16[384,128]{1,0:T(8,128)(2,1)S(1)}, u32[]{:S(2)}, u32[]{:S(2)}) collective-permute-start(bf16[384,128]{1,0:T(8,128)(2,1)S(1)} %get-tuple-element.46), channel_id=1, source_target_pairs={{0,1},{1,2},{2,3},{3,0},{4,5},{5,6},{6,7},{7,4},{8,9},{9,10},{10,1... | collective-permute-start | bytes 294920 | tf_op jit(solution)/shard_map/ppermute | solution.py:82
  66.5 7.1 %collective-permute-start.4 = (bf16[384,128]{1,0:T(8,128)(2,1)S(1)}, bf16[384,128]{1,0:T(8,128)(2,1)S(1)}, u32[]{:S(2)}, u32[]{:S(2)}) collective-permute-start(bf16[384,128]{1,0:T(8,128)(2,1)S(1)} %get-tuple-element.47), channel_id=1, source_target_pairs={{0,2},{1,3},{2,0},{3,1},{4,6},{5,7},{6,4},{7,5},{8,10},{9,11},{10,... | collective-permute-start | bytes 294920 | tf_op jit(solution)/shard_map/ppermute | solution.py:82
  68.9 5.1 %collective-permute-start.5 = (bf16[384,128]{1,0:T(8,128)(2,1)S(1)}, bf16[384,128]{1,0:T(8,128)(2,1)S(1)}, u32[]{:S(2)}, u32[]{:S(2)}) collective-permute-start(bf16[384,128]{1,0:T(8,128)(2,1)S(1)} %get-tuple-element.48), channel_id=1, source_target_pairs={{0,3},{1,0},{2,1},{3,2},{4,7},{5,4},{6,5},{7,6},{8,11},{9,8},{10,9... | collective-permute-start | bytes 294920 | tf_op jit(solution)/shard_map/ppermute | solution.py:82
  86.8 10.2 %collective-permute-start.9 = (bf16[4,256,768]{2,1,0:T(8,128)(2,1)}, bf16[4,256,768]{2,1,0:T(8,128)(2,1)S(1)}, u32[]{:S(2)}, u32[]{:S(2)}) collective-permute-start(bf16[4,256,768]{2,1,0:T(8,128)(2,1)} %get-tuple-element.55), channel_id=1, source_target_pairs={{0,4},{4,0},{1,5},{5,1},{2,6},{6,2},{3,7},{7,3},{8,12},{12,8},{9,1... | collective-permute-start | bytes 4718600 | tf_op jit(solution)/shard_map/ppermute | solution.py:655
  88.5 5.6 %collective-permute-start.6 = (bf16[384,128]{1,0:T(8,128)(2,1)S(1)}, bf16[384,128]{1,0:T(8,128)(2,1)S(1)}, u32[]{:S(2)}, u32[]{:S(2)}) collective-permute-start(bf16[384,128]{1,0:T(8,128)(2,1)S(1)} %get-tuple-element.51), channel_id=1, source_target_pairs={{0,1},{1,2},{2,3},{3,0},{4,5},{5,6},{6,7},{7,4},{8,9},{9,10},{10,1... | collective-permute-start | bytes 294920 | tf_op jit(solution)/shard_map/ppermute | solution.py:82
  89.4 7.6 %collective-permute-start.7 = (bf16[384,128]{1,0:T(8,128)(2,1)S(1)}, bf16[384,128]{1,0:T(8,128)(2,1)S(1)}, u32[]{:S(2)}, u32[]{:S(2)}) collective-permute-start(bf16[384,128]{1,0:T(8,128)(2,1)S(1)} %get-tuple-element.52), channel_id=1, source_target_pairs={{0,2},{1,3},{2,0},{3,1},{4,6},{5,7},{6,4},{7,5},{8,10},{9,11},{10,... | collective-permute-start | bytes 294920 | tf_op jit(solution)/shard_map/ppermute | solution.py:82
  92.1 5.0 %collective-permute-start.8 = (bf16[384,128]{1,0:T(8,128)(2,1)S(1)}, bf16[384,128]{1,0:T(8,128)(2,1)S(1)}, u32[]{:S(2)}, u32[]{:S(2)}) collective-permute-start(bf16[384,128]{1,0:T(8,128)(2,1)S(1)} %get-tuple-element.53), channel_id=1, source_target_pairs={{0,3},{1,0},{2,1},{3,2},{4,7},{5,4},{6,5},{7,6},{8,11},{9,8},{10,9... | collective-permute-start | bytes 294920 | tf_op jit(solution)/shard_map/ppermute | solution.py:82
  102.0 17.1 %collective-permute-start.10 = (bf16[32,80,128]{2,1,0:T(8,128)(2,1)}, bf16[32,80,128]{2,1,0:T(8,128)(2,1)S(1)}, u32[]{:S(2)}, u32[]{:S(2)}) collective-permute-start(bf16[32,80,128]{2,1,0:T(8,128)(2,1)} %get-tuple-element.61), channel_id=1, source_target_pairs={{0,1},{1,2},{2,3},{3,0},{4,5},{5,6},{6,7},{7,4},{8,9},{9,10},{10,1... | collective-permute-start | bytes 1966088 | tf_op jit(solution)/shard_map/ppermute | solution.py:82
  103.2 31.4 %collective-permute-start.11 = (bf16[32,80,128]{2,1,0:T(8,128)(2,1)}, bf16[32,80,128]{2,1,0:T(8,128)(2,1)S(1)}, u32[]{:S(2)}, u32[]{:S(2)}) collective-permute-start(bf16[32,80,128]{2,1,0:T(8,128)(2,1)} %get-tuple-element.62), channel_id=1, source_target_pairs={{0,2},{1,3},{2,0},{3,1},{4,6},{5,7},{6,4},{7,5},{8,10},{9,11},{10,... | collective-permute-start | bytes 1966088 | tf_op jit(solution)/shard_map/ppermute | solution.py:82
  105.9 28.7 %collective-permute-start.12 = (bf16[32,80,128]{2,1,0:T(8,128)(2,1)}, bf16[32,80,128]{2,1,0:T(8,128)(2,1)S(1)}, u32[]{:S(2)}, u32[]{:S(2)}) collective-permute-start(bf16[32,80,128]{2,1,0:T(8,128)(2,1)} %get-tuple-element.63), channel_id=1, source_target_pairs={{0,3},{1,0},{2,1},{3,2},{4,7},{5,4},{6,5},{7,6},{8,11},{9,8},{10,9... | collective-permute-start | bytes 1966088 | tf_op jit(solution)/shard_map/ppermute | solution.py:82
  108.1 30.1 %all-to-all-start.2 = ((bf16[64,48,128]{2,1,0:T(8,128)(2,1)}), bf16[64,48,128]{2,1,0:T(8,128)(2,1)}, u32[]{:S(2)}, u32[]{:S(2)}) async-start(bf16[64,48,128]{2,1,0:T(8,128)(2,1)} %shard_map.202), calls=%async_computation.2 | async-start | bytes 1572864 | tf_op jit(solution)/shard_map/all_to_all | solution.py:572
  138.1 21.5 %all-to-all-start.3 = ((bf16[32,80,128]{2,1,0:T(8,128)(2,1)}), bf16[32,80,128]{2,1,0:T(8,128)(2,1)S(1)}, u32[]{:S(2)}, u32[]{:S(2)}) async-start(bf16[32,80,128]{2,1,0:T(8,128)(2,1)} %shard_map.205), calls=%async_computation.3 | async-start | bytes 1310720 | tf_op jit(solution)/shard_map/all_to_all | solution.py:572
  160.4 13.7 %all-to-all-start.4 = ((bf16[8,80,128]{2,1,0:T(8,128)(2,1)}), bf16[8,80,128]{2,1,0:T(8,128)(2,1)S(1)}, u32[]{:S(2)}, u32[]{:S(2)}) async-start(bf16[8,80,128]{2,1,0:T(8,128)(2,1)} %shard_map.206), calls=%async_computation.4 | async-start | bytes 327680 | tf_op jit(solution)/shard_map/all_to_all | solution.py:572

commit v4 on v3

--- a/solution.py
+++ b/solution.py
@@ -193,22 +193,27 @@
         c.wait()
 
 
-def owner_kernel(asked_ref, table_ref, out_ref):
-    asked = four_groups(asked_ref[...])
-    part = asked.shape[0]
+def owner_kernel(asked_ref, table_ref, out_ref, held):
+    held[...] = four_groups(asked_ref[...])
+    part = held.shape[0]
     stored = table_ref.shape[1]
     step = 4
-    for r in range(0, part, step):
-        column = jnp.concatenate([as_column(asked[r + i : r + i + 1]) for i in range(step)], axis=0)
-        lane = iota((128 * step, 128), 1)
+    lane = iota((128 * step, 128), 1)
+
+    def look(at, carry):
+        r = step * at
+        column = jnp.concatenate([as_column(held[pl.ds(r + i, 1), :]) for i in range(step)], axis=0)
         chosen = jnp.concatenate(
             [(column == lane + 128 * t).astype(F32).astype(BF) for t in range(stored // 128)], axis=1
         )
         rows = dot(chosen, table_ref[...], 1, 1)
         for i in range(step):
             for k in range(4):
-                at = 128 * i + CAP * k
-                out_ref[part * k + r + i] = pack(rows[at : at + CAP], CAP // 2)
+                first = 128 * i + CAP * k
+                out_ref[part * k + r + i] = pack(rows[first : first + CAP], CAP // 2)
+        return carry
+
+    lax.fori_loop(0, part // step, look, 0)
 
 
 def pieces_kernel(me_ref, slot_ref, fetched_ref, own_hbm, *refs):
@@ -234,9 +239,9 @@
     grads = unpack(held[...])
     groups = out_ref.shape[0]
     step = 16 * CAP
-    copies = []
-    for r in range(0, groups * CAP, step):
-        row = iota((step, 128), 0) + r
+
+    def place(at, carry):
+        row = iota((step, 128), 0) + step * at
         chosen = jnp.concatenate(
             [
                 (jnp.broadcast_to(slot_ref[q : q + 1, :], (step, 128)) == row).astype(F32).astype(BF)
@@ -246,12 +251,15 @@
         )
         rows = dot(chosen, grads)
         for i in range(16):
-            out_ref[r // CAP + i] = pack(rows[CAP * i : CAP * (i + 1)], CAP // 2)
-        at = pl.ds(r // CAP, 16)
-        copies.append(pltpu.make_async_copy(out_ref.at[at], out_hbm.at[at], sem.at[r // step]))
-        copies[-1].start()
-    for c in copies:
-        c.wait()
+            out_ref[16 * at + i] = pack(rows[CAP * i : CAP * (i + 1)], CAP // 2)
+        part = pl.ds(16 * at, 16)
+        pltpu.make_async_copy(out_ref.at[part], out_hbm.at[part], sem.at[at]).start()
+        return carry
+
+    lax.fori_loop(0, groups // 16, place, 0)
+    for at in range(groups // 16):
+        part = pl.ds(16 * at, 16)
+        pltpu.make_async_copy(out_ref.at[part], out_hbm.at[part], sem.at[at]).wait()
 
 
 def landing_kernel(asked_ref, arrived_ref, out_hbm, token_ref, out_ref, sem):
@@ -266,18 +274,22 @@
         [columns[g % part][CAP * (g // part) : CAP * (g // part + 1)] for g in range(4 * part)], axis=0
     )
     step = 512
-    copies = []
     lane = iota((slots, 128), 1)
-    for r in range(0, stored, step):
+
+    def land(i, carry):
+        r = pl.multiple_of(step * i, step)
         chosen = jnp.concatenate(
             [(column == lane + (r + 128 * t)).astype(F32).astype(BF) for t in range(step // 128)], axis=1
         )
-        out_ref[:, r : r + step] = dot(arrived, chosen, 0, 0)[:SLAB]
         at = pl.ds(r, step)
-        copies.append(pltpu.make_async_copy(out_ref.at[:, at], out_hbm.at[:, at], sem.at[r // step]))
-        copies[-1].start()
-    for c in copies:
-        c.wait()
+        out_ref[:, at] = dot(arrived, chosen, 0, 0)[:SLAB]
+        pltpu.make_async_copy(out_ref.at[:, at], out_hbm.at[:, at], sem.at[i]).start()
+        return carry
+
+    lax.fori_loop(0, stored // step, land, 0)
+    for i in range(stored // step):
+        at = pl.ds(step * i, step)
+        pltpu.make_async_copy(out_ref.at[:, at], out_hbm.at[:, at], sem.at[i]).wait()
 
 
 def lane_mean(x):
@@ -477,8 +489,11 @@
         c.wait()
 
 
-def gradients_kernel(me_ref, keep_hbm, other_ref, vectors_ref, *refs):
-    out_refs, (token_ref, grads, held, keep_ref, sem) = refs[:4], refs[4:]
+FIRST = 48
+
+
+def gradients_kernel(x_ref, y_ref, keep_hbm, other_ref, vectors_ref, *refs):
+    x_refs, y_refs, (token_ref, grads, by_x, by_y, keep_ref, sem) = refs[:4], refs[4:8], refs[8:]
     token_ref[...] = jnp.zeros_like(token_ref)
     copies = [pltpu.make_async_copy(keep_hbm.at[i], keep_ref.at[i], sem.at[i]) for i in (0, 2, 1, 3)]
     for c in copies:
@@ -498,17 +513,16 @@
                 rb, t = h // 6, h % 6
                 tiles.append(rows48[8 * rb : 8 * rb + 8, 128 * t : 128 * (t + 1)])
             tiles.append(vectors_ref[8 * m : 8 * m + 8, :])
-            held[m, at] = jnp.concatenate(tiles, axis=0).astype(BF)
+            block = jnp.concatenate(tiles, axis=0).astype(BF)
+            by_x[m, at] = block[:FIRST]
+            by_y[at >> 3, 8 * m + (at & 7)] = block[FIRST:]
         return carry
 
+    lax.fori_loop(0, by_x.shape[1], assemble, 0)
     copies = []
-    n = held.shape[1] // 2
-    for part in (0, 1):
-        lax.fori_loop(n * part, n * (part + 1), assemble, 0)
-        at = pl.ds(n * part, n)
+    for j, (me, held, out_refs) in enumerate(((x_ref[0], by_x, x_refs), (y_ref[0], by_y, y_refs))):
         for k, ref in enumerate(out_refs):
-            source = held.at[(me_ref[0] + k) & 3, at]
-            copies.append(pltpu.make_async_copy(source, ref.at[at], sem.at[4 + 4 * part + k]))
+            copies.append(pltpu.make_async_copy(held.at[(me + k) & 3], ref, sem.at[4 + 4 * j + k]))
             copies[-1].start()
     for c in copies:
         c.wait()
@@ -521,22 +535,25 @@
     return total.astype(BF)
 
 
-def sum_kernel(own_hbm, b_ref, c_ref, d_ref, out_hbm, own_ref, out_ref, sem):
-    n = own_ref.shape[0] // 4
-    loads = [
-        pltpu.make_async_copy(own_hbm.at[pl.ds(n * i, n)], own_ref.at[pl.ds(n * i, n)], sem.at[i]) for i in range(4)
-    ]
-    for c in loads:
-        c.start()
-    copies = []
-    for i in range(4):
-        at = pl.ds(n * i, n)
-        loads[i].wait()
-        out_ref[n * i : n * (i + 1)] = plus(*[r[n * i : n * (i + 1)] for r in (own_ref, b_ref, c_ref, d_ref)])
-        copies.append(pltpu.make_async_copy(out_ref.at[at], out_hbm.at[at], sem.at[4 + i]))
-        copies[-1].start()
-    for c in copies:
-        c.wait()
+def second_kernel(me_ref, own_hbm, b_ref, c_ref, d_ref, *refs):
+    out_refs, (own_ref, total_ref, sem) = refs[:4], refs[4:]
+    copy = pltpu.make_async_copy(own_hbm, own_ref, sem.at[0])
+    copy.start()
+    copy.wait()
+
+    def add(i, carry):
+        total_ref[i] = plus(own_ref[i], b_ref[i], c_ref[i], d_ref[i])
+        return carry
+
+    lax.fori_loop(0, total_ref.shape[0], add, 0)
+    for k, ref in enumerate(out_refs):
+        ref[...] = total_ref[(me_ref[0] + k) & 3]
+
+
+def third_kernel(*refs):
+    x_refs, y_refs, out_ref = refs[:4], refs[4:8], refs[8]
+    out_ref[:, :FIRST, :] = plus(*[r[...] for r in x_refs])
+    out_ref[:, FIRST:, :] = plus(*[r[...] for r in y_refs])
 
 
 def last_kernel(parts_ref, out_ref):
@@ -595,6 +612,7 @@
     slots = n_dp * CAP
 
     along_x = lax.axis_index("x").astype(jnp.int32).reshape(1)
+    along_y = lax.axis_index("y").astype(jnp.int32).reshape(1)
     core = lax.axis_index("c").astype(jnp.int32).reshape(1)
 
     ids = exchange([cand_item] * 4, "x")
@@ -616,7 +634,8 @@
         [pltpu.SemaphoreType.DMA((2,))], 0, (0,), (request,),
     )
     found = call(
-        owner_kernel, shape((n_dp, 48, 128)), (asked, inside(table)), 16, 2 * 10**9, 2 * 10**6
+        owner_kernel, shape((n_dp, 48, 128)), (asked, inside(table)), 16, 2 * 10**9, 2 * 10**6,
+        [pltpu.VMEM((n_dp // 4, 128), jnp.int32)],
     )
     fetched = swap(found, ROWS)
     pieces = call(
@@ -653,18 +672,21 @@
     column_grads = exchange(diff_base, "x")
 
     other = lax.ppermute(send, "c", [(0, 1), (1, 0)])
-    block = shape((n_yz, 80, 128))
+    counts = (FIRST, 80 - FIRST)
     *blocks, made = call(
-        gradients_kernel, [pltpu.HBM(block.shape, BF)] * n_mp + [shape((8, 128), F32)], (along_x, keep, other, vectors), 32, 2 * 10**9, 10**7,
+        gradients_kernel,
+        [pltpu.HBM((n_yz, count, 128), BF) for count in counts for _ in range(4)] + [shape((8, 128), F32)],
+        (along_x, along_y, keep, other, vectors), 32, 2 * 10**9, 10**7,
         [
             pltpu.VMEM((2, width, width), F32),
-            pltpu.VMEM((n_mp, n_yz, 80, 128), BF),
+            pltpu.VMEM((4, n_yz, counts[0], 128), BF),
+            pltpu.VMEM((4, n_yz, counts[1], 128), BF),
             pltpu.VMEM((4, queries * size, width), BF),
             pltpu.SemaphoreType.DMA((12,)),
         ],
-        1, (1,), column_grads[1:],
-    )
-    arrive = exchange(blocks, "x")
+        2, (2,), column_grads[1:],
+    )
+    over_first = [exchange(blocks[:4], "x"), exchange(blocks[4:], "y")]
 
     outgoing = call(
         slots_kernel, pltpu.HBM((n_dp, 48, 128), BF), (along_x, slot, *column_grads), 16, 10**9, 2 * 10**6,
@@ -679,11 +701,16 @@
     )
     table_grad = landed.T
 
-    over_x = call(
-        sum_kernel, pltpu.HBM(block.shape, BF), tuple(arrive), 8, 10**12, 10**7,
-        [pltpu.VMEM(block.shape, BF), pltpu.VMEM(block.shape, BF), pltpu.SemaphoreType.DMA((8,))], 0, (0,),
-    )
-    parts = swap(after(over_x, arrived), ("y", "z"))
+    over_second = []
+    for axis, me, arrive, count in (("y", along_y, over_first[0], counts[0]), ("x", along_x, over_first[1], counts[1])):
+        dims = (4, n_yz // 4, count, 128)
+        blocks = call(
+            second_kernel, [shape(dims[1:])] * 4, (me, *[a.reshape(dims) for a in arrive]), 8, (10**12 if axis == 'y' else 10**6), 10**7,
+            [pltpu.VMEM(dims, BF), pltpu.VMEM(dims, BF), pltpu.SemaphoreType.DMA((1,))], 1, (1,),
+        )
+        over_second += exchange(blocks, axis)
+    along = call(third_kernel, shape((n_yz // 4, 80, 128)), tuple(over_second), 8, 10**6, 10**6)
+    parts = swap(after(along, arrived), "z")
     copies = call(last_kernel, shape((2 * n_mp, 80, 128)), (parts,), 4, 10**6, 10**6, awaited=(token,))
     blocks = swap(copies, ("c", "x"))
     rows = width // n_dp

time: 175 us -> 177 us (1.011)
  waiting for transfers between devices: 55.7 us -> 36.9 us
  starting transfers between devices: 52.5 us -> 68.8 us
  Pallas kernels: 38 us -> 41.6 us
    ppermute x12 -> x21, starting transfers between devices: 16.3 us -> 30.4 us  [shift(): return lax.ppermute(x, axis, [(i, (i + by) % 4) for i in range(4)])]
    ppermute x12 -> x21, waiting for transfers between devices: 30 us -> 16.2 us  [shift(): return lax.ppermute(x, axis, [(i, (i + by) % 4) for i in range(4)])]
    all_to_all x4, waiting for transfers between devices: 25.7 us -> 20.7 us  [swap(): return lax.all_to_all(x, axes, split_axis=0, concat_axis=0, tiled=True)]
    pallas_call x12 -> x14, Pallas kernels: 38 us -> 41.6 us  [call(): pl.pallas_call(run, out_shape=out_shape, in_specs=in_specs, out_specs=spe...]
    all_to_all x4, starting transfers between devices: 34.6 us -> 36.9 us  [swap(): return lax.all_to_all(x, axes, split_axis=0, concat_axis=0, tiled=True)]
  transfers between devices with their start and end apart: 17 -> 26, of which waited for: 12 -> 14; matrix products, arithmetic and copies ran while one was open for 0% -> 0% of each run, Pallas kernels for 6% -> 8%
where the time goes in v4:
time: 177 us
  starting transfers between devices  68.8 us (39%)
  Pallas kernels  41.6 us (24%)
  waiting for transfers between devices  36.9 us (21%)
  blocking collectives  27 us (15%)
    pallas_call x14, Pallas kernels, call(): pl.pallas_call(run, out_shape=out_shape, in_specs=in_specs, out_specs=spe...  41.6 us
    all_to_all x4, starting transfers between devices, swap(): return lax.all_to_all(x, axes, split_axis=0, concat_axis=0, tiled=True)  36.9 us
    ppermute x21, starting transfers between devices, shift(): return lax.ppermute(x, axis, [(i, (i + by) % 4) for i in range(4)])  30.4 us
    all_to_all x1, blocking collectives, swap(): return lax.all_to_all(x, axes, split_axis=0, concat_axis=0, tiled=True)  27 us
    all_to_all x4, waiting for transfers between devices, swap(): return lax.all_to_all(x, axes, split_axis=0, concat_axis=0, tiled=True)  20.7 us
    ppermute x21, waiting for transfers between devices, shift(): return lax.ppermute(x, axis, [(i, (i + by) % 4) for i in range(4)])  16.2 us
  transfers between devices with their start and end apart: 26, of which 14 were waited for; matrix products, arithmetic and copies ran while one was open for 0% of the time, Pallas kernels for 8%

profile of v4, /device:TPU:1, one launch (start us, length us, event | category | flops | bytes accessed | tf_op | source)
XLA Modules:
  0.0 176.5 jit_solution(334469960544886251)
XLA Ops:
  0.6 2.1 %collective-permute-start = (s32[2,128]{1,0:T(2,128)}, s32[2,128]{1,0:T(2,128)S(1)}, u32[]{:S(2)}, u32[]{:S(2)}) collective-permute-start(s32[2,128]{1,0:T(2,128)} %refs_1_.1), channel_id=1, source_target_pairs={{0,1},{1,2},{2,3},{3,0},{4,5},{5,6},{6,7},{7,4},{8,9},{9,10},{10,1... | collective-permute-start | bytes 3080 | tf_op jit(solution)/shard_map/ppermute | solution.py:82
  2.8 1.4 collective-permute-start.2
  4.1 1.6 collective-permute-start.1
  5.8 0.8 shard_map.195
  6.5 0.0 collective-permute-done.refs_2_
  6.5 0.0 collective-permute-done.2.refs_4_
  6.5 1.7 collective-permute-done.1.refs_3_
  8.3 3.4 %shard_map.196 = (s32[64,32]{1,0:T(8,128)}, s32[8,128]{1,0:T(8,128)S(1)}) custom-call(s32[1]{0:T(128)} %bitcast.refs_0_, s32[2,128]{1,0:T(2,128)S(1)} %get-tuple-element.53.refs_1_, s32[2,128]{1,0:T(2,128)S(1)} %collective-permute-done.refs_2_, s32[2,128]{1,0:T(2,128)S(1)} %collective-permute-done.1.refs_3_, s32[2,128]{1,0:T(2,128)S(1)} %collective-permute-done.2.refs_4_, ...), custom_call_target="tpu_custom_call" | custom-call | flops 300000000 | bytes 1000000 | tf_op jit(solution)/shard_map/pallas_call | solution.py:60
  11.7 14.1 %all-to-all-start = ((s32[64,1,32]{2,1,0:T(1,128)}), s32[64,1,32]{2,1,0:T(1,128)S(1)}, u32[]{:S(2)}, u32[]{:S(2)}) async-start(s32[64,1,32]{2,1,0:T(1,128)} %bitcast.4), calls=%async_computation | async-start | bytes 65536 | tf_op jit(solution)/shard_map/all_to_all | solution.py:589
  25.8 1.2 shard_map.197.refs_1_
  27.1 8.0 %all-to-all-done = s32[64,1,32]{2,1,0:T(1,128)S(1)} async-done(((s32[64,1,32]{2,1,0:T(1,128)}), s32[64,1,32]{2,1,0:T(1,128)S(1)}, u32[]{:S(2)}, u32[]{:S(2)}) %all-to-all-start) | async-done | bytes 8224 | tf_op jit(solution)/shard_map/all_to_all | solution.py:589
  35.1 3.1 %shard_map.198 = bf16[64,48,128]{2,1,0:T(8,128)(2,1)S(1)} custom-call(s32[64,32]{1,0:T(8,128)S(1)} %bitcast.21, bf16[256,2048]{1,0:T(8,128)(2,1)S(1)} %shard_map.197.refs_1_), custom_call_target="tpu_custom_call" | custom-call | flops 2000000000 | bytes 2000000 | tf_op jit(solution)/shard_map/pallas_call | solution.py:60
  38.2 27.0 %all_to_all.31.refs_2_ = bf16[64,48,128]{2,1,0:T(8,128)(2,1)S(1)} all-to-all(bf16[64,48,128]{2,1,0:T(8,128)(2,1)S(1)} %shard_map.198), channel_id=1, replica_groups=mesh['y'=4,'z'=8,'c'=2,'x'=4] {'y','z','c'}, dimensions={0} | all-to-all | bytes 1572864 | tf_op jit(solution)/shard_map/all_to_all | solution.py:589
  65.2 0.0 copy-start.2
  65.2 1.8 %shard_map.199 = (bf16[384,128]{1,0:T(8,128)(2,1)}, bf16[384,128]{1,0:T(8,128)(2,1)S(1)}, bf16[384,128]{1,0:T(8,128)(2,1)S(1)}, bf16[384,128]{1,0:T(8,128)(2,1)S(1)}) custom-call(s32[1]{0:T(128)} %bitcast.refs_0_, s32[8,128]{1,0:T(8,128)S(1)} %get-tuple-element.55.refs_1_, bf16[64,48,128]{2,1,0:T(8,128)(2,1)S(1)} %all_to_all.31.refs_2_), custom_call_target="tpu_custom_call" | custom-call | flops 1000000000 | bytes 2000000 | tf_op jit(solution)/shard_map/pallas_call | solution.py:60
  67.0 0.1 collective-permute-start.3
  67.1 2.4 %collective-permute-start.4 = (bf16[384,128]{1,0:T(8,128)(2,1)S(1)}, bf16[384,128]{1,0:T(8,128)(2,1)S(1)}, u32[]{:S(2)}, u32[]{:S(2)}) collective-permute-start(bf16[384,128]{1,0:T(8,128)(2,1)S(1)} %get-tuple-element.59), channel_id=1, source_target_pairs={{0,2},{1,3},{2,0},{3,1},{4,6},{5,7},{6,4},{7,5},{8,10},{9,11},{10,... | collective-permute-start | bytes 294920 | tf_op jit(solution)/shard_map/ppermute | solution.py:82
  69.6 1.2 collective-permute-start.5
  70.8 1.7 collective-permute-done.3.refs_3_
  72.5 1.7 collective-permute-done.4.refs_4_
  74.2 0.5 collective-permute-done.5.refs_5_
  74.7 12.8 %shard_map.200 = (f32[2,128]{1,0:T(2,128)S(1)}, f32[2,768]{1,0:T(2,128)}, bf16[384,128]{1,0:T(8,128)(2,1)S(1)}, bf16[384,128]{1,0:T(8,128)(2,1)S(1)}, bf16[384,1...) custom-call(s32[1]{0:T(128)} %bitcast.refs_0_, ...), custom_call_target="tpu_custom_call" | custom-call | flops 4000000000 | bytes 10000000 | tf_op jit(solution)/shard_map/pallas_call | solution.py:60
  87.5 1.6 collective-permute-start.9
  89.1 0.9 collective-permute-start.6
  90.1 2.7 %collective-permute-start.7 = (bf16[384,128]{1,0:T(8,128)(2,1)S(1)}, bf16[384,128]{1,0:T(8,128)(2,1)S(1)}, u32[]{:S(2)}, u32[]{:S(2)}) collective-permute-start(bf16[384,128]{1,0:T(8,128)(2,1)S(1)} %get-tuple-element.64), channel_id=1, source_target_pairs={{0,2},{1,3},{2,0},{3,1},{4,6},{5,7},{6,4},{7,5},{8,10},{9,11},{10,... | collective-permute-start | bytes 294920 | tf_op jit(solution)/shard_map/ppermute | solution.py:82
  92.7 0.0 collective-permute-start.8
  92.7 1.9 %collective-permute-done.6.refs_5_.refs_3_ = bf16[384,128]{1,0:T(8,128)(2,1)S(1)} collective-permute-done((bf16[384,128]{1,0:T(8,128)(2,1)S(1)}, bf16[384,128]{1,0:T(8,128)(2,1)S(1)}, u32[]{:S(2)}, u32[]{:S(2)}) %collective-permute-start.6) | collective-permute-done | bytes 98336 | tf_op jit(solution)/shard_map/ppermute | solution.py:82
  94.7 3.0 %collective-permute-done.7.refs_6_.refs_4_ = bf16[384,128]{1,0:T(8,128)(2,1)S(1)} collective-permute-done((bf16[384,128]{1,0:T(8,128)(2,1)S(1)}, bf16[384,128]{1,0:T(8,128)(2,1)S(1)}, u32[]{:S(2)}, u32[]{:S(2)}) %collective-permute-start.7) | collective-permute-done | bytes 98336 | tf_op jit(solution)/shard_map/ppermute | solution.py:82
  97.7 0.0 collective-permute-done.8.refs_7_.refs_5_
  97.7 5.1 %shard_map.201 = (bf16[32,48,128]{2,1,0:T(8,128)(2,1)}, bf16[32,48,128]{2,1,0:T(8,128)(2,1)}, bf16[32,48,128]{2,1,0:T(8,128)(2,1)}, bf16[32,48,128]{2,1,0:T(8,12...) custom-call(s32[1]{0:T(128)} %bitcast.refs_0_, ...), custom_call_target="tpu_custom_call" | custom-call | flops 2000000000 | bytes 10000000 | tf_op jit(solution)/shard_map/pallas_call | solution.py:60
  102.8 1.5 collective-permute-start.16
  104.3 0.9 collective-permute-start.10
  105.2 2.7 %collective-permute-start.11 = (bf16[32,48,128]{2,1,0:T(8,128)(2,1)}, bf16[32,48,128]{2,1,0:T(8,128)(2,1)S(1)}, u32[]{:S(2)}, u32[]{:S(2)}) collective-permute-start(bf16[32,48,128]{2,1,0:T(8,128)(2,1)} %get-tuple-element.74), channel_id=1, source_target_pairs={{0,2},{1,3},{2,0},{3,1},{4,6},{5,7},{6,4},{7,5},{8,10},{9,11},{10,... | collective-permute-start | bytes 1179656 | tf_op jit(solution)/shard_map/ppermute | solution.py:82
  107.9 2.6 %collective-permute-start.17 = (bf16[32,32,128]{2,1,0:T(8,128)(2,1)}, bf16[32,32,128]{2,1,0:T(8,128)(2,1)S(1)}, u32[]{:S(2)}, u32[]{:S(2)}) collective-permute-start(bf16[32,32,128]{2,1,0:T(8,128)(2,1)} %get-tuple-element.82), channel_id=1, source_target_pairs={{0,128},{64,192},{128,0},{192,64},{1,129},{65,193},{129,1},{193,65... | collective-permute-start | bytes 786440 | tf_op jit(solution)/shard_map/ppermute | solution.py:82
  110.5 1.0 collective-permute-done.16
  111.5 1.4 collective-permute-start.18
  112.9 2.7 %shard_map.202 = bf16[64,48,128]{2,1,0:T(8,128)(2,1)} custom-call(s32[1]{0:T(128)} %bitcast.refs_0_, s32[8,128]{1,0:T(8,128)S(1)} %get-tuple-element.55.refs_1_, bf16[384,128]{1,0:T(8,128)(2,1)S(1)} %get-tuple-element.62.refs_2_, bf16[384,128]{1,0:T(8,128)(2,1)S(1)} %collective-permute-done.6.refs_5_.refs_3_, ...), custom_call_target="tpu_custom_call" | custom-call | flops 1000000000 | bytes 2000000 | tf_op jit(solution)/shard_map/pallas_call | solution.py:60
  115.6 12.4 %all-to-all-start.2 = ((bf16[64,48,128]{2,1,0:T(8,128)(2,1)}), bf16[64,48,128]{2,1,0:T(8,128)(2,1)}, u32[]{:S(2)}, u32[]{:S(2)}) async-start(bf16[64,48,128]{2,1,0:T(8,128)(2,1)} %shard_map.202), calls=%async_computation.2 | async-start | bytes 1572864 | tf_op jit(solution)/shard_map/all_to_all | solution.py:589
  128.0 0.0 collective-permute-done.17
  128.0 1.7 shard_map.205
  129.8 1.0 collective-permute-start.19
  130.8 0.0 collective-permute-done.10
  130.8 1.3 shard_map.204
  132.1 1.5 collective-permute-start.13
  133.5 2.6 %collective-permute-start.14 = (bf16[8,48,128]{2,1,0:T(8,128)(2,1)S(1)}, bf16[8,48,128]{2,1,0:T(8,128)(2,1)S(1)}, u32[]{:S(2)}, u32[]{:S(2)}) collective-permute-start(bf16[8,48,128]{2,1,0:T(8,128)(2,1)S(1)} %get-tuple-element.78), channel_id=1, source_target_pairs={{0,128},{64,192},{128,0},{192,64},{1,129},{65,193},{129,1},{193,65... | collective-permute-start | bytes 294920 | tf_op jit(solution)/shard_map/ppermute | solution.py:82
  136.1 1.1 collective-permute-start.15
  137.2 2.7 %collective-permute-start.20 = (bf16[8,32,128]{2,1,0:T(8,128)(2,1)S(1)}, bf16[8,32,128]{2,1,0:T(8,128)(2,1)S(1)}, u32[]{:S(2)}, u32[]{:S(2)}) collective-permute-start(bf16[8,32,128]{2,1,0:T(8,128)(2,1)S(1)} %get-tuple-element.86), channel_id=1, source_target_pairs={{0,2},{1,3},{2,0},{3,1},{4,6},{5,7},{6,4},{7,5},{8,10},{9,11},{10,... | collective-permute-start | bytes 196616 | tf_op jit(solution)/shard_map/ppermute | solution.py:82
  139.9 0.0 collective-permute-done.19.refs_5_
  139.9 0.0 collective-permute-start.21
  139.9 2.3 %collective-permute-done.20.refs_6_ = bf16[8,32,128]{2,1,0:T(8,128)(2,1)S(1)} collective-permute-done((bf16[8,32,128]{2,1,0:T(8,128)(2,1)S(1)}, bf16[8,32,128]{2,1,0:T(8,128)(2,1)S(1)}, u32[]{:S(2)}, u32[]{:S(2)}) %collective-permute-start.20) | collective-permute-done | bytes 65568 | tf_op jit(solution)/shard_map/ppermute | solution.py:82
  142.2 1.8 %collective-permute-done.21.refs_7_ = bf16[8,32,128]{2,1,0:T(8,128)(2,1)S(1)} collective-permute-done((bf16[8,32,128]{2,1,0:T(8,128)(2,1)S(1)}, bf16[8,32,128]{2,1,0:T(8,128)(2,1)S(1)}, u32[]{:S(2)}, u32[]{:S(2)}) %collective-permute-start.21) | collective-permute-done | bytes 65568 | tf_op jit(solution)/shard_map/ppermute | solution.py:82
  144.0 0.5 collective-permute-done.14.refs_2_
  144.6 0.0 collective-permute-done.15.refs_3_
  144.6 0.9 shard_map.206.refs_0_
  145.5 0.6 copy-done
  146.2 4.8 %all-to-all-done.2.refs_1_ = bf16[64,48,128]{2,1,0:T(8,128)(2,1)} async-done(((bf16[64,48,128]{2,1,0:T(8,128)(2,1)}), bf16[64,48,128]{2,1,0:T(8,128)(2,1)}, u32[]{:S(2)}, u32[]{:S(2)}) %all-to-all-start.2) | async-done | bytes 786464 | tf_op jit(solution)/shard_map/all_to_all | solution.py:589
  150.9 4.0 %all-to-all-start.3 = ((bf16[8,80,128]{2,1,0:T(8,128)(2,1)}), bf16[8,80,128]{2,1,0:T(8,128)(2,1)S(1)}, u32[]{:S(2)}, u32[]{:S(2)}) async-start(bf16[8,80,128]{2,1,0:T(8,128)(2,1)} %shard_map.207), calls=%async_computation.3 | async-start | bytes 327680 | tf_op jit(solution)/shard_map/all_to_all | solution.py:589
  154.9 5.4 %shard_map.203 = (f32[192,2048]{1,0:T(8,128)}, f32[8,128]{1,0:T(8,128)S(1)}) custom-call(s32[64,32]{1,0:T(8,128)S(1)} %bitcast.22, bf16[64,48,128]{2,1,0:T(8,128)(2,1)} %all-to-all-done.2.refs_1_), custom_call_target="tpu_custom_call" | custom-call | flops 2000000000 | bytes 4000000 | tf_op jit(solution)/shard_map/pallas_call | solution.py:60
  160.3 3.0 %all-to-all-done.3.refs_0_ = bf16[8,80,128]{2,1,0:T(8,128)(2,1)S(1)} async-done(((bf16[8,80,128]{2,1,0:T(8,128)(2,1)}), bf16[8,80,128]{2,1,0:T(8,128)(2,1)S(1)}, u32[]{:S(2)}, u32[]{:S(2)}) %all-to-all-start.3) | async-done | bytes 163872 | tf_op jit(solution)/shard_map/all_to_all | solution.py:589
  163.4 0.7 shard_map.208
  164.1 6.3 %all-to-all-start.4 = ((bf16[8,80,128]{2,1,0:T(8,128)(2,1)}), bf16[8,80,128]{2,1,0:T(8,128)(2,1)S(1)}, u32[]{:S(2)}, u32[]{:S(2)}) async-start(bf16[8,80,128]{2,1,0:T(8,128)(2,1)} %shard_map.208), calls=%async_computation.4 | async-start | bytes 327680 | tf_op jit(solution)/shard_map/all_to_all | solution.py:589
  170.3 0.6 slice_reduce_fusion
  171.0 4.9 %all-to-all-done.4.refs_1_ = bf16[8,80,128]{2,1,0:T(8,128)(2,1)S(1)} async-done(((bf16[8,80,128]{2,1,0:T(8,128)(2,1)}), bf16[8,80,128]{2,1,0:T(8,128)(2,1)S(1)}, u32[]{:S(2)}, u32[]{:S(2)}) %all-to-all-start.4) | async-done | bytes 163872 | tf_op jit(solution)/shard_map/all_to_all | solution.py:589
  175.8 0.7 shard_map.209
  (20 shorter events, 0.0 us)
Async XLA Ops:
  0.6 5.9 %collective-permute-start = (s32[2,128]{1,0:T(2,128)}, s32[2,128]{1,0:T(2,128)S(1)}, u32[]{:S(2)}, u32[]{:S(2)}) collective-permute-start(s32[2,128]{1,0:T(2,128)} %refs_1_.1), channel_id=1, source_target_pairs={{0,1},{1,2},{2,3},{3,0},{4,5},{5,6},{6,7},{7,4},{8,9},{9,10},{10,1... | collective-permute-start | bytes 3080 | tf_op jit(solution)/shard_map/ppermute | solution.py:82
  2.8 3.8 %collective-permute-start.2 = (s32[2,128]{1,0:T(2,128)}, s32[2,128]{1,0:T(2,128)S(1)}, u32[]{:S(2)}, u32[]{:S(2)}) collective-permute-start(s32[2,128]{1,0:T(2,128)} %refs_1_.1), channel_id=1, source_target_pairs={{0,3},{1,0},{2,1},{3,2},{4,7},{5,4},{6,5},{7,6},{8,11},{9,8},{10,9... | collective-permute-start | bytes 3080 | tf_op jit(solution)/shard_map/ppermute | solution.py:82
  4.1 4.1 %collective-permute-start.1 = (s32[2,128]{1,0:T(2,128)}, s32[2,128]{1,0:T(2,128)S(1)}, u32[]{:S(2)}, u32[]{:S(2)}) collective-permute-start(s32[2,128]{1,0:T(2,128)} %refs_1_.1), channel_id=1, source_target_pairs={{0,2},{1,3},{2,0},{3,1},{4,6},{5,7},{6,4},{7,5},{8,10},{9,11},{10,... | collective-permute-start | bytes 3080 | tf_op jit(solution)/shard_map/ppermute | solution.py:82
  11.7 23.4 %all-to-all-start = ((s32[64,1,32]{2,1,0:T(1,128)}), s32[64,1,32]{2,1,0:T(1,128)S(1)}, u32[]{:S(2)}, u32[]{:S(2)}) async-start(s32[64,1,32]{2,1,0:T(1,128)} %bitcast.4), calls=%async_computation | async-start | bytes 65536 | tf_op jit(solution)/shard_map/all_to_all | solution.py:589
  65.2 5.5 %copy-start.3 = (f32[768]{0:T(1024)S(1)}, f32[768]{0:T(1024)}, u32[]{:S(2)}) copy-start(f32[768]{0:T(1024)} %param.21) | copy-start | bytes 9220
  65.2 5.5 %copy-start.4 = (f32[768]{0:T(1024)S(1)}, f32[768]{0:T(1024)}, u32[]{:S(2)}) copy-start(f32[768]{0:T(1024)} %param.22) | copy-start | bytes 9220
  65.2 5.6 %copy-start.5 = (f32[768]{0:T(1024)S(1)}, f32[768]{0:T(1024)}, u32[]{:S(2)}) copy-start(f32[768]{0:T(1024)} %param.23) | copy-start | bytes 9220
  65.2 9.5 %copy-start.1 = (bf16[2,768]{1,0:T(2,128)(2,1)S(1)}, bf16[2,768]{1,0:T(2,128)(2,1)}, u32[]{:S(2)}) copy-start(bf16[2,768]{1,0:T(2,128)(2,1)} %refs_6_.1) | copy-start | bytes 9220
  65.2 9.5 %copy-start.2 = (s32[2,128]{1,0:T(2,128)S(1)}, s32[2,128]{1,0:T(2,128)}, u32[]{:S(2)}) copy-start(s32[2,128]{1,0:T(2,128)} %refs_7_.1) | copy-start | bytes 3076
  67.0 5.5 %collective-permute-start.3 = (bf16[384,128]{1,0:T(8,128)(2,1)S(1)}, bf16[384,128]{1,0:T(8,128)(2,1)S(1)}, u32[]{:S(2)}, u32[]{:S(2)}) collective-permute-start(bf16[384,128]{1,0:T(8,128)(2,1)S(1)} %get-tuple-element.58), channel_id=1, source_target_pairs={{0,1},{1,2},{2,3},{3,0},{4,5},{5,6},{6,7},{7,4},{8,9},{9,10},{10,1... | collective-permute-start | bytes 294920 | tf_op jit(solution)/shard_map/ppermute | solution.py:82
  67.1 7.1 %collective-permute-start.4 = (bf16[384,128]{1,0:T(8,128)(2,1)S(1)}, bf16[384,128]{1,0:T(8,128)(2,1)S(1)}, u32[]{:S(2)}, u32[]{:S(2)}) collective-permute-start(bf16[384,128]{1,0:T(8,128)(2,1)S(1)} %get-tuple-element.59), channel_id=1, source_target_pairs={{0,2},{1,3},{2,0},{3,1},{4,6},{5,7},{6,4},{7,5},{8,10},{9,11},{10,... | collective-permute-start | bytes 294920 | tf_op jit(solution)/shard_map/ppermute | solution.py:82
  69.6 5.1 %collective-permute-start.5 = (bf16[384,128]{1,0:T(8,128)(2,1)S(1)}, bf16[384,128]{1,0:T(8,128)(2,1)S(1)}, u32[]{:S(2)}, u32[]{:S(2)}) collective-permute-start(bf16[384,128]{1,0:T(8,128)(2,1)S(1)} %get-tuple-element.60), channel_id=1, source_target_pairs={{0,3},{1,0},{2,1},{3,2},{4,7},{5,4},{6,5},{7,6},{8,11},{9,8},{10,9... | collective-permute-start | bytes 294920 | tf_op jit(solution)/shard_map/ppermute | solution.py:82
  87.5 10.2 %collective-permute-start.9 = (bf16[4,256,768]{2,1,0:T(8,128)(2,1)}, bf16[4,256,768]{2,1,0:T(8,128)(2,1)S(1)}, u32[]{:S(2)}, u32[]{:S(2)}) collective-permute-start(bf16[4,256,768]{2,1,0:T(8,128)(2,1)} %get-tuple-element.67), channel_id=1, source_target_pairs={{0,4},{4,0},{1,5},{5,1},{2,6},{6,2},{3,7},{7,3},{8,12},{12,8},{9,1... | collective-permute-start | bytes 4718600 | tf_op jit(solution)/shard_map/ppermute | solution.py:674
  89.1 5.6 %collective-permute-start.6 = (bf16[384,128]{1,0:T(8,128)(2,1)S(1)}, bf16[384,128]{1,0:T(8,128)(2,1)S(1)}, u32[]{:S(2)}, u32[]{:S(2)}) collective-permute-start(bf16[384,128]{1,0:T(8,128)(2,1)S(1)} %get-tuple-element.63), channel_id=1, source_target_pairs={{0,1},{1,2},{2,3},{3,0},{4,5},{5,6},{6,7},{7,4},{8,9},{9,10},{10,1... | collective-permute-start | bytes 294920 | tf_op jit(solution)/shard_map/ppermute | solution.py:82
  90.1 7.6 %collective-permute-start.7 = (bf16[384,128]{1,0:T(8,128)(2,1)S(1)}, bf16[384,128]{1,0:T(8,128)(2,1)S(1)}, u32[]{:S(2)}, u32[]{:S(2)}) collective-permute-start(bf16[384,128]{1,0:T(8,128)(2,1)S(1)} %get-tuple-element.64), channel_id=1, source_target_pairs={{0,2},{1,3},{2,0},{3,1},{4,6},{5,7},{6,4},{7,5},{8,10},{9,11},{10,... | collective-permute-start | bytes 294920 | tf_op jit(solution)/shard_map/ppermute | solution.py:82
  92.7 5.0 %collective-permute-start.8 = (bf16[384,128]{1,0:T(8,128)(2,1)S(1)}, bf16[384,128]{1,0:T(8,128)(2,1)S(1)}, u32[]{:S(2)}, u32[]{:S(2)}) collective-permute-start(bf16[384,128]{1,0:T(8,128)(2,1)S(1)} %get-tuple-element.65), channel_id=1, source_target_pairs={{0,3},{1,0},{2,1},{3,2},{4,7},{5,4},{6,5},{7,6},{8,11},{9,8},{10,9... | collective-permute-start | bytes 294920 | tf_op jit(solution)/shard_map/ppermute | solution.py:82
  102.8 8.7 %collective-permute-start.16 = (bf16[32,32,128]{2,1,0:T(8,128)(2,1)}, bf16[32,32,128]{2,1,0:T(8,128)(2,1)S(1)}, u32[]{:S(2)}, u32[]{:S(2)}) collective-permute-start(bf16[32,32,128]{2,1,0:T(8,128)(2,1)} %get-tuple-element.81), channel_id=1, source_target_pairs={{0,64},{64,128},{128,192},{192,0},{1,65},{65,129},{129,193},{193,1... | collective-permute-start | bytes 786440 | tf_op jit(solution)/shard_map/ppermute | solution.py:82
  104.3 26.5 %collective-permute-start.10 = (bf16[32,48,128]{2,1,0:T(8,128)(2,1)}, bf16[32,48,128]{2,1,0:T(8,128)(2,1)S(1)}, u32[]{:S(2)}, u32[]{:S(2)}) collective-permute-start(bf16[32,48,128]{2,1,0:T(8,128)(2,1)} %get-tuple-element.73), channel_id=1, source_target_pairs={{0,1},{1,2},{2,3},{3,0},{4,5},{5,6},{6,7},{7,4},{8,9},{9,10},{10,1... | collective-permute-start | bytes 1179656 | tf_op jit(solution)/shard_map/ppermute | solution.py:82
  105.2 25.6 %collective-permute-start.11 = (bf16[32,48,128]{2,1,0:T(8,128)(2,1)}, bf16[32,48,128]{2,1,0:T(8,128)(2,1)S(1)}, u32[]{:S(2)}, u32[]{:S(2)}) collective-permute-start(bf16[32,48,128]{2,1,0:T(8,128)(2,1)} %get-tuple-element.74), channel_id=1, source_target_pairs={{0,2},{1,3},{2,0},{3,1},{4,6},{5,7},{6,4},{7,5},{8,10},{9,11},{10,... | collective-permute-start | bytes 1179656 | tf_op jit(solution)/shard_map/ppermute | solution.py:82
  107.9 22.9 %collective-permute-start.12 = (bf16[32,48,128]{2,1,0:T(8,128)(2,1)}, bf16[32,48,128]{2,1,0:T(8,128)(2,1)S(1)}, u32[]{:S(2)}, u32[]{:S(2)}) collective-permute-start(bf16[32,48,128]{2,1,0:T(8,128)(2,1)} %get-tuple-element.75), channel_id=1, source_target_pairs={{0,3},{1,0},{2,1},{3,2},{4,7},{5,4},{6,5},{7,6},{8,11},{9,8},{10,9... | collective-permute-start | bytes 1179656 | tf_op jit(solution)/shard_map/ppermute | solution.py:82
  107.9 20.1 %collective-permute-start.17 = (bf16[32,32,128]{2,1,0:T(8,128)(2,1)}, bf16[32,32,128]{2,1,0:T(8,128)(2,1)S(1)}, u32[]{:S(2)}, u32[]{:S(2)}) collective-permute-start(bf16[32,32,128]{2,1,0:T(8,128)(2,1)} %get-tuple-element.82), channel_id=1, source_target_pairs={{0,128},{64,192},{128,0},{192,64},{1,129},{65,193},{129,1},{193,65... | collective-permute-start | bytes 786440 | tf_op jit(solution)/shard_map/ppermute | solution.py:82
  111.5 16.5 %collective-permute-start.18 = (bf16[32,32,128]{2,1,0:T(8,128)(2,1)}, bf16[32,32,128]{2,1,0:T(8,128)(2,1)S(1)}, u32[]{:S(2)}, u32[]{:S(2)}) collective-permute-start(bf16[32,32,128]{2,1,0:T(8,128)(2,1)} %get-tuple-element.83), channel_id=1, source_target_pairs={{0,192},{64,0},{128,64},{192,128},{1,193},{65,1},{129,65},{193,129... | collective-permute-start | bytes 786440 | tf_op jit(solution)/shard_map/ppermute | solution.py:82
  115.6 35.4 %all-to-all-start.2 = ((bf16[64,48,128]{2,1,0:T(8,128)(2,1)}), bf16[64,48,128]{2,1,0:T(8,128)(2,1)}, u32[]{:S(2)}, u32[]{:S(2)}) async-start(bf16[64,48,128]{2,1,0:T(8,128)(2,1)} %shard_map.202), calls=%async_computation.2 | async-start | bytes 1572864 | tf_op jit(solution)/shard_map/all_to_all | solution.py:589
  129.8 10.1 %collective-permute-start.19 = (bf16[8,32,128]{2,1,0:T(8,128)(2,1)}, bf16[8,32,128]{2,1,0:T(8,128)(2,1)}, u32[]{:S(2)}, u32[]{:S(2)}) collective-permute-start(bf16[8,32,128]{2,1,0:T(8,128)(2,1)} %get-tuple-element.85), channel_id=1, source_target_pairs={{0,1},{1,2},{2,3},{3,0},{4,5},{5,6},{6,7},{7,4},{8,9},{9,10},{10,1... | collective-permute-start | bytes 196616 | tf_op jit(solution)/shard_map/ppermute | solution.py:82
  132.1 11.9 %collective-permute-start.13 = (bf16[8,48,128]{2,1,0:T(8,128)(2,1)S(1)}, bf16[8,48,128]{2,1,0:T(8,128)(2,1)S(1)}, u32[]{:S(2)}, u32[]{:S(2)}) collective-permute-start(bf16[8,48,128]{2,1,0:T(8,128)(2,1)S(1)} %get-tuple-element.77), channel_id=1, source_target_pairs={{0,64},{64,128},{128,192},{192,0},{1,65},{65,129},{129,193},{193,1... | collective-permute-start | bytes 294920 | tf_op jit(solution)/shard_map/ppermute | solution.py:82
  133.5 11.0 %collective-permute-start.14 = (bf16[8,48,128]{2,1,0:T(8,128)(2,1)S(1)}, bf16[8,48,128]{2,1,0:T(8,128)(2,1)S(1)}, u32[]{:S(2)}, u32[]{:S(2)}) collective-permute-start(bf16[8,48,128]{2,1,0:T(8,128)(2,1)S(1)} %get-tuple-element.78), channel_id=1, source_target_pairs={{0,128},{64,192},{128,0},{192,64},{1,129},{65,193},{129,1},{193,65... | collective-permute-start | bytes 294920 | tf_op jit(solution)/shard_map/ppermute | solution.py:82
  136.1 8.4 %collective-permute-start.15 = (bf16[8,48,128]{2,1,0:T(8,128)(2,1)S(1)}, bf16[8,48,128]{2,1,0:T(8,128)(2,1)S(1)}, u32[]{:S(2)}, u32[]{:S(2)}) collective-permute-start(bf16[8,48,128]{2,1,0:T(8,128)(2,1)S(1)} %get-tuple-element.79), channel_id=1, source_target_pairs={{0,192},{64,0},{128,64},{192,128},{1,193},{65,1},{129,65},{193,129... | collective-permute-start | bytes 294920 | tf_op jit(solution)/shard_map/ppermute | solution.py:82
  137.2 5.0 %collective-permute-start.20 = (bf16[8,32,128]{2,1,0:T(8,128)(2,1)S(1)}, bf16[8,32,128]{2,1,0:T(8,128)(2,1)S(1)}, u32[]{:S(2)}, u32[]{:S(2)}) collective-permute-start(bf16[8,32,128]{2,1,0:T(8,128)(2,1)S(1)} %get-tuple-element.86), channel_id=1, source_target_pairs={{0,2},{1,3},{2,0},{3,1},{4,6},{5,7},{6,4},{7,5},{8,10},{9,11},{10,... | collective-permute-start | bytes 196616 | tf_op jit(solution)/shard_map/ppermute | solution.py:82
  139.9 4.1 %collective-permute-start.21 = (bf16[8,32,128]{2,1,0:T(8,128)(2,1)S(1)}, bf16[8,32,128]{2,1,0:T(8,128)(2,1)S(1)}, u32[]{:S(2)}, u32[]{:S(2)}) collective-permute-start(bf16[8,32,128]{2,1,0:T(8,128)(2,1)S(1)} %get-tuple-element.87), channel_id=1, source_target_pairs={{0,3},{1,0},{2,1},{3,2},{4,7},{5,4},{6,5},{7,6},{8,11},{9,8},{10,9... | collective-permute-start | bytes 196616 | tf_op jit(solution)/shard_map/ppermute | solution.py:82
  145.5 0.7 copy-start
  150.9 12.4 %all-to-all-start.3 = ((bf16[8,80,128]{2,1,0:T(8,128)(2,1)}), bf16[8,80,128]{2,1,0:T(8,128)(2,1)S(1)}, u32[]{:S(2)}, u32[]{:S(2)}) async-start(bf16[8,80,128]{2,1,0:T(8,128)(2,1)} %shard_map.207), calls=%async_computation.3 | async-start | bytes 327680 | tf_op jit(solution)/shard_map/all_to_all | solution.py:589
  164.1 11.8 %all-to-all-start.4 = ((bf16[8,80,128]{2,1,0:T(8,128)(2,1)}), bf16[8,80,128]{2,1,0:T(8,128)(2,1)S(1)}, u32[]{:S(2)}, u32[]{:S(2)}) async-start(bf16[8,80,128]{2,1,0:T(8,128)(2,1)} %shard_map.208), calls=%async_computation.4 | async-start | bytes 327680 | tf_op jit(solution)/shard_map/all_to_all | solution.py:589

commit v5 on v3

--- a/solution.py
+++ b/solution.py
@@ -293,7 +293,7 @@
     d_ref,
     query_ref,
     labels_ref,
-    wq_hbm,
+    wq_ref,
     wk_hbm,
     wv_hbm,
     wo_hbm,
@@ -312,7 +312,6 @@
     held,
     scores_t,
     attend_t,
-    wq_ref,
     wk_ref,
     wv_ref,
     wo_ref,
@@ -323,8 +322,8 @@
     me = me_ref[0]
     own = pltpu.make_async_copy(a_hbm, held.at[me], sem.at[8])
     own.start()
-    sources = (wq_hbm, wk_hbm, wv_hbm, wo_hbm)
-    weights = (wq_ref, wk_ref, wv_ref, wo_ref)
+    sources = (wk_hbm, wv_hbm, wo_hbm)
+    weights = (wk_ref, wv_ref, wo_ref)
     half = wq_ref.shape[0] // 2
     copies = [
         pltpu.make_async_copy(a.at[pl.ds(half * h, half)], b.at[pl.ds(half * h, half)], sem.at[2 * i + h])
@@ -356,13 +355,11 @@
     normed_one = base * inv_one
     gain_attn = gain_attn_ref[...]
     first_input = (normed_one * gain_attn).astype(BF)
+    q_all = dot(first_input, wq_ref[...]).astype(BF)
     for c in copies[0 : 2]:
         c.wait()
-    q_all = dot(first_input, wq_ref[...]).astype(BF)
+    k_all = dot(first_input, wk_ref[...]).astype(BF)
     for c in copies[2 : 4]:
-        c.wait()
-    k_all = dot(first_input, wk_ref[...]).astype(BF)
-    for c in copies[4 : 6]:
         c.wait()
     v_all = dot(first_input, wv_ref[...]).astype(BF)
 
@@ -391,7 +388,7 @@
         context.append(jnp.concatenate(line, axis=1))
     context = jnp.concatenate(context, axis=0).astype(BF)
 
-    for c in copies[6 : 8]:
+    for c in copies[4 : 6]:
         c.wait()
     mixed = base + dot(context, wo_ref[...])
     inv_two = 1.0 / jnp.sqrt(lane_mean(mixed * mixed) + EPSILON)
@@ -480,15 +477,16 @@
 def gradients_kernel(me_ref, keep_hbm, other_ref, vectors_ref, *refs):
     out_refs, (token_ref, grads, held, keep_ref, sem) = refs[:4], refs[4:]
     token_ref[...] = jnp.zeros_like(token_ref)
-    copies = [pltpu.make_async_copy(keep_hbm.at[i], keep_ref.at[i], sem.at[i]) for i in (0, 2, 1, 3)]
-    for c in copies:
+    loads = [pltpu.make_async_copy(keep_hbm.at[i], keep_ref.at[i], sem.at[i]) for i in (0, 2, 1, 3)]
+    for c in loads:
         c.start()
-    for j in (0, 1):
-        copies[2 * j].wait()
-        copies[2 * j + 1].wait()
-        left = jnp.concatenate([keep_ref[j], other_ref[j]], axis=0)
-        right = jnp.concatenate([keep_ref[2 + j], other_ref[2 + j]], axis=0)
-        grads[j] = dot(left, right, 0, 0)
+    grads[0] = dot(other_ref[0], other_ref[2], 0, 0)
+    for c in loads:
+        c.wait()
+    grads[0] = grads[0] + dot(keep_ref[0], keep_ref[2], 0, 0)
+    left = jnp.concatenate([keep_ref[1], other_ref[1]], axis=0)
+    right = jnp.concatenate([keep_ref[3], other_ref[3]], axis=0)
+    grads[1] = dot(left, right, 0, 0)
 
     def assemble(at, carry):
         rows48 = jnp.concatenate([grads[j, pl.ds(pl.multiple_of(24 * at, 8), 24), :] for j in (0, 1)], axis=0)
@@ -501,17 +499,12 @@
             held[m, at] = jnp.concatenate(tiles, axis=0).astype(BF)
         return carry
 
-    copies = []
-    n = held.shape[1] // 2
-    for part in (0, 1):
-        lax.fori_loop(n * part, n * (part + 1), assemble, 0)
-        at = pl.ds(n * part, n)
-        for k, ref in enumerate(out_refs):
-            source = held.at[(me_ref[0] + k) & 3, at]
-            copies.append(pltpu.make_async_copy(source, ref.at[at], sem.at[4 + 4 * part + k]))
-            copies[-1].start()
-    for c in copies:
-        c.wait()
+    lax.fori_loop(0, held.shape[1], assemble, 0)
+    own = pltpu.make_async_copy(held.at[me_ref[0]], out_refs[0], sem.at[4])
+    own.start()
+    for k in (1, 2, 3):
+        out_refs[k][...] = held[(me_ref[0] + k) & 3]
+    own.wait()
 
 
 def plus(*refs):
@@ -642,10 +635,10 @@
             pltpu.VMEM((HEADS * queries // 2, 128, 256), F32),
             pltpu.VMEM((HEADS * queries // 2, 128, 256), F32),
         ]
-        + [pltpu.VMEM((width, width), BF)] * 4
+        + [pltpu.VMEM((width, width), BF)] * 3
         + [pltpu.VMEM((4, queries * size, width), BF)] * 2
         + [pltpu.SemaphoreType.DMA((17,))],
-        2, (2, 8, 9, 10, 11),
+        2, (2, 9, 10, 11),
     )
     losses, query_grad, diff_base = outs[0], outs[1], outs[2:6]
     keep, send, vectors = outs[6:]
@@ -655,12 +648,12 @@
     other = lax.ppermute(send, "c", [(0, 1), (1, 0)])
     block = shape((n_yz, 80, 128))
     *blocks, made = call(
-        gradients_kernel, [pltpu.HBM(block.shape, BF)] * n_mp + [shape((8, 128), F32)], (along_x, keep, other, vectors), 32, 2 * 10**9, 10**7,
+        gradients_kernel, [pltpu.HBM(block.shape, BF)] + [block] * 3 + [shape((8, 128), F32)], (along_x, keep, other, vectors), 32, 2 * 10**9, 10**7,
         [
             pltpu.VMEM((2, width, width), F32),
             pltpu.VMEM((n_mp, n_yz, 80, 128), BF),
             pltpu.VMEM((4, queries * size, width), BF),
-            pltpu.SemaphoreType.DMA((12,)),
+            pltpu.SemaphoreType.DMA((5,)),
         ],
         1, (1,), column_grads[1:],
     )

time: 175 us -> 176 us (level)
  transfers between devices with their start and end apart: 17 -> 17, of which waited for: 12 -> 12; matrix products, arithmetic and copies ran while one was open for 0% -> 0% of each run, Pallas kernels for 6% -> 7%
where the time goes in v5:
time: 176 us; the launch traced here: 175 us
  waiting for transfers between devices  54.8 us (31%)
  starting transfers between devices  52.8 us (30%)
  Pallas kernels  39 us (22%)
  blocking collectives  27 us (15%)
    pallas_call x12, Pallas kernels, call(): pl.pallas_call(run, out_shape=out_shape, in_specs=in_specs, out_specs=spe...  39 us
    all_to_all x4, starting transfers between devices, swap(): return lax.all_to_all(x, axes, split_axis=0, concat_axis=0, tiled=True)  34.8 us
    ppermute x12, waiting for transfers between devices, shift(): return lax.ppermute(x, axis, [(i, (i + by) % 4) for i in range(4)])  30 us
    all_to_all x1, blocking collectives, swap(): return lax.all_to_all(x, axes, split_axis=0, concat_axis=0, tiled=True)  27 us
    all_to_all x4, waiting for transfers between devices, swap(): return lax.all_to_all(x, axes, split_axis=0, concat_axis=0, tiled=True)  24.8 us
    ppermute x12, starting transfers between devices, shift(): return lax.ppermute(x, axis, [(i, (i + by) % 4) for i in range(4)])  16.3 us
  transfers between devices with their start and end apart: 17, of which 12 were waited for; matrix products, arithmetic and copies ran while one was open for 0% of the time, Pallas kernels for 7%

profile of v5, /device:TPU:1, one launch (start us, length us, event | category | flops | bytes accessed | tf_op | source)
XLA Modules:
  0.0 175.1 jit_solution(13425506870120418121)
XLA Ops:
  0.6 2.1 %collective-permute-start = (s32[2,128]{1,0:T(2,128)}, s32[2,128]{1,0:T(2,128)S(1)}, u32[]{:S(2)}, u32[]{:S(2)}) collective-permute-start(s32[2,128]{1,0:T(2,128)} %refs_1_.1), channel_id=1, source_target_pairs={{0,1},{1,2},{2,3},{3,0},{4,5},{5,6},{6,7},{7,4},{8,9},{9,10},{10,1... | collective-permute-start | bytes 3080 | tf_op jit(solution)/shard_map/ppermute | solution.py:82
  2.8 1.4 collective-permute-start.2
  4.1 1.6 collective-permute-start.1
  5.8 0.8 shard_map.195
  6.5 0.0 collective-permute-done.refs_2_
  6.5 0.0 collective-permute-done.2.refs_4_
  6.5 1.7 collective-permute-done.1.refs_3_
  8.3 3.4 %shard_map.196 = (s32[64,32]{1,0:T(8,128)}, s32[8,128]{1,0:T(8,128)S(1)}) custom-call(s32[1]{0:T(128)} %bitcast.refs_0_, s32[2,128]{1,0:T(2,128)S(1)} %get-tuple-element.41.refs_1_, s32[2,128]{1,0:T(2,128)S(1)} %collective-permute-done.refs_2_, s32[2,128]{1,0:T(2,128)S(1)} %collective-permute-done.1.refs_3_, s32[2,128]{1,0:T(2,128)S(1)} %collective-permute-done.2.refs_4_, ...), custom_call_target="tpu_custom_call" | custom-call | flops 300000000 | bytes 1000000 | tf_op jit(solution)/shard_map/pallas_call | solution.py:60
  11.7 14.1 %all-to-all-start = ((s32[64,1,32]{2,1,0:T(1,128)}), s32[64,1,32]{2,1,0:T(1,128)S(1)}, u32[]{:S(2)}, u32[]{:S(2)}) async-start(s32[64,1,32]{2,1,0:T(1,128)} %bitcast.4), calls=%async_computation | async-start | bytes 65536 | tf_op jit(solution)/shard_map/all_to_all | solution.py:565
  25.8 1.2 shard_map.197.refs_1_
  27.1 8.0 %all-to-all-done = s32[64,1,32]{2,1,0:T(1,128)S(1)} async-done(((s32[64,1,32]{2,1,0:T(1,128)}), s32[64,1,32]{2,1,0:T(1,128)S(1)}, u32[]{:S(2)}, u32[]{:S(2)}) %all-to-all-start) | async-done | bytes 8224 | tf_op jit(solution)/shard_map/all_to_all | solution.py:565
  35.1 2.4 %shard_map.198 = bf16[64,48,128]{2,1,0:T(8,128)(2,1)S(1)} custom-call(s32[64,32]{1,0:T(8,128)S(1)} %bitcast.9, bf16[256,2048]{1,0:T(8,128)(2,1)S(1)} %shard_map.197.refs_1_), custom_call_target="tpu_custom_call" | custom-call | flops 2000000000 | bytes 2000000 | tf_op jit(solution)/shard_map/pallas_call | solution.py:60
  37.5 27.0 %all_to_all.31.refs_2_ = bf16[64,48,128]{2,1,0:T(8,128)(2,1)S(1)} all-to-all(bf16[64,48,128]{2,1,0:T(8,128)(2,1)S(1)} %shard_map.198), channel_id=1, replica_groups=mesh['y'=4,'z'=8,'c'=2,'x'=4] {'y','z','c'}, dimensions={0} | all-to-all | bytes 1572864 | tf_op jit(solution)/shard_map/all_to_all | solution.py:565
  64.5 0.0 copy-start.3
  64.5 0.0 copy-start.4
  64.5 0.0 copy-start.5
  64.5 0.0 copy-start
  64.5 0.0 copy-start.1
  64.6 0.0 copy-start.2
  64.6 1.8 %shard_map.199 = (bf16[384,128]{1,0:T(8,128)(2,1)}, bf16[384,128]{1,0:T(8,128)(2,1)S(1)}, bf16[384,128]{1,0:T(8,128)(2,1)S(1)}, bf16[384,128]{1,0:T(8,128)(2,1)S(1)}) custom-call(s32[1]{0:T(128)} %bitcast.refs_0_, s32[8,128]{1,0:T(8,128)S(1)} %get-tuple-element.43.refs_1_, bf16[64,48,128]{2,1,0:T(8,128)(2,1)S(1)} %all_to_all.31.refs_2_), custom_call_target="tpu_custom_call" | custom-call | flops 1000000000 | bytes 2000000 | tf_op jit(solution)/shard_map/pallas_call | solution.py:60
  66.4 0.1 collective-permute-start.3
  66.5 2.4 %collective-permute-start.4 = (bf16[384,128]{1,0:T(8,128)(2,1)S(1)}, bf16[384,128]{1,0:T(8,128)(2,1)S(1)}, u32[]{:S(2)}, u32[]{:S(2)}) collective-permute-start(bf16[384,128]{1,0:T(8,128)(2,1)S(1)} %get-tuple-element.47), channel_id=1, source_target_pairs={{0,2},{1,3},{2,0},{3,1},{4,6},{5,7},{6,4},{7,5},{8,10},{9,11},{10,... | collective-permute-start | bytes 294920 | tf_op jit(solution)/shard_map/ppermute | solution.py:82
  68.9 1.2 collective-permute-start.5
  70.1 0.0 copy-done.3
  70.1 0.0 copy-done.4
  70.1 0.0 copy-done.5
  70.1 1.7 collective-permute-done.3.refs_3_
  71.9 1.7 collective-permute-done.4.refs_4_
  73.6 0.5 collective-permute-done.5.refs_5_
  74.0 0.0 copy-done
  74.0 0.0 copy-done.1
  74.0 0.0 copy-done.2
  74.1 12.8 %shard_map.200 = (f32[2,128]{1,0:T(2,128)S(1)}, f32[2,768]{1,0:T(2,128)}, bf16[384,128]{1,0:T(8,128)(2,1)S(1)}, bf16[384,128]{1,0:T(8,128)(2,1)S(1)}, bf16[384,1...) custom-call(s32[1]{0:T(128)} %bitcast.refs_0_, ...), custom_call_target="tpu_custom_call" | custom-call | flops 4000000000 | bytes 10000000 | tf_op jit(solution)/shard_map/pallas_call | solution.py:60
  86.9 1.6 collective-permute-start.9
  88.5 0.9 collective-permute-start.6
  89.4 2.6 %collective-permute-start.7 = (bf16[384,128]{1,0:T(8,128)(2,1)S(1)}, bf16[384,128]{1,0:T(8,128)(2,1)S(1)}, u32[]{:S(2)}, u32[]{:S(2)}) collective-permute-start(bf16[384,128]{1,0:T(8,128)(2,1)S(1)} %get-tuple-element.52), channel_id=1, source_target_pairs={{0,2},{1,3},{2,0},{3,1},{4,6},{5,7},{6,4},{7,5},{8,10},{9,11},{10,... | collective-permute-start | bytes 294920 | tf_op jit(solution)/shard_map/ppermute | solution.py:82
  92.1 0.0 collective-permute-start.8
  92.1 1.9 %collective-permute-done.6.refs_4_.refs_3_ = bf16[384,128]{1,0:T(8,128)(2,1)S(1)} collective-permute-done((bf16[384,128]{1,0:T(8,128)(2,1)S(1)}, bf16[384,128]{1,0:T(8,128)(2,1)S(1)}, u32[]{:S(2)}, u32[]{:S(2)}) %collective-permute-start.6) | collective-permute-done | bytes 98336 | tf_op jit(solution)/shard_map/ppermute | solution.py:82
  94.1 3.0 %collective-permute-done.7.refs_5_.refs_4_ = bf16[384,128]{1,0:T(8,128)(2,1)S(1)} collective-permute-done((bf16[384,128]{1,0:T(8,128)(2,1)S(1)}, bf16[384,128]{1,0:T(8,128)(2,1)S(1)}, u32[]{:S(2)}, u32[]{:S(2)}) %collective-permute-start.7) | collective-permute-done | bytes 98336 | tf_op jit(solution)/shard_map/ppermute | solution.py:82
  97.1 0.0 collective-permute-done.8.refs_6_.refs_5_
  97.1 0.0 collective-permute-done.9.refs_2_
  97.1 4.9 %shard_map.201 = (bf16[32,80,128]{2,1,0:T(8,128)(2,1)}, bf16[32,80,128]{2,1,0:T(8,128)(2,1)}, bf16[32,80,128]{2,1,0:T(8,128)(2,1)S(1)}, bf16[32,80,128]{2,1,0:T(8,128)(2,1)S(1)}, f32[8,128]{1,0:T(8,128)S(1)}) custom-call(s32[1]{0:T(128)} %bitcast.refs_0_, bf16[4,256,768]{2,1,0:T(8,128)(2,1)} %get-tuple-element.54.refs_1_, ...), custom_call_target="tpu_custom_call" | custom-call | flops 2000000000 | bytes 10000000 | tf_op jit(solution)/shard_map/pallas_call | solution.py:60
  101.9 1.2 collective-permute-start.10
  103.2 2.7 %collective-permute-start.11 = (bf16[32,80,128]{2,1,0:T(8,128)(2,1)S(1)}, bf16[32,80,128]{2,1,0:T(8,128)(2,1)S(1)}, u32[]{:S(2)}, u32[]{:S(2)}) collective-permute-start(bf16[32,80,128]{2,1,0:T(8,128)(2,1)S(1)} %get-tuple-element.62), channel_id=1, source_target_pairs={{0,2},{1,3},{2,0},{3,1},{4,6},{5,7},{6,4},{7,5},{8,10},{9,11},{10,... | collective-permute-start | bytes 1966088 | tf_op jit(solution)/shard_map/ppermute | solution.py:82
  105.9 0.0 collective-permute-start.12
  105.9 2.2 %shard_map.202 = bf16[64,48,128]{2,1,0:T(8,128)(2,1)} custom-call(s32[1]{0:T(128)} %bitcast.refs_0_, s32[8,128]{1,0:T(8,128)S(1)} %get-tuple-element.43.refs_1_, bf16[384,128]{1,0:T(8,128)(2,1)S(1)} %get-tuple-element.50.refs_2_, bf16[384,128]{1,0:T(8,128)(2,1)S(1)} %collective-permute-done.6.refs_4_.refs_3_, ...), custom_call_target="tpu_custom_call" | custom-call | flops 1000000000 | bytes 2000000 | tf_op jit(solution)/shard_map/pallas_call | solution.py:60
  108.0 7.1 %all-to-all-start.2 = ((bf16[64,48,128]{2,1,0:T(8,128)(2,1)}), bf16[64,48,128]{2,1,0:T(8,128)(2,1)}, u32[]{:S(2)}, u32[]{:S(2)}) async-start(bf16[64,48,128]{2,1,0:T(8,128)(2,1)} %shard_map.202), calls=%async_computation.2 | async-start | bytes 1572864 | tf_op jit(solution)/shard_map/all_to_all | solution.py:565
  115.2 3.9 %collective-permute-done.10.refs_1_ = bf16[32,80,128]{2,1,0:T(8,128)(2,1)S(1)} collective-permute-done((bf16[32,80,128]{2,1,0:T(8,128)(2,1)}, bf16[32,80,128]{2,1,0:T(8,128)(2,1)S(1)}, u32[]{:S(2)}, u32[]{:S(2)}) %collective-permute-start.10) | collective-permute-done | bytes 655392 | tf_op jit(solution)/shard_map/ppermute | solution.py:82
  119.0 15.5 %collective-permute-done.11.refs_2_ = bf16[32,80,128]{2,1,0:T(8,128)(2,1)S(1)} collective-permute-done((bf16[32,80,128]{2,1,0:T(8,128)(2,1)S(1)}, bf16[32,80,128]{2,1,0:T(8,128)(2,1)S(1)}, u32[]{:S(2)}, u32[]{:S(2)}) %collective-permute-start.11) | collective-permute-done | bytes 655392 | tf_op jit(solution)/shard_map/ppermute | solution.py:82
  134.6 0.0 collective-permute-done.12.refs_3_
  134.6 3.1 %shard_map.204.refs_0_ = bf16[32,80,128]{2,1,0:T(8,128)(2,1)} custom-call(bf16[32,80,128]{2,1,0:T(8,128)(2,1)} %get-tuple-element.60.refs_0_, bf16[32,80,128]{2,1,0:T(8,128)(2,1)S(1)} %collective-permute-done.10.refs_1_, bf16[32,80,128]{2,1,0:T(8,128)(2,1)S(1)} %collective-permute-done.11.refs_2_, bf16[32,80,128]{2,1,0:T(8,128)(2,1)} %collective-permute-done.12.refs_3_), custom_call_target="tpu_custom_call" | custom-call | flops 999999995904 | bytes 10000000 | tf_op jit(solution)/shard_map/pallas_call | solution.py:60
  137.7 0.4 all-to-all-done.2.refs_1_
  138.1 5.1 %all-to-all-start.3 = ((bf16[32,80,128]{2,1,0:T(8,128)(2,1)}), bf16[32,80,128]{2,1,0:T(8,128)(2,1)S(1)}, u32[]{:S(2)}, u32[]{:S(2)}) async-start(bf16[32,80,128]{2,1,0:T(8,128)(2,1)} %shard_map.205), calls=%async_computation.3 | async-start | bytes 1310720 | tf_op jit(solution)/shard_map/all_to_all | solution.py:565
  143.2 5.0 %shard_map.203 = (f32[192,2048]{1,0:T(8,128)}, f32[8,128]{1,0:T(8,128)S(1)}) custom-call(s32[64,32]{1,0:T(8,128)S(1)} %bitcast.10, bf16[64,48,128]{2,1,0:T(8,128)(2,1)} %all-to-all-done.2.refs_1_), custom_call_target="tpu_custom_call" | custom-call | flops 2000000000 | bytes 4000000 | tf_op jit(solution)/shard_map/pallas_call | solution.py:60
  148.2 11.5 %all-to-all-done.3.refs_0_ = bf16[32,80,128]{2,1,0:T(8,128)(2,1)S(1)} async-done(((bf16[32,80,128]{2,1,0:T(8,128)(2,1)}), bf16[32,80,128]{2,1,0:T(8,128)(2,1)S(1)}, u32[]{:S(2)}, u32[]{:S(2)}) %all-to-all-start.3) | async-done | bytes 655392 | tf_op jit(solution)/shard_map/all_to_all | solution.py:565
  159.7 0.8 shard_map.206
  160.5 8.4 %all-to-all-start.4 = ((bf16[8,80,128]{2,1,0:T(8,128)(2,1)}), bf16[8,80,128]{2,1,0:T(8,128)(2,1)S(1)}, u32[]{:S(2)}, u32[]{:S(2)}) async-start(bf16[8,80,128]{2,1,0:T(8,128)(2,1)} %shard_map.206), calls=%async_computation.4 | async-start | bytes 327680 | tf_op jit(solution)/shard_map/all_to_all | solution.py:565
  168.9 0.6 slice_reduce_fusion
  169.5 4.9 %all-to-all-done.4.refs_1_ = bf16[8,80,128]{2,1,0:T(8,128)(2,1)S(1)} async-done(((bf16[8,80,128]{2,1,0:T(8,128)(2,1)}), bf16[8,80,128]{2,1,0:T(8,128)(2,1)S(1)}, u32[]{:S(2)}, u32[]{:S(2)}) %all-to-all-start.4) | async-done | bytes 163872 | tf_op jit(solution)/shard_map/all_to_all | solution.py:565
  174.4 0.7 shard_map.207
  (4 shorter events, 0.0 us)
Async XLA Ops:
  0.6 5.9 %collective-permute-start = (s32[2,128]{1,0:T(2,128)}, s32[2,128]{1,0:T(2,128)S(1)}, u32[]{:S(2)}, u32[]{:S(2)}) collective-permute-start(s32[2,128]{1,0:T(2,128)} %refs_1_.1), channel_id=1, source_target_pairs={{0,1},{1,2},{2,3},{3,0},{4,5},{5,6},{6,7},{7,4},{8,9},{9,10},{10,1... | collective-permute-start | bytes 3080 | tf_op jit(solution)/shard_map/ppermute | solution.py:82
  2.8 3.8 %collective-permute-start.2 = (s32[2,128]{1,0:T(2,128)}, s32[2,128]{1,0:T(2,128)S(1)}, u32[]{:S(2)}, u32[]{:S(2)}) collective-permute-start(s32[2,128]{1,0:T(2,128)} %refs_1_.1), channel_id=1, source_target_pairs={{0,3},{1,0},{2,1},{3,2},{4,7},{5,4},{6,5},{7,6},{8,11},{9,8},{10,9... | collective-permute-start | bytes 3080 | tf_op jit(solution)/shard_map/ppermute | solution.py:82
  4.1 4.1 %collective-permute-start.1 = (s32[2,128]{1,0:T(2,128)}, s32[2,128]{1,0:T(2,128)S(1)}, u32[]{:S(2)}, u32[]{:S(2)}) collective-permute-start(s32[2,128]{1,0:T(2,128)} %refs_1_.1), channel_id=1, source_target_pairs={{0,2},{1,3},{2,0},{3,1},{4,6},{5,7},{6,4},{7,5},{8,10},{9,11},{10,... | collective-permute-start | bytes 3080 | tf_op jit(solution)/shard_map/ppermute | solution.py:82
  11.7 23.4 %all-to-all-start = ((s32[64,1,32]{2,1,0:T(1,128)}), s32[64,1,32]{2,1,0:T(1,128)S(1)}, u32[]{:S(2)}, u32[]{:S(2)}) async-start(s32[64,1,32]{2,1,0:T(1,128)} %bitcast.4), calls=%async_computation | async-start | bytes 65536 | tf_op jit(solution)/shard_map/all_to_all | solution.py:565
  64.5 5.6 %copy-start.3 = (f32[768]{0:T(1024)S(1)}, f32[768]{0:T(1024)}, u32[]{:S(2)}) copy-start(f32[768]{0:T(1024)} %param.21) | copy-start | bytes 9220
  64.5 5.6 %copy-start.4 = (f32[768]{0:T(1024)S(1)}, f32[768]{0:T(1024)}, u32[]{:S(2)}) copy-start(f32[768]{0:T(1024)} %param.22) | copy-start | bytes 9220
  64.5 5.6 %copy-start.5 = (f32[768]{0:T(1024)S(1)}, f32[768]{0:T(1024)}, u32[]{:S(2)}) copy-start(f32[768]{0:T(1024)} %param.23) | copy-start | bytes 9220
  64.5 9.5 %copy-start = (bf16[768,768]{1,0:T(8,128)(2,1)S(1)}, bf16[768,768]{1,0:T(8,128)(2,1)}, u32[]{:S(2)}) copy-start(bf16[768,768]{1,0:T(8,128)(2,1)} %refs_8_.1) | copy-start | bytes 3538948
  64.5 9.5 %copy-start.1 = (bf16[2,768]{1,0:T(2,128)(2,1)S(1)}, bf16[2,768]{1,0:T(2,128)(2,1)}, u32[]{:S(2)}) copy-start(bf16[2,768]{1,0:T(2,128)(2,1)} %refs_6_.1) | copy-start | bytes 9220
  64.6 9.5 %copy-start.2 = (s32[2,128]{1,0:T(2,128)S(1)}, s32[2,128]{1,0:T(2,128)}, u32[]{:S(2)}) copy-start(s32[2,128]{1,0:T(2,128)} %refs_7_.1) | copy-start | bytes 3076
  66.4 5.5 %collective-permute-start.3 = (bf16[384,128]{1,0:T(8,128)(2,1)S(1)}, bf16[384,128]{1,0:T(8,128)(2,1)S(1)}, u32[]{:S(2)}, u32[]{:S(2)}) collective-permute-start(bf16[384,128]{1,0:T(8,128)(2,1)S(1)} %get-tuple-element.46), channel_id=1, source_target_pairs={{0,1},{1,2},{2,3},{3,0},{4,5},{5,6},{6,7},{7,4},{8,9},{9,10},{10,1... | collective-permute-start | bytes 294920 | tf_op jit(solution)/shard_map/ppermute | solution.py:82
  66.5 7.1 %collective-permute-start.4 = (bf16[384,128]{1,0:T(8,128)(2,1)S(1)}, bf16[384,128]{1,0:T(8,128)(2,1)S(1)}, u32[]{:S(2)}, u32[]{:S(2)}) collective-permute-start(bf16[384,128]{1,0:T(8,128)(2,1)S(1)} %get-tuple-element.47), channel_id=1, source_target_pairs={{0,2},{1,3},{2,0},{3,1},{4,6},{5,7},{6,4},{7,5},{8,10},{9,11},{10,... | collective-permute-start | bytes 294920 | tf_op jit(solution)/shard_map/ppermute | solution.py:82
  68.9 5.1 %collective-permute-start.5 = (bf16[384,128]{1,0:T(8,128)(2,1)S(1)}, bf16[384,128]{1,0:T(8,128)(2,1)S(1)}, u32[]{:S(2)}, u32[]{:S(2)}) collective-permute-start(bf16[384,128]{1,0:T(8,128)(2,1)S(1)} %get-tuple-element.48), channel_id=1, source_target_pairs={{0,3},{1,0},{2,1},{3,2},{4,7},{5,4},{6,5},{7,6},{8,11},{9,8},{10,9... | collective-permute-start | bytes 294920 | tf_op jit(solution)/shard_map/ppermute | solution.py:82
  86.9 10.2 %collective-permute-start.9 = (bf16[4,256,768]{2,1,0:T(8,128)(2,1)}, bf16[4,256,768]{2,1,0:T(8,128)(2,1)S(1)}, u32[]{:S(2)}, u32[]{:S(2)}) collective-permute-start(bf16[4,256,768]{2,1,0:T(8,128)(2,1)} %get-tuple-element.55), channel_id=1, source_target_pairs={{0,4},{4,0},{1,5},{5,1},{2,6},{6,2},{3,7},{7,3},{8,12},{12,8},{9,1... | collective-permute-start | bytes 4718600 | tf_op jit(solution)/shard_map/ppermute | solution.py:648
  88.5 5.6 %collective-permute-start.6 = (bf16[384,128]{1,0:T(8,128)(2,1)S(1)}, bf16[384,128]{1,0:T(8,128)(2,1)S(1)}, u32[]{:S(2)}, u32[]{:S(2)}) collective-permute-start(bf16[384,128]{1,0:T(8,128)(2,1)S(1)} %get-tuple-element.51), channel_id=1, source_target_pairs={{0,1},{1,2},{2,3},{3,0},{4,5},{5,6},{6,7},{7,4},{8,9},{9,10},{10,1... | collective-permute-start | bytes 294920 | tf_op jit(solution)/shard_map/ppermute | solution.py:82
  89.4 7.6 %collective-permute-start.7 = (bf16[384,128]{1,0:T(8,128)(2,1)S(1)}, bf16[384,128]{1,0:T(8,128)(2,1)S(1)}, u32[]{:S(2)}, u32[]{:S(2)}) collective-permute-start(bf16[384,128]{1,0:T(8,128)(2,1)S(1)} %get-tuple-element.52), channel_id=1, source_target_pairs={{0,2},{1,3},{2,0},{3,1},{4,6},{5,7},{6,4},{7,5},{8,10},{9,11},{10,... | collective-permute-start | bytes 294920 | tf_op jit(solution)/shard_map/ppermute | solution.py:82
  92.1 5.0 %collective-permute-start.8 = (bf16[384,128]{1,0:T(8,128)(2,1)S(1)}, bf16[384,128]{1,0:T(8,128)(2,1)S(1)}, u32[]{:S(2)}, u32[]{:S(2)}) collective-permute-start(bf16[384,128]{1,0:T(8,128)(2,1)S(1)} %get-tuple-element.53), channel_id=1, source_target_pairs={{0,3},{1,0},{2,1},{3,2},{4,7},{5,4},{6,5},{7,6},{8,11},{9,8},{10,9... | collective-permute-start | bytes 294920 | tf_op jit(solution)/shard_map/ppermute | solution.py:82
  101.9 17.1 %collective-permute-start.10 = (bf16[32,80,128]{2,1,0:T(8,128)(2,1)}, bf16[32,80,128]{2,1,0:T(8,128)(2,1)S(1)}, u32[]{:S(2)}, u32[]{:S(2)}) collective-permute-start(bf16[32,80,128]{2,1,0:T(8,128)(2,1)} %get-tuple-element.61), channel_id=1, source_target_pairs={{0,1},{1,2},{2,3},{3,0},{4,5},{5,6},{6,7},{7,4},{8,9},{9,10},{10,1... | collective-permute-start | bytes 1966088 | tf_op jit(solution)/shard_map/ppermute | solution.py:82
  103.2 31.4 %collective-permute-start.11 = (bf16[32,80,128]{2,1,0:T(8,128)(2,1)S(1)}, bf16[32,80,128]{2,1,0:T(8,128)(2,1)S(1)}, u32[]{:S(2)}, u32[]{:S(2)}) collective-permute-start(bf16[32,80,128]{2,1,0:T(8,128)(2,1)S(1)} %get-tuple-element.62), channel_id=1, source_target_pairs={{0,2},{1,3},{2,0},{3,1},{4,6},{5,7},{6,4},{7,5},{8,10},{9,11},{10,... | collective-permute-start | bytes 1966088 | tf_op jit(solution)/shard_map/ppermute | solution.py:82
  105.9 28.7 %collective-permute-start.12 = (bf16[32,80,128]{2,1,0:T(8,128)(2,1)S(1)}, bf16[32,80,128]{2,1,0:T(8,128)(2,1)}, u32[]{:S(2)}, u32[]{:S(2)}) collective-permute-start(bf16[32,80,128]{2,1,0:T(8,128)(2,1)S(1)} %get-tuple-element.63), channel_id=1, source_target_pairs={{0,3},{1,0},{2,1},{3,2},{4,7},{5,4},{6,5},{7,6},{8,11},{9,8},{10,9... | collective-permute-start | bytes 1966088 | tf_op jit(solution)/shard_map/ppermute | solution.py:82
  108.0 30.1 %all-to-all-start.2 = ((bf16[64,48,128]{2,1,0:T(8,128)(2,1)}), bf16[64,48,128]{2,1,0:T(8,128)(2,1)}, u32[]{:S(2)}, u32[]{:S(2)}) async-start(bf16[64,48,128]{2,1,0:T(8,128)(2,1)} %shard_map.202), calls=%async_computation.2 | async-start | bytes 1572864 | tf_op jit(solution)/shard_map/all_to_all | solution.py:565
  138.1 21.6 %all-to-all-start.3 = ((bf16[32,80,128]{2,1,0:T(8,128)(2,1)}), bf16[32,80,128]{2,1,0:T(8,128)(2,1)S(1)}, u32[]{:S(2)}, u32[]{:S(2)}) async-start(bf16[32,80,128]{2,1,0:T(8,128)(2,1)} %shard_map.205), calls=%async_computation.3 | async-start | bytes 1310720 | tf_op jit(solution)/shard_map/all_to_all | solution.py:565
  160.5 13.9 %all-to-all-start.4 = ((bf16[8,80,128]{2,1,0:T(8,128)(2,1)}), bf16[8,80,128]{2,1,0:T(8,128)(2,1)S(1)}, u32[]{:S(2)}, u32[]{:S(2)}) async-start(bf16[8,80,128]{2,1,0:T(8,128)(2,1)} %shard_map.206), calls=%async_computation.4 | async-start | bytes 327680 | tf_op jit(solution)/shard_map/all_to_all | solution.py:565
